TPU v7x, 1024 devices: a whole 8x8x8 slice. The times are simulated.
1024 devices in a mesh: replica: 8 (over z), fsdp: 64 (over x_lo, y, core), tensor: 2 (over x_hi).
Axes of the slice: x: 8 (x_hi: 2, x_lo: 4; x = x_hi * 4 + x_lo), y: 8, z: 8, core: 2. Of those that a mesh axis runs over, the one named last changes fastest.
Arguments:
- hidden_in: bfloat16 [65536, 8192], P(('replica', 'fsdp')), may hold values from -500 to 500
- norm_gain: bfloat16 [8192], replicated, may hold values from 0.099609375 to 1.8984375
- key_cotangent: bfloat16 [65536, 512], P(('replica', 'fsdp'), 'tensor'), may hold values from -220 to 220
- inner_params: float32 [8, 8192, 512], P('replica', 'fsdp', 'tensor'), may hold values from -6 to 6
- inner_first: float32 [8, 8192, 512], P('replica', 'fsdp', 'tensor'), may hold values from -6 to 6
- inner_second: float32 [8, 8192, 512], P('replica', 'fsdp', 'tensor'), may hold values from 1 to 10
- frag_local: float32 [8, 8, 8192, 512], P('replica', None, 'fsdp', 'tensor'), may hold values from -6 to 6
- frag_global: float32 [8, 8192, 512], P(None, 'fsdp', 'tensor'), may hold values from -6 to 6
- outer_momentum: float32 [8, 8192, 512], P(None, 'fsdp', 'tensor'), may hold values from -6 to 6
- frag_index: int32 [1], replicated, may hold values from 0 to 7
Outputs:
- new_params: float32 [8, 8192, 512], P('replica', 'fsdp', 'tensor')
- new_first: float32 [8, 8192, 512], P('replica', 'fsdp', 'tensor')
- new_second: float32 [8, 8192, 512], P('replica', 'fsdp', 'tensor')
- new_fragment: float32 [8192, 512], P('fsdp', 'tensor')
- new_momentum: float32 [8192, 512], P('fsdp', 'tensor')
All inputs are finite; a program needn't handle non-finite values.
Results may differ from a plain program's by a relative error of at most 0.0029.
Values may be sent and summed in bfloat16 or wider, within the bound.
No kernel may reach another device: no remote copies, remote signals or barrier semaphores. Data moves between devices by JAX's collectives and lax.ppermute only.
A program may use at most 32 MiB of HBM per device.

v0:
```python
import jax
import jax.numpy as jnp
from jax import lax
from jax.sharding import PartitionSpec as P

NORM_EPS = 1e-05
CLIP_RMS = 8.0
FIRST_BETA = 0.9
SECOND_BETA = 0.95
FIRST_FIX = 1.0 - 0.9**10
SECOND_FIX = 1.0 - 0.95**10
ADAM_EPS = 1e-08
INNER_RATE = 0.01
DECAY_WEIGHT = 0.1
OUTER_RATE = 0.7
OUTER_BETA = 0.9


def outer_update(summed, global_layer, moment_layer, workers):
    pseudo = global_layer - summed / workers
    new_momentum = OUTER_BETA * moment_layer + pseudo
    new_fragment = global_layer - OUTER_RATE * (pseudo + OUTER_BETA * new_momentum)
    return (new_fragment, new_momentum)


def on_device(
    hidden_in,
    norm_gain,
    key_cotangent,
    inner_params,
    inner_first,
    inner_second,
    frag_local,
    frag_global,
    outer_momentum,
    frag_index,
):
    widened = hidden_in.astype(jnp.float32)
    mean_square = jnp.mean(widened * widened, axis=1, keepdims=True)
    normed = (
        widened * lax.rsqrt(mean_square + NORM_EPS) * norm_gain.astype(jnp.float32)[None, :]
    ).astype(jnp.bfloat16)
    contract = (((0,), (0,)), ((), ()))
    feature_rows = lax.all_to_all(normed, "fsdp", split_axis=1, concat_axis=0, tiled=True)
    gradient = lax.dot_general(
        feature_rows,
        lax.all_gather(key_cotangent, "fsdp", axis=0, tiled=True),
        contract,
        preferred_element_type=jnp.float32,
    )
    total_square = lax.psum(jnp.sum(gradient * gradient), ("fsdp", "tensor"))
    entries = (
        gradient.shape[0] * gradient.shape[1] * lax.axis_size("fsdp") * lax.axis_size("tensor")
    )
    factor = jnp.minimum(1.0, CLIP_RMS * lax.rsqrt(total_square / entries + 1e-06))
    clipped = factor * gradient
    params = inner_params[0]
    new_first = FIRST_BETA * inner_first[0] + (1.0 - FIRST_BETA) * clipped
    new_second = SECOND_BETA * inner_second[0] + (1.0 - SECOND_BETA) * clipped * clipped
    direction = new_first / FIRST_FIX / (jnp.sqrt(new_second / SECOND_FIX) + ADAM_EPS)
    new_params = params - INNER_RATE * (direction + DECAY_WEIGHT * params)
    layer_index = frag_index[0]
    local_layer = lax.dynamic_index_in_dim(frag_local[0], layer_index, 0, keepdims=False)
    global_layer = lax.dynamic_index_in_dim(frag_global, layer_index, 0, keepdims=False)
    moment_layer = lax.dynamic_index_in_dim(outer_momentum, layer_index, 0, keepdims=False)
    workers = lax.axis_size("replica")
    summed = lax.psum(local_layer, "replica")
    new_fragment, new_momentum = outer_update(summed, global_layer, moment_layer, workers)
    return (new_params[None], new_first[None], new_second[None], new_fragment, new_momentum)


def solution(mesh):
    return jax.shard_map(
        on_device,
        mesh=mesh,
        in_specs=(
            P(("replica", "fsdp"), None),
            P(),
            P(("replica", "fsdp"), "tensor"),
            P("replica", "fsdp", "tensor"),
            P("replica", "fsdp", "tensor"),
            P("replica", "fsdp", "tensor"),
            P("replica", None, "fsdp", "tensor"),
            P(None, "fsdp", "tensor"),
            P(None, "fsdp", "tensor"),
            P(),
        ),
        out_specs=(
            P("replica", "fsdp", "tensor"),
            P("replica", "fsdp", "tensor"),
            P("replica", "fsdp", "tensor"),
            P("fsdp", "tensor"),
            P("fsdp", "tensor"),
        ),
        check_vma=False,
    )
```

profile of v0, /device:TPU:1, one launch (start us, length us, event | category | flops | bytes accessed | tf_op | source)
XLA Modules:
  0.0 520.3 jit_solution(1746522901360925068)
XLA Ops:
  8.0 0.0 copy-start
  8.0 0.0 copy-start.4
  8.0 0.0 all-reduce.2.cloned.1.call-start
  8.8 0.4 copy-done
  9.2 0.7 dynamic-slice_bitcast_fusion
  9.9 0.0 all-reduce.2.cloned.1.call-update
  9.9 0.0 all-gather.2.cloned.1.call-start
  10.0 0.5 all-gather.2.cloned.1.call-update
  10.5 3.2 copy.15
  13.7 0.0 copy-done.4
  13.8 1.1 fusion
  14.9 4.3 fusion.2
  19.2 18.3 %all-to-all-start = ((bf16[128,64,128]{0,2,1:T(8,128)(2,1)}), bf16[128,64,128]{0,2,1:T(8,128)(2,1)S(1)}, u32[]{:S(2)}, u32[]{:S(2)}) async-start(bf16[128,64,128]{0,2,1:T(8,128)(2,1)} %bitcast.53), calls=%async_computation | async-start | bytes 4194304 | tf_op jit(solution)/shard_map/all_to_all | solution.py:44
  37.5 67.3 %all-reduce.2.cloned.1.call-done = f32[128,256]{1,0:T(8,128)} async-done(((f32[128,256]{1,0:T(8,128)}), f32[128,256]{1,0:T(8,128)}) %all-reduce.2.cloned.1.call-update) | async-done | bytes 131088 | tf_op jit(solution)/shard_map/psum | solution.py:67
  104.8 1.8 bitcast_subtract_fusion
  106.5 0.0 all-to-all-done
  106.5 0.0 copy-start.1
  106.5 1.3 copy-done.1
  107.9 3.2 copy.16
  111.1 0.0 copy-start.2
  111.1 0.0 copy-start.3
  111.1 72.7 %all-gather.2.cloned.1.call-done = bf16[8192,256]{1,0:T(8,128)(2,1)} async-done(((bf16[128,256]{1,0:T(8,128)(2,1)}), bf16[8192,256]{1,0:T(8,128)(2,1)}) %all-gather.2.cloned.1.call-update) | async-done | bytes 4194320 | tf_op jit(solution)/shard_map/all_gather | solution.py:47
  183.9 3.6 multiply_reduce_fusion
  187.5 322.9 %psum.14 = f32[]{:T(128)} all-reduce(f32[]{:T(128)} %get-tuple-element.10), channel_id=1, replica_groups=mesh['replica'=8,'fsdp'=64,'tensor'=2] {'fsdp','tensor'}, use_global_device_ids=true, to_apply=%region_2.0 | all-reduce | flops 1 | bytes 8 | tf_op jit(solution)/shard_map/psum | solution.py:51
  511.1 0.0 copy-done.2
  511.1 0.0 copy-done.3
  511.1 1.7 fusion.8
  (2 shorter events, 0.0 us)
Async XLA Ops:
  8.0 1.2 copy-start
  8.0 5.7 %copy-start.4 = (bf16[8192]{0:T(1024)(128)(2,1)S(1)}, bf16[8192]{0:T(1024)(128)(2,1)}, u32[]{:S(2)}) copy-start(bf16[8192]{0:T(1024)(128)(2,1)} %param.11) | copy-start | bytes 49156
  8.0 96.8 %all-reduce.2.cloned.1.call-start = ((), (), s32[]{:S(2)}) async-start(), calls=%async_computation.2 | async-start | bytes 262144 | tf_op jit(solution)/shard_map/psum | solution.py:67
  9.9 173.9 %all-gather.2.cloned.1.call-start = ((), (), s32[]{:S(2)}) async-start(), calls=%async_computation.1 | async-start | bytes 4259840 | tf_op jit(solution)/shard_map/all_gather | solution.py:47
  19.2 87.3 %all-to-all-start = ((bf16[128,64,128]{0,2,1:T(8,128)(2,1)}), bf16[128,64,128]{0,2,1:T(8,128)(2,1)S(1)}, u32[]{:S(2)}, u32[]{:S(2)}) async-start(bf16[128,64,128]{0,2,1:T(8,128)(2,1)} %bitcast.53), calls=%async_computation | async-start | bytes 4194304 | tf_op jit(solution)/shard_map/all_to_all | solution.py:44
  106.5 1.3 copy-start.1
  111.1 400.0 %copy-start.2 = (f32[1,128,256]{2,1,0:T(8,128)S(1)}, f32[1,128,256]{2,1,0:T(8,128)}, u32[]{:S(2)}) copy-start(f32[1,128,256]{2,1,0:T(8,128)} %param.15) | copy-start | bytes 393220
  111.1 400.0 %copy-start.3 = (f32[1,128,256]{2,1,0:T(8,128)S(1)}, f32[1,128,256]{2,1,0:T(8,128)}, u32[]{:S(2)}) copy-start(f32[1,128,256]{2,1,0:T(8,128)} %param.14) | copy-start | bytes 393220
Sparse Core Ops, SparseCore 0:
  11.7 92.9 all-reduce.1
Sparse Core Ops, SparseCore 1:
  13.1 170.7 all-gather.1
where the time goes:
time: 530 us; the launch traced here: 520 us
  blocking collectives  323 us (61%)
  waiting for transfers between devices  141 us (27%)
  starting transfers between devices  18.4 us (3%)
  between operations  17 us (3%)
  other arithmetic  8.97 us (2%)
  local copies, waits for them, and re-layouts  8.91 us (2%)
    psum x1, blocking collectives, on_device(): total_square = lax.psum(jnp.sum(gradient * gradient), ('fsdp', 'tensor'))  323 us
    all_gather x1, waiting for transfers between devices, on_device(): lax.all_gather(key_cotangent, 'fsdp', axis=0, tiled=True)  72.7 us
    psum x1, waiting for transfers between devices, on_device(): summed = lax.psum(local_layer, 'replica')  67.3 us
    all_to_all x1, starting transfers between devices, on_device(): lax.all_to_all(normed, 'fsdp', split_axis=1, concat_axis=0, tiled=True)  18.3 us
  transfers between devices with their start and end apart: 3, of which 2 were waited for; matrix products, arithmetic and copies ran while one was open for 3% of the time, Pallas kernels for 0%

commit v1 on v0

v1 whole, which is shorter than its diff:
```python
import jax
import jax.numpy as jnp
from jax import lax
from jax.sharding import Mesh, PartitionSpec as P

NORM_EPS = 1e-05
CLIP_RMS = 8.0
FIRST_BETA = 0.9
SECOND_BETA = 0.95
FIRST_FIX = 1.0 - 0.9**10
SECOND_FIX = 1.0 - 0.95**10
ADAM_EPS = 1e-08
INNER_RATE = 0.01
DECAY_WEIGHT = 0.1
OUTER_RATE = 0.7
OUTER_BETA = 0.9

XL, YN, CORES, XH = 4, 8, 2, 2
CHIP_SCALE = 2.0**-8
X_SCALE = 2.0**-10
Y_SCALE = 2.0**-11


def outer_update(summed, global_layer, moment_layer, workers):
    pseudo = global_layer - summed / workers
    new_momentum = OUTER_BETA * moment_layer + pseudo
    new_fragment = global_layer - OUTER_RATE * (pseudo + OUTER_BETA * new_momentum)
    return (new_fragment, new_momentum)


def swap_x(block, k):
    return lax.ppermute(block, "xl", [(i, i ^ k) for i in range(XL)])


def worker_gradient(hidden_in, norm_gain, key_cotangent):
    x_at, c_at = lax.axis_index("xl"), lax.axis_index("c")
    other_cot = lax.ppermute(key_cotangent, "c", [(0, 1), (1, 0)])
    first_core = c_at == 0
    cot = jnp.concatenate(
        [
            jnp.where(first_core, key_cotangent, other_cot),
            jnp.where(first_core, other_cot, key_cotangent),
        ],
        axis=0,
    )
    widened = hidden_in.astype(jnp.float32)
    mean_square = jnp.mean(widened * widened, axis=1, keepdims=True)
    normed = (
        widened * lax.rsqrt(mean_square + NORM_EPS) * norm_gain.astype(jnp.float32)[None, :]
    ).astype(jnp.bfloat16)
    tokens = hidden_in.shape[0]
    halves = normed.reshape(tokens, XL * YN, CORES, 128).transpose(2, 0, 1, 3)
    halves = lax.all_to_all(halves.reshape(CORES, tokens, XL * YN * 128), "c", 0, 0, tiled=True)
    halves = halves.reshape(CORES * tokens, XL * YN * 128)
    partial = lax.dot_general(
        cot, halves, (((0,), (0,)), ((), ())), preferred_element_type=jnp.float32
    )
    partial = (partial * CHIP_SCALE).astype(jnp.float16)
    blocks = partial.reshape(2, 128, XL, YN, 128)
    x_first = blocks[0].transpose(1, 2, 0, 3)
    y_first = blocks[1].transpose(2, 1, 0, 3)

    y_parts = lax.all_to_all(y_first, "y", 0, 0, tiled=True)
    mine = lax.dynamic_index_in_dim(x_first, x_at, 0, keepdims=False)
    x_sum = mine.astype(jnp.float32)
    for k in range(1, XL):
        part = lax.dynamic_index_in_dim(x_first, x_at ^ k, 0, keepdims=False)
        x_sum = x_sum + swap_x(part, k).astype(jnp.float32)
    x_sum = (x_sum * (X_SCALE / CHIP_SCALE)).astype(jnp.float16)
    y_sum = jnp.sum(y_parts.astype(jnp.float32), axis=0)
    y_sum = (y_sum * (Y_SCALE / CHIP_SCALE)).astype(jnp.float16)

    top = lax.all_to_all(x_sum, "y", 0, 0, tiled=True)
    bottom = lax.dynamic_index_in_dim(y_sum, x_at, 0, keepdims=False).astype(jnp.float32)
    for k in range(1, XL):
        part = lax.dynamic_index_in_dim(y_sum, x_at ^ k, 0, keepdims=False)
        bottom = bottom + swap_x(part, k).astype(jnp.float32)
    top = jnp.sum(top.astype(jnp.float32), axis=0) * (1.0 / X_SCALE)
    return jnp.concatenate([top, bottom * (1.0 / Y_SCALE)], axis=0)


def sum_worker(value):
    devices = XL * YN * CORES * XH
    rows = jnp.broadcast_to(value, (devices, 1, 128))
    rows = lax.all_to_all(rows, ("xl", "y", "c", "xh"), 0, 0, tiled=True)
    return jnp.sum(rows[:, 0, 0])


def on_device(
    hidden_in,
    norm_gain,
    key_cotangent,
    inner_params,
    inner_first,
    inner_second,
    frag_local,
    frag_global,
    outer_momentum,
    frag_index,
):
    layer_index = frag_index[0]
    local_layer = lax.dynamic_index_in_dim(frag_local[0], layer_index, 0, keepdims=False)
    summed = lax.psum(local_layer, "z")

    gradient = worker_gradient(hidden_in, norm_gain, key_cotangent)
    total_square = sum_worker(jnp.sum(gradient * gradient))
    entries = gradient.shape[0] * gradient.shape[1] * XL * YN * CORES * XH
    factor = jnp.minimum(1.0, CLIP_RMS * lax.rsqrt(total_square / entries + 1e-06))
    clipped = factor * gradient.T
    params = inner_params[0]
    new_first = FIRST_BETA * inner_first[0] + (1.0 - FIRST_BETA) * clipped
    new_second = SECOND_BETA * inner_second[0] + (1.0 - SECOND_BETA) * clipped * clipped
    direction = new_first / FIRST_FIX / (jnp.sqrt(new_second / SECOND_FIX) + ADAM_EPS)
    new_params = params - INNER_RATE * (direction + DECAY_WEIGHT * params)

    global_layer = lax.dynamic_index_in_dim(frag_global, layer_index, 0, keepdims=False)
    moment_layer = lax.dynamic_index_in_dim(outer_momentum, layer_index, 0, keepdims=False)
    workers = lax.axis_size("z")
    new_fragment, new_momentum = outer_update(summed, global_layer, moment_layer, workers)
    return (new_params[None], new_first[None], new_second[None], new_fragment, new_momentum)


def solution(mesh):
    workers = mesh.shape["replica"]
    devices = mesh.devices.reshape(workers, XL, YN, CORES, XH)
    split = Mesh(devices, ("z", "xl", "y", "c", "xh"))
    fsdp = ("xl", "y", "c")
    return jax.shard_map(
        on_device,
        mesh=split,
        in_specs=(
            P(("z",) + fsdp, None),
            P(),
            P(("z",) + fsdp, "xh"),
            P("z", fsdp, "xh"),
            P("z", fsdp, "xh"),
            P("z", fsdp, "xh"),
            P("z", None, fsdp, "xh"),
            P(None, fsdp, "xh"),
            P(None, fsdp, "xh"),
            P(),
        ),
        out_specs=(
            P("z", fsdp, "xh"),
            P("z", fsdp, "xh"),
            P("z", fsdp, "xh"),
            P(fsdp, "xh"),
            P(fsdp, "xh"),
        ),
        check_vma=False,
    )
```

time: 530 us -> 196 us (0.37)
  the two profiles are of different devices: /device:TPU:1 before, /device:TPU:2 now
where the time goes in v1:
time: 196 us; the launch traced here: 195 us
  waiting for transfers between devices  97.4 us (50%)
  starting transfers between devices  53.2 us (27%)
  local copies, waits for them, and re-layouts  18 us (9%)
  between operations  15.8 us (8%)
  other arithmetic  8.31 us (4%)
  matrix products  2.33 us (1%)
    psum x1, waiting for transfers between devices, on_device(): summed = lax.psum(local_layer, 'z')  45.1 us
    ppermute x6, starting transfers between devices, swap_x(): return lax.ppermute(block, 'xl', [(i, i ^ k) for i in range(XL)])  35 us
    all_to_all x1, waiting for transfers between devices, worker_gradient(): y_parts = lax.all_to_all(y_first, 'y', 0, 0, tiled=True)  24.2 us
    ppermute x6, waiting for transfers between devices, swap_x(): return lax.ppermute(block, 'xl', [(i, i ^ k) for i in range(XL)])  15.3 us
    all_to_all x1, waiting for transfers between devices, worker_gradient(): top = lax.all_to_all(x_sum, 'y', 0, 0, tiled=True)  9.9 us
    unnamed x28, local copies, waits for them, and re-layouts  8.78 us
    all_to_all x1, starting transfers between devices, sum_worker(): rows = lax.all_to_all(rows, ('xl', 'y', 'c', 'xh'), 0, 0, tiled=True)  5.37 us
  transfers between devices with their start and end apart: 12, of which 7 were waited for; matrix products, arithmetic and copies ran while one was open for 11% of the time, Pallas kernels for 0%

profile of v1, /device:TPU:2, one launch (start us, length us, event | category | flops | bytes accessed | tf_op | source)
XLA Modules:
  0.0 195.1 jit_solution(1644113213690222987)
XLA Ops:
  7.2 2.1 %collective-permute-start = (bf16[128,256]{1,0:T(8,128)(2,1)}, bf16[128,256]{1,0:T(8,128)(2,1)S(1)}, u32[]{:S(2)}, u32[]{:S(2)}) collective-permute-start(bf16[128,256]{1,0:T(8,128)(2,1)} %param.12), channel_id=1, source_target_pairs={{0,2},{2,0},{1,3},{3,1},{4,6},{6,4},{5,7},{7,5},{8,10},{10,8},{9,1... | collective-permute-start | bytes 196616 | tf_op jit(solution)/shard_map/ppermute | solution.py:37
  9.3 3.2 %copy.96 = bf16[128,8192]{0,1:T(8,128)(2,1)S(1)} copy(bf16[128,8192]{1,0:T(8,128)(2,1)} %param.10) | data formatting | bytes 4194304 | tf_op args[0]
  12.5 1.1 fusion.1
  13.6 3.5 %fusion.3 = bf16[128,8192]{0,1:T(8,128)(2,1)S(1)} fusion(bf16[128,8192]{0,1:T(8,128)(2,1)S(1)} %copy.96, f32[8192]{0:T(1024)S(1)} %convert_element_type.58, f32[128]{0:T(128)S(1)} %add_rsqrt_fusion), kind=kLoop, calls=%fused_computation.6 | loop fusion | flops 4194304 | bytes 4227584 | tf_op jit(solution)/shard_map/convert_element_type | solution.py:50
  17.1 1.5 copy.97
  18.6 3.8 %all-to-all-start = ((bf16[2,128,4096]{1,2,0:T(8,128)(2,1)}), bf16[2,128,4096]{1,2,0:T(8,128)(2,1)S(1)}, u32[]{:S(2)}, u32[]{:S(2)}) async-start(bf16[2,128,4096]{1,2,0:T(8,128)(2,1)} %bitcast.113), calls=%async_computation | async-start | bytes 4194304 | tf_op jit(solution)/shard_map/all_to_all | solution.py:53
  22.4 2.8 %all-to-all-done = bf16[2,128,4096]{1,2,0:T(8,128)(2,1)S(1)} async-done(((bf16[2,128,4096]{1,2,0:T(8,128)(2,1)}), bf16[2,128,4096]{1,2,0:T(8,128)(2,1)S(1)}, u32[]{:S(2)}, u32[]{:S(2)}) %all-to-all-start) | async-done | bytes 2097184 | tf_op jit(solution)/shard_map/all_to_all | solution.py:53
  25.2 2.8 %copy.98 = bf16[2,128,4096]{2,1,0:T(8,128)(2,1)} copy(bf16[2,128,4096]{1,2,0:T(8,128)(2,1)S(1)} %all-to-all-done) | data formatting | bytes 4194304 | tf_op jit(solution)/shard_map/all_to_all | solution.py:53
  28.0 2.3 %fusion = f16[256,4096]{1,0:T(8,128)(2,1)S(1)} fusion(bf16[256,4096]{1,0:T(8,128)(2,1)} %bitcast.114, bf16[128,256]{1,0:T(8,128)(2,1)S(1)} %get-tuple-element.40, bf16[128,256]{1,0:T(8,128)(2,1)S(1)} %get-tuple-element.39), kind=kOutput, calls=%fused_computation.3 | convolution fusion | flops 539230208 | bytes 4325376 | tf_op jit(solution)/shard_map/dot_general | solution.py:55
  30.3 0.5 slice_bitcast_fusion.1
  30.8 0.3 copy.126
  31.1 0.2 constant_dynamic-slice_fusion.6
  31.5 3.4 %collective-permute-start.3 = (f16[8,128,128]{2,1,0:T(8,128)(2,1)S(1)}, f16[8,128,128]{2,1,0:T(8,128)(2,1)S(1)}, u32[]{:S(2)}, u32[]{:S(2)}) collective-permute-start(f16[8,128,128]{2,1,0:T(8,128)(2,1)S(1)} %bitcast.119), channel_id=1, source_target_pairs={{0,96},{32,64},{64,32},{96,0},{1,97},{33,65},{65,33},{97,1},{2,98}... | collective-permute-start | bytes 786440 | tf_op jit(solution)/shard_map/ppermute | solution.py:32
  35.0 16.0 %collective-permute-start.2 = (f16[8,128,128]{2,1,0:T(8,128)(2,1)S(1)}, f16[8,128,128]{2,1,0:T(8,128)(2,1)S(1)}, u32[]{:S(2)}, u32[]{:S(2)}) collective-permute-start(f16[8,128,128]{2,1,0:T(8,128)(2,1)S(1)} %bitcast.120), channel_id=1, source_target_pairs={{0,64},{32,96},{64,0},{96,32},{1,65},{33,97},{65,1},{97,33},{2,66}... | collective-permute-start | bytes 786440 | tf_op jit(solution)/shard_map/ppermute | solution.py:32
  51.0 1.9 collective-permute-start.1
  53.0 10.5 %collective-permute-done.2 = f16[8,128,128]{2,1,0:T(8,128)(2,1)S(1)} collective-permute-done((f16[8,128,128]{2,1,0:T(8,128)(2,1)S(1)}, f16[8,128,128]{2,1,0:T(8,128)(2,1)S(1)}, u32[]{:S(2)}, u32[]{:S(2)}) %collective-permute-start.2) | collective-permute-done | bytes 262176 | tf_op jit(solution)/shard_map/ppermute | solution.py:32
  63.4 1.0 collective-permute-done.1
  64.4 0.9 fusion.7
  65.4 3.4 %all-to-all-start.1 = ((f16[8,128,128]{2,1,0:T(8,128)(2,1)}), f16[8,128,128]{2,1,0:T(8,128)(2,1)S(1)}, u32[]{:S(2)}, u32[]{:S(2)}) async-start(f16[8,128,128]{2,1,0:T(8,128)(2,1)} %fusion.7), calls=%async_computation.1 | async-start | bytes 524288 | tf_op jit(solution)/shard_map/all_to_all | solution.py:73
  68.8 0.3 copy.127
  69.1 1.6 copy.134
  70.7 9.9 %all-to-all-done.1 = f16[8,128,128]{2,1,0:T(8,128)(2,1)S(1)} async-done(((f16[8,128,128]{2,1,0:T(8,128)(2,1)}), f16[8,128,128]{2,1,0:T(8,128)(2,1)S(1)}, u32[]{:S(2)}, u32[]{:S(2)}) %all-to-all-start.1) | async-done | bytes 262176 | tf_op jit(solution)/shard_map/all_to_all | solution.py:73
  80.6 3.6 %all-to-all-start.2 = ((f16[8,4,128,128]{3,1,2,0:T(4,128)(2,1)}), f16[8,4,128,128]{3,1,2,0:T(4,128)(2,1)S(1)}, u32[]{:S(2)}, u32[]{:S(2)}) async-start(f16[8,4,128,128]{3,1,2,0:T(4,128)(2,1)} %bitcast.106), calls=%async_computation.2 | async-start | bytes 2097152 | tf_op jit(solution)/shard_map/all_to_all | solution.py:63
  84.9 0.8 copy.111
  85.7 0.1 copy.109
  85.8 0.1 copy.95
  85.9 0.1 copy.94
  86.0 1.0 constant_dynamic-slice_fusion
  87.0 0.1 copy.125
  87.1 0.1 copy.110
  87.3 24.2 %all-to-all-done.2 = f16[8,4,128,128]{3,1,2,0:T(4,128)(2,1)S(1)} async-done(((f16[8,4,128,128]{3,1,2,0:T(4,128)(2,1)}), f16[8,4,128,128]{3,1,2,0:T(4,128)(2,1)S(1)}, u32[]{:S(2)}, u32[]{:S(2)}) %all-to-all-start.2) | async-done | bytes 1048608 | tf_op jit(solution)/shard_map/all_to_all | solution.py:63
  111.5 0.3 convert_reduce_fusion
  111.8 3.8 %collective-permute-start.6 = (f16[128,128]{1,0:T(8,128)(2,1)S(1)}, f16[128,128]{1,0:T(8,128)(2,1)S(1)}, u32[]{:S(2)}, u32[]{:S(2)}) collective-permute-start(f16[128,128]{1,0:T(8,128)(2,1)S(1)} %get-tuple-element.37), channel_id=1, source_target_pairs={{0,96},{32,64},{64,32},{96,0},{1,97},{33,65},{65,33},{97,1},{2,98}... | collective-permute-start | bytes 98312 | tf_op jit(solution)/shard_map/ppermute | solution.py:32
  115.7 8.0 %collective-permute-start.5 = (f16[128,128]{1,0:T(8,128)(2,1)S(1)}, f16[128,128]{1,0:T(8,128)(2,1)S(1)}, u32[]{:S(2)}, u32[]{:S(2)}) collective-permute-start(f16[128,128]{1,0:T(8,128)(2,1)S(1)} %get-tuple-element.38), channel_id=1, source_target_pairs={{0,64},{32,96},{64,0},{96,32},{1,65},{33,97},{65,1},{97,33},{2,66}... | collective-permute-start | bytes 98312 | tf_op jit(solution)/shard_map/ppermute | solution.py:32
  123.7 1.9 collective-permute-start.4
  125.6 3.8 %collective-permute-done.4 = f16[128,128]{1,0:T(8,128)(2,1)S(1)} collective-permute-done((f16[128,128]{1,0:T(8,128)(2,1)S(1)}, f16[128,128]{1,0:T(8,128)(2,1)S(1)}, u32[]{:S(2)}, u32[]{:S(2)}) %collective-permute-start.4) | collective-permute-done | bytes 32800 | tf_op jit(solution)/shard_map/ppermute | solution.py:32
  129.5 0.6 multiply_reduce_fusion
  130.1 1.3 broadcast_in_dim.14
  131.4 5.4 %all-to-all-start.3 = ((f32[128,1,128]{2,1,0:T(1,128)}), f32[128,1,128]{2,1,0:T(1,128)S(1)}, u32[]{:S(2)}, u32[]{:S(2)}) async-start(f32[128,1,128]{2,1,0:T(1,128)} %broadcast_in_dim.14), calls=%async_computation.3 | async-start | bytes 131072 | tf_op jit(solution)/shard_map/all_to_all | solution.py:85
  136.8 45.1 %all-reduce.2.cloned.1.call-done = f32[128,256]{0,1:T(8,128)} async-done(((f32[128,256]{0,1:T(8,128)}), f32[128,256]{0,1:T(8,128)}) %all-reduce.2.cloned.1.call-update) | async-done | bytes 131088 | tf_op jit(solution)/shard_map/psum | solution.py:103
  181.9 0.9 bitcast_add_fusion.1
  182.9 0.8 copy.116
  183.6 0.8 copy.117
  184.4 0.7 slice_reduce_fusion
  185.8 0.1 fusion.20
  185.9 0.8 copy.113
  186.7 0.8 copy.114
  187.5 0.8 copy.115
  (31 shorter events, 0.5 us)
Async XLA Ops:
  7.2 77.7 %copy-start = (f32[1,8,128,256]{3,2,1,0:T(8,128)S(1)}, f32[1,8,128,256]{3,2,1,0:T(8,128)}, u32[]{:S(2)}) copy-start(f32[1,8,128,256]{3,2,1,0:T(8,128)} %param.16) | copy-start | bytes 3145732
  7.2 5.3 %copy-start.5 = (bf16[8192]{0:T(1024)(128)(2,1)S(1)}, bf16[8192]{0:T(1024)(128)(2,1)}, u32[]{:S(2)}) copy-start(bf16[8192]{0:T(1024)(128)(2,1)} %param.11) | copy-start | bytes 49156
  7.2 20.8 %collective-permute-start = (bf16[128,256]{1,0:T(8,128)(2,1)}, bf16[128,256]{1,0:T(8,128)(2,1)S(1)}, u32[]{:S(2)}, u32[]{:S(2)}) collective-permute-start(bf16[128,256]{1,0:T(8,128)(2,1)} %param.12), channel_id=1, source_target_pairs={{0,2},{2,0},{1,3},{3,1},{4,6},{6,4},{5,7},{7,5},{8,10},{10,8},{9,1... | collective-permute-start | bytes 196616 | tf_op jit(solution)/shard_map/ppermute | solution.py:37
  18.6 6.6 %all-to-all-start = ((bf16[2,128,4096]{1,2,0:T(8,128)(2,1)}), bf16[2,128,4096]{1,2,0:T(8,128)(2,1)S(1)}, u32[]{:S(2)}, u32[]{:S(2)}) async-start(bf16[2,128,4096]{1,2,0:T(8,128)(2,1)} %bitcast.113), calls=%async_computation | async-start | bytes 4194304 | tf_op jit(solution)/shard_map/all_to_all | solution.py:53
  22.4 5.6 %copy-start.4 = (bf16[128,256]{1,0:T(8,128)(2,1)S(1)}, bf16[128,256]{1,0:T(8,128)(2,1)}, u32[]{:S(2)}) copy-start(bf16[128,256]{1,0:T(8,128)(2,1)} %param.12) | copy-start | bytes 196612
  31.5 21.5 %collective-permute-start.3 = (f16[8,128,128]{2,1,0:T(8,128)(2,1)S(1)}, f16[8,128,128]{2,1,0:T(8,128)(2,1)S(1)}, u32[]{:S(2)}, u32[]{:S(2)}) collective-permute-start(f16[8,128,128]{2,1,0:T(8,128)(2,1)S(1)} %bitcast.119), channel_id=1, source_target_pairs={{0,96},{32,64},{64,32},{96,0},{1,97},{33,65},{65,33},{97,1},{2,98}... | collective-permute-start | bytes 786440 | tf_op jit(solution)/shard_map/ppermute | solution.py:32
  35.0 28.5 %collective-permute-start.2 = (f16[8,128,128]{2,1,0:T(8,128)(2,1)S(1)}, f16[8,128,128]{2,1,0:T(8,128)(2,1)S(1)}, u32[]{:S(2)}, u32[]{:S(2)}) collective-permute-start(f16[8,128,128]{2,1,0:T(8,128)(2,1)S(1)} %bitcast.120), channel_id=1, source_target_pairs={{0,64},{32,96},{64,0},{96,32},{1,65},{33,97},{65,1},{97,33},{2,66}... | collective-permute-start | bytes 786440 | tf_op jit(solution)/shard_map/ppermute | solution.py:32
  51.0 13.4 %collective-permute-start.1 = (f16[8,128,128]{2,1,0:T(8,128)(2,1)S(1)}, f16[8,128,128]{2,1,0:T(8,128)(2,1)S(1)}, u32[]{:S(2)}, u32[]{:S(2)}) collective-permute-start(f16[8,128,128]{2,1,0:T(8,128)(2,1)S(1)} %bitcast.121), channel_id=1, source_target_pairs={{0,32},{32,0},{64,96},{96,64},{1,33},{33,1},{65,97},{97,65},{2,34}... | collective-permute-start | bytes 786440 | tf_op jit(solution)/shard_map/ppermute | solution.py:32
  65.4 15.3 %all-to-all-start.1 = ((f16[8,128,128]{2,1,0:T(8,128)(2,1)}), f16[8,128,128]{2,1,0:T(8,128)(2,1)S(1)}, u32[]{:S(2)}, u32[]{:S(2)}) async-start(f16[8,128,128]{2,1,0:T(8,128)(2,1)} %fusion.7), calls=%async_computation.1 | async-start | bytes 524288 | tf_op jit(solution)/shard_map/all_to_all | solution.py:73
  69.1 16.6 %copy-start.1 = (f32[1,128,256]{2,1,0:T(8,128)S(1)}, f32[1,128,256]{2,1,0:T(8,128)}, u32[]{:S(2)}) copy-start(f32[1,128,256]{2,1,0:T(8,128)} %param.15) | copy-start | bytes 393220
  69.1 16.7 %copy-start.2 = (f32[1,128,256]{2,1,0:T(8,128)S(1)}, f32[1,128,256]{2,1,0:T(8,128)}, u32[]{:S(2)}) copy-start(f32[1,128,256]{2,1,0:T(8,128)} %param.14) | copy-start | bytes 393220
  70.7 15.2 %copy-start.3 = (f32[1,128,256]{2,1,0:T(8,128)S(1)}, f32[1,128,256]{2,1,0:T(8,128)}, u32[]{:S(2)}) copy-start(f32[1,128,256]{2,1,0:T(8,128)} %param.13) | copy-start | bytes 393220
  80.6 30.9 %all-to-all-start.2 = ((f16[8,4,128,128]{3,1,2,0:T(4,128)(2,1)}), f16[8,4,128,128]{3,1,2,0:T(4,128)(2,1)S(1)}, u32[]{:S(2)}, u32[]{:S(2)}) async-start(f16[8,4,128,128]{3,1,2,0:T(4,128)(2,1)} %bitcast.106), calls=%async_computation.2 | async-start | bytes 2097152 | tf_op jit(solution)/shard_map/all_to_all | solution.py:63
  84.2 97.7 %all-reduce.2.cloned.1.call-start = ((), (), s32[]{:S(2)}) async-start(), calls=%async_computation.4 | async-start | bytes 262144 | tf_op jit(solution)/shard_map/psum | solution.py:103
  111.8 13.8 %collective-permute-start.6 = (f16[128,128]{1,0:T(8,128)(2,1)S(1)}, f16[128,128]{1,0:T(8,128)(2,1)S(1)}, u32[]{:S(2)}, u32[]{:S(2)}) collective-permute-start(f16[128,128]{1,0:T(8,128)(2,1)S(1)} %get-tuple-element.37), channel_id=1, source_target_pairs={{0,96},{32,64},{64,32},{96,0},{1,97},{33,65},{65,33},{97,1},{2,98}... | collective-permute-start | bytes 98312 | tf_op jit(solution)/shard_map/ppermute | solution.py:32
  115.7 9.9 %collective-permute-start.5 = (f16[128,128]{1,0:T(8,128)(2,1)S(1)}, f16[128,128]{1,0:T(8,128)(2,1)S(1)}, u32[]{:S(2)}, u32[]{:S(2)}) collective-permute-start(f16[128,128]{1,0:T(8,128)(2,1)S(1)} %get-tuple-element.38), channel_id=1, source_target_pairs={{0,64},{32,96},{64,0},{96,32},{1,65},{33,97},{65,1},{97,33},{2,66}... | collective-permute-start | bytes 98312 | tf_op jit(solution)/shard_map/ppermute | solution.py:32
  123.7 5.8 %collective-permute-start.4 = (f16[128,128]{1,0:T(8,128)(2,1)S(1)}, f16[128,128]{1,0:T(8,128)(2,1)S(1)}, u32[]{:S(2)}, u32[]{:S(2)}) collective-permute-start(f16[128,128]{1,0:T(8,128)(2,1)S(1)} %get-tuple-element.36), channel_id=1, source_target_pairs={{0,32},{32,0},{64,96},{96,64},{1,33},{33,1},{65,97},{97,65},{2,34}... | collective-permute-start | bytes 98312 | tf_op jit(solution)/shard_map/ppermute | solution.py:32
  131.4 53.0 %all-to-all-start.3 = ((f32[128,1,128]{2,1,0:T(1,128)}), f32[128,1,128]{2,1,0:T(1,128)S(1)}, u32[]{:S(2)}, u32[]{:S(2)}) async-start(f32[128,1,128]{2,1,0:T(1,128)} %broadcast_in_dim.14), calls=%async_computation.3 | async-start | bytes 131072 | tf_op jit(solution)/shard_map/all_to_all | solution.py:85
Sparse Core Ops, SparseCore 0:
  87.9 93.9 all-reduce.1

commit v2 on v1

v2 whole, which is shorter than its diff:
```python
import jax
import jax.numpy as jnp
from jax import lax
from jax.experimental import pallas as pl
from jax.experimental.pallas import tpu as pltpu
from jax.sharding import Mesh, PartitionSpec as P

NORM_EPS = 1e-05
CLIP_RMS = 8.0
FIRST_BETA = 0.9
SECOND_BETA = 0.95
FIRST_FIX = 1.0 - 0.9**10
SECOND_FIX = 1.0 - 0.95**10
ADAM_EPS = 1e-08
INNER_RATE = 0.01
DECAY_WEIGHT = 0.1
OUTER_RATE = 0.7
OUTER_BETA = 0.9

XL, YN, CORES, XH = 4, 8, 2, 2
PEERS = XL * YN * CORES * XH
TOK, COLS, FEAT = 128, 256, 128
HALF = XL * YN * FEAT
WIDE = HALF * CORES
HC = COLS // 2
NORM_ROWS = 32
CHIP_SCALE = 2.0**-8
X_SCALE = 2.0**-10
Y_SCALE = 2.0**-11
VMEM_BYTES = 24 * 2**20


def outer_update(summed, global_layer, moment_layer, workers):
    pseudo = global_layer - summed / workers
    new_momentum = OUTER_BETA * moment_layer + pseudo
    new_fragment = global_layer - OUTER_RATE * (pseudo + OUTER_BETA * new_momentum)
    return (new_fragment, new_momentum)


def norm_kernel(place, hidden, gain, cot, keep, send):
    send[:, HALF:] = cot[...]
    widened = hidden[...].astype(jnp.float32)
    mean_square = jnp.sum(widened * widened, axis=1, keepdims=True) * (1.0 / WIDE)
    inverse = lax.rsqrt(mean_square + NORM_EPS)
    first_core = place[1] == 0
    for block in range(XL * YN):
        pair = []
        for core in range(CORES):
            at = (block * CORES + core) * FEAT
            part = hidden[:, at : at + FEAT].astype(jnp.float32)
            scale = gain[at : at + FEAT].astype(jnp.float32)[None, :]
            pair.append((part * inverse * scale).astype(jnp.bfloat16))
        out = slice(block * FEAT, (block + 1) * FEAT)
        keep[:, out] = jnp.where(first_core, pair[0], pair[1])
        send[:, out] = jnp.where(first_core, pair[1], pair[0])


def split_norm(place, hidden_in, norm_gain, cot):
    def rows(width):
        return pl.BlockSpec((NORM_ROWS, width), lambda i, place: (i, 0))

    return pl.pallas_call(
        norm_kernel,
        grid_spec=pltpu.PrefetchScalarGridSpec(
            num_scalar_prefetch=1,
            grid=(TOK // NORM_ROWS,),
            in_specs=[
                rows(WIDE),
                pl.BlockSpec((WIDE,), lambda i, place: (0,)),
                rows(COLS),
            ],
            out_specs=[rows(HALF), rows(HALF + COLS)],
        ),
        out_shape=[
            pltpu.HBM((TOK, HALF), jnp.bfloat16),
            pltpu.HBM((TOK, HALF + COLS), jnp.bfloat16),
        ],
        cost_estimate=pl.CostEstimate(
            flops=8 * TOK * WIDE, bytes_accessed=4 * TOK * WIDE, transcendentals=TOK
        ),
        compiler_params=pltpu.CompilerParams(vmem_limit_bytes=VMEM_BYTES),
        name="split_norm",
    )(place, hidden_in, norm_gain, cot)


def partial_kernel(place, keep, recv, cot, other_cot, x_out, y_out, turned):
    @pl.when(pl.program_id(0) == 0)
    def _():
        turned[:, :TOK] = cot[...].T
        turned[:, TOK:] = other_cot[...].T

    contract = (((1,), (0,)), ((), ()))
    product = lax.dot_general(
        turned[:, :TOK], keep[...], contract, preferred_element_type=jnp.float32
    ) + lax.dot_general(
        turned[:, TOK:], recv[...], contract, preferred_element_type=jnp.float32
    )
    product = product * CHIP_SCALE
    for row in range(YN):
        block = product[:, row * FEAT : (row + 1) * FEAT]
        x_out[0, row] = block[:HC]
        y_out[row, 0] = block[HC:]


def chip_partial(place, keep, recv, cot):
    chunk = pl.BlockSpec((TOK, YN * FEAT), lambda k, place: (0, place[0] ^ k))
    mine = pl.BlockSpec((TOK, COLS), lambda k, place: (0, 0))
    other = pl.BlockSpec((TOK, COLS), lambda k, place: (0, HALF // COLS))
    return pl.pallas_call(
        partial_kernel,
        grid_spec=pltpu.PrefetchScalarGridSpec(
            num_scalar_prefetch=1,
            grid=(XL,),
            in_specs=[chunk, chunk, mine, other],
            out_specs=[
                pl.BlockSpec((1, YN, HC, FEAT), lambda k, place: (k, 0, 0, 0)),
                pl.BlockSpec((YN, 1, HC, FEAT), lambda k, place: (0, k, 0, 0)),
            ],
            scratch_shapes=[pltpu.VMEM((COLS, CORES * TOK), jnp.bfloat16)],
        ),
        out_shape=[
            jax.ShapeDtypeStruct((XL, YN, HC, FEAT), jnp.float32),
            jax.ShapeDtypeStruct((YN, XL, HC, FEAT), jnp.float32),
        ],
        cost_estimate=pl.CostEstimate(
            flops=4 * TOK * HALF * COLS, bytes_accessed=6 * 2**20, transcendentals=0
        ),
        compiler_params=pltpu.CompilerParams(vmem_limit_bytes=VMEM_BYTES),
        name="chip_partial",
    )(place, keep, recv, cot, recv)


def square_kernel(top, bottom, gradient, rows):
    upper, lower = top[...] * (1.0 / X_SCALE), bottom[...] * (1.0 / Y_SCALE)
    gradient[:, :HC] = upper.T
    gradient[:, HC:] = lower.T
    total = jnp.sum(upper * upper + lower * lower)
    rows[...] = jnp.full(rows.shape, total, jnp.float32)


def turn_and_square(top, bottom):
    return pl.pallas_call(
        square_kernel,
        in_specs=[pl.BlockSpec(memory_space=pltpu.VMEM)] * 2,
        out_specs=[pl.BlockSpec(memory_space=pltpu.VMEM)] * 2,
        out_shape=[
            jax.ShapeDtypeStruct((FEAT, COLS), jnp.float32),
            jax.ShapeDtypeStruct((PEERS, 1, 128), jnp.float32),
        ],
        cost_estimate=pl.CostEstimate(
            flops=4 * FEAT * COLS, bytes_accessed=2**18, transcendentals=0
        ),
        name="turn_and_square",
    )(top, bottom)


def update_kernel(rows, gradient, params, first, second, out_params, out_first, out_second):
    total_square = jnp.sum(jnp.sum(rows[...], axis=0), axis=1, keepdims=True) * (1.0 / 128)
    entries = FEAT * COLS * PEERS
    factor = jnp.minimum(1.0, CLIP_RMS * lax.rsqrt(total_square * (1.0 / entries) + 1e-06))
    clipped = factor * gradient[...]
    old = params[0]
    new_first = FIRST_BETA * first[0] + (1.0 - FIRST_BETA) * clipped
    new_second = SECOND_BETA * second[0] + (1.0 - SECOND_BETA) * clipped * clipped
    direction = new_first * (1.0 / FIRST_FIX) / (
        jnp.sqrt(new_second * (1.0 / SECOND_FIX)) + ADAM_EPS
    )
    out_params[0] = old - INNER_RATE * (direction + DECAY_WEIGHT * old)
    out_first[0] = new_first
    out_second[0] = new_second


def inner_update(rows, gradient, params, first, second):
    vmem = pl.BlockSpec(memory_space=pltpu.VMEM)
    block = jax.ShapeDtypeStruct((1, FEAT, COLS), jnp.float32)
    return pl.pallas_call(
        update_kernel,
        in_specs=[vmem] * 5,
        out_specs=[vmem] * 3,
        out_shape=[block, block, block],
        cost_estimate=pl.CostEstimate(
            flops=16 * FEAT * COLS, bytes_accessed=2**20, transcendentals=2 * FEAT * COLS
        ),
        name="inner_update",
    )(rows, gradient, params, first, second)


def swap_x(block, k):
    return lax.ppermute(block, "xl", [(i, i ^ k) for i in range(XL)])


def add_replica(value, step):
    return value + lax.ppermute(value, "z", [(i, i ^ step) for i in range(8)])


def worker_gradient(hidden_in, norm_gain, key_cotangent, local_layer):
    place = jnp.stack([lax.axis_index("xl"), lax.axis_index("c")]).astype(jnp.int32)
    local_layer = add_replica(local_layer, 1)
    keep, send = split_norm(place, hidden_in, norm_gain, key_cotangent)
    recv = lax.ppermute(send, "c", [(0, 1), (1, 0)])
    recv, local_layer = lax.optimization_barrier((recv, local_layer))
    x_wide, y_wide = chip_partial(place, keep, recv, key_cotangent)

    y_parts = lax.all_to_all(y_wide.astype(jnp.float16), "y", 0, 0, tiled=True)
    x_parts = [x_wide[k].astype(jnp.float16) for k in range(1, XL)]
    x_parts, local_layer = lax.optimization_barrier((x_parts, local_layer))
    x_sum = x_wide[0]
    for k in range(1, XL):
        x_sum = x_sum + swap_x(x_parts[k - 1], k).astype(jnp.float32)
    summed = add_replica(local_layer, 2)
    x_sum = (x_sum * (X_SCALE / CHIP_SCALE)).astype(jnp.float16)
    x_sum, y_parts, summed = lax.optimization_barrier((x_sum, y_parts, summed))
    y_sum = jnp.sum(y_parts.astype(jnp.float32) * (Y_SCALE / CHIP_SCALE), axis=0)

    top = lax.all_to_all(x_sum, "y", 0, 0, tiled=True)
    bottom = y_sum[0]
    for k in range(1, XL):
        bottom = bottom + swap_x(y_sum[k].astype(jnp.float16), k).astype(jnp.float32)
    top = jnp.sum(top.astype(jnp.float32), axis=0)
    return top, bottom, add_replica(summed, 4)


def on_device(
    hidden_in,
    norm_gain,
    key_cotangent,
    inner_params,
    inner_first,
    inner_second,
    frag_local,
    frag_global,
    outer_momentum,
    frag_index,
):
    layer_index = frag_index[0]
    local_layer = lax.dynamic_index_in_dim(frag_local[0], layer_index, 0, keepdims=False)
    top, bottom, summed = worker_gradient(hidden_in, norm_gain, key_cotangent, local_layer)
    gradient, rows = turn_and_square(top, bottom)
    rows = lax.all_to_all(rows, ("xl", "y", "c", "xh"), 0, 0, tiled=True)
    new_params, new_first, new_second = inner_update(
        rows, gradient, inner_params, inner_first, inner_second
    )

    global_layer = lax.dynamic_index_in_dim(frag_global, layer_index, 0, keepdims=False)
    moment_layer = lax.dynamic_index_in_dim(outer_momentum, layer_index, 0, keepdims=False)
    workers = lax.axis_size("z")
    new_fragment, new_momentum = outer_update(summed, global_layer, moment_layer, workers)
    return (new_params, new_first, new_second, new_fragment, new_momentum)


def solution(mesh):
    workers = mesh.shape["replica"]
    devices = mesh.devices.reshape(workers, XL, YN, CORES, XH)
    split = Mesh(devices, ("z", "xl", "y", "c", "xh"))
    fsdp = ("xl", "y", "c")
    return jax.shard_map(
        on_device,
        mesh=split,
        in_specs=(
            P(("z",) + fsdp, None),
            P(),
            P(("z",) + fsdp, "xh"),
            P("z", fsdp, "xh"),
            P("z", fsdp, "xh"),
            P("z", fsdp, "xh"),
            P("z", None, fsdp, "xh"),
            P(None, fsdp, "xh"),
            P(None, fsdp, "xh"),
            P(),
        ),
        out_specs=(
            P("z", fsdp, "xh"),
            P("z", fsdp, "xh"),
            P("z", fsdp, "xh"),
            P(fsdp, "xh"),
            P(fsdp, "xh"),
        ),
        check_vma=False,
    )
```

time: 196 us -> 128 us (0.65)
  the two profiles are of different devices: /device:TPU:2 before, /device:TPU:1 now
where the time goes in v2:
time: 128 us; the launch traced here: 127 us
  starting transfers between devices  71.5 us (56%)
  waiting for transfers between devices  31.3 us (24%)
  Pallas kernels  10 us (8%)
  other arithmetic  6.57 us (5%)
  local copies, waits for them, and re-layouts  6.14 us (5%)
  between operations  1.52 us (1%)
    ppermute x6, starting transfers between devices, swap_x(): return lax.ppermute(block, 'xl', [(i, i ^ k) for i in range(XL)])  20.4 us
    ppermute x1, starting transfers between devices, worker_gradient(): recv = lax.ppermute(send, 'c', [(0, 1), (1, 0)])  16.1 us
    all_to_all x1, starting transfers between devices, on_device(): rows = lax.all_to_all(rows, ('xl', 'y', 'c', 'xh'), 0, 0, tiled=True)  16 us
    ppermute x3, waiting for transfers between devices, add_replica(): return value + lax.ppermute(value, 'z', [(i, i ^ step) for i in range(8)])  13.6 us
    ppermute x3, starting transfers between devices, add_replica(): return value + lax.ppermute(value, 'z', [(i, i ^ step) for i in range(8)])  12 us
    all_to_all x1, waiting for transfers between devices, on_device(): rows = lax.all_to_all(rows, ('xl', 'y', 'c', 'xh'), 0, 0, tiled=True)  9.62 us
    unnamed x12, local copies, waits for them, and re-layouts  4.99 us
    all_to_all x1, waiting for transfers between devices, worker_gradient(): y_parts = lax.all_to_all(y_wide.astype(jnp.float16), 'y', 0, 0, tiled=True)  4.76 us
  transfers between devices with their start and end apart: 13, of which 5 were waited for; matrix products, arithmetic and copies ran while one was open for 5% of the time, Pallas kernels for 1%

profile of v2, /device:TPU:1, one launch (start us, length us, event | category | flops | bytes accessed | tf_op | source)
XLA Modules:
  0.0 127.1 jit_solution(1101178044080858025)
XLA Ops:
  0.6 0.1 pad_add_fusion.place
  0.7 1.6 %copy-done = bf16[128,8192]{1,0:T(8,128)(2,1)S(1)} copy-done((bf16[128,8192]{1,0:T(8,128)(2,1)S(1)}, bf16[128,8192]{1,0:T(8,128)(2,1)}, u32[]{:S(2)}) %copy-start) | copy-done | bytes 2097176
  2.3 0.8 copy-done.2
  3.1 0.7 copy-done.4
  3.9 3.3 %split_norm.1 = (bf16[128,4096]{1,0:T(8,128)(2,1)}, bf16[128,4352]{1,0:T(8,128)(2,1)}) custom-call(s32[2]{0:T(128)S(1)} %pad_add_fusion.place, bf16[128,8192]{1,0:T(8,128)(2,1)S(1)} %copy-done, bf16[8192]{0:T(1024)(128)(2,1)S(1)} %copy-done.4, bf16[128,256]{1,0:T(8,128)(2,1)S(1)} %copy-done.2), custom_call_target="tpu_custom_call" | custom-call | flops 8388608 | bytes 4194304 | tf_op jit(solution)/shard_map/split_norm/pallas_call | solution.py:62
  7.1 16.1 %collective-permute-start = (bf16[128,4352]{1,0:T(8,128)(2,1)}, bf16[128,4352]{1,0:T(8,128)(2,1)S(1)}, u32[]{:S(2)}, u32[]{:S(2)}) collective-permute-start(bf16[128,4352]{1,0:T(8,128)(2,1)} %get-tuple-element.24), channel_id=1, source_target_pairs={{0,2},{2,0},{1,3},{3,1},{4,6},{6,4},{5,7},{7,5},{8,10},{10,8},{9,1... | collective-permute-start | bytes 3342344 | tf_op jit(solution)/shard_map/ppermute | solution.py:200
  23.9 0.9 dynamic-slice_bitcast_fusion
  24.8 1.9 %collective-permute-start.1 = (f32[128,256]{1,0:T(8,128)S(1)}, f32[128,256]{1,0:T(8,128)S(1)}, u32[]{:S(2)}, u32[]{:S(2)}) collective-permute-start(f32[128,256]{1,0:T(8,128)S(1)} %dynamic-slice_bitcast_fusion), channel_id=1, source_target_pairs={{0,128},{128,0},{256,384},{384,256},{512,640},{640,512},{768,896},... | collective-permute-start | bytes 393224 | tf_op jit(solution)/shard_map/ppermute | solution.py:193
  26.7 5.1 %collective-permute-done.1 = f32[128,256]{1,0:T(8,128)S(1)} collective-permute-done((f32[128,256]{1,0:T(8,128)S(1)}, f32[128,256]{1,0:T(8,128)S(1)}, u32[]{:S(2)}, u32[]{:S(2)}) %collective-permute-start.1) | collective-permute-done | bytes 131104 | tf_op jit(solution)/shard_map/ppermute | solution.py:193
  31.8 0.9 fusion.7
  32.7 0.0 collective-permute-done.recv.other_cot
  32.7 0.0 copy-done.3
  32.7 0.0 copy-start.1
  32.7 1.2 copy-done.1
  34.0 2.8 %chip_partial.1 = (f32[4,8,128,128]{3,2,1,0:T(8,128)S(1)}, f32[8,4,128,128]{3,2,1,0:T(8,128)S(1)}) custom-call(s32[2]{0:T(128)S(1)} %pad_add_fusion.place, bf16[128,4096]{1,0:T(8,128)(2,1)S(1)} %copy-done.1, bf16[128,4352]{1,0:T(8,128)(2,1)S(1)} %collective-permute-done.recv.other_cot, bf16[128,256]{1,0:T(8,128)(2,1)S(1)} %copy-done.3, ...), custom_call_target="tpu_custom_call" | custom-call | flops 536870912 | bytes 6291456 | tf_op jit(solution)/shard_map/chip_partial/pallas_call | solution.py:109
  36.8 1.2 convert_element_type.61
  38.0 3.6 %all-to-all-start = ((f16[8,4,128,128]{3,2,1,0:T(8,128)(2,1)}), f16[8,4,128,128]{3,2,1,0:T(8,128)(2,1)S(1)}, u32[]{:S(2)}, u32[]{:S(2)}) async-start(f16[8,4,128,128]{3,2,1,0:T(8,128)(2,1)} %convert_element_type.61), calls=%async_computation | async-start | bytes 2097152 | tf_op jit(solution)/shard_map/all_to_all | solution.py:204
  41.6 0.2 convert.10
  41.8 0.2 slice_bitcast_fusion
  42.0 1.9 %collective-permute-start.2 = (f16[8,128,128]{2,1,0:T(8,128)(2,1)S(1)}, f16[8,128,128]{2,1,0:T(8,128)(2,1)S(1)}, u32[]{:S(2)}, u32[]{:S(2)}) collective-permute-start(f16[8,128,128]{2,1,0:T(8,128)(2,1)S(1)} %get-tuple-element.28), channel_id=1, source_target_pairs={{0,32},{32,0},{64,96},{96,64},{1,33},{33,1},{65,97},{97,65},{2,34}... | collective-permute-start | bytes 786440 | tf_op jit(solution)/shard_map/ppermute | solution.py:189
  43.9 1.9 %collective-permute-start.3 = (f16[8,128,128]{2,1,0:T(8,128)(2,1)S(1)}, f16[8,128,128]{2,1,0:T(8,128)(2,1)S(1)}, u32[]{:S(2)}, u32[]{:S(2)}) collective-permute-start(f16[8,128,128]{2,1,0:T(8,128)(2,1)S(1)} %get-tuple-element.29), channel_id=1, source_target_pairs={{0,64},{32,96},{64,0},{96,32},{1,65},{33,97},{65,1},{97,33},{2,66}... | collective-permute-start | bytes 786440 | tf_op jit(solution)/shard_map/ppermute | solution.py:189
  45.9 5.4 %collective-permute-start.4 = (f16[8,128,128]{2,1,0:T(8,128)(2,1)S(1)}, f16[8,128,128]{2,1,0:T(8,128)(2,1)S(1)}, u32[]{:S(2)}, u32[]{:S(2)}) collective-permute-start(f16[8,128,128]{2,1,0:T(8,128)(2,1)S(1)} %get-tuple-element.30), channel_id=1, source_target_pairs={{0,96},{32,64},{64,32},{96,0},{1,97},{33,65},{65,33},{97,1},{2,98}... | collective-permute-start | bytes 786440 | tf_op jit(solution)/shard_map/ppermute | solution.py:189
  51.3 1.9 %collective-permute-start.5 = (f32[128,256]{1,0:T(8,128)S(1)}, f32[128,256]{1,0:T(8,128)S(1)}, u32[]{:S(2)}, u32[]{:S(2)}) collective-permute-start(f32[128,256]{1,0:T(8,128)S(1)} %fusion.7), channel_id=1, source_target_pairs={{0,256},{128,384},{256,0},{384,128},{512,768},{640,896},{768,512},... | collective-permute-start | bytes 393224 | tf_op jit(solution)/shard_map/ppermute | solution.py:193
  53.2 8.6 %collective-permute-done.5 = f32[128,256]{1,0:T(8,128)S(1)} collective-permute-done((f32[128,256]{1,0:T(8,128)S(1)}, f32[128,256]{1,0:T(8,128)S(1)}, u32[]{:S(2)}, u32[]{:S(2)}) %collective-permute-start.5) | collective-permute-done | bytes 131104 | tf_op jit(solution)/shard_map/ppermute | solution.py:193
  61.8 0.0 collective-permute-done.2
  61.8 3.3 %collective-permute-done.3 = f16[8,128,128]{2,1,0:T(8,128)(2,1)S(1)} collective-permute-done((f16[8,128,128]{2,1,0:T(8,128)(2,1)S(1)}, f16[8,128,128]{2,1,0:T(8,128)(2,1)S(1)}, u32[]{:S(2)}, u32[]{:S(2)}) %collective-permute-start.3) | collective-permute-done | bytes 262176 | tf_op jit(solution)/shard_map/ppermute | solution.py:189
  65.1 0.0 collective-permute-done.4
  65.1 0.9 fusion.3
  66.0 4.8 %all-to-all-done = f16[8,4,128,128]{3,2,1,0:T(8,128)(2,1)S(1)} async-done(((f16[8,4,128,128]{3,2,1,0:T(8,128)(2,1)}), f16[8,4,128,128]{3,2,1,0:T(8,128)(2,1)S(1)}, u32[]{:S(2)}, u32[]{:S(2)}) %all-to-all-start) | async-done | bytes 1048608 | tf_op jit(solution)/shard_map/all_to_all | solution.py:204
  70.7 3.4 %all-to-all-start.1 = ((f16[8,128,128]{2,1,0:T(8,128)(2,1)}), f16[8,128,128]{2,1,0:T(8,128)(2,1)S(1)}, u32[]{:S(2)}, u32[]{:S(2)}) async-start(f16[8,128,128]{2,1,0:T(8,128)(2,1)} %fusion.3), calls=%async_computation.1 | async-start | bytes 524288 | tf_op jit(solution)/shard_map/all_to_all | solution.py:215
  74.2 0.2 multiply_reduce_fusion
  74.5 6.1 %collective-permute-start.6 = (f16[128,128]{1,0:T(8,128)(2,1)S(1)}, f16[128,128]{1,0:T(8,128)(2,1)S(1)}, u32[]{:S(2)}, u32[]{:S(2)}) collective-permute-start(f16[128,128]{1,0:T(8,128)(2,1)S(1)} %get-tuple-element.46), channel_id=1, source_target_pairs={{0,32},{32,0},{64,96},{96,64},{1,33},{33,1},{65,97},{97,65},{2,34}... | collective-permute-start | bytes 98312 | tf_op jit(solution)/shard_map/ppermute | solution.py:189
  80.6 2.7 %collective-permute-start.8 = (f16[128,128]{1,0:T(8,128)(2,1)S(1)}, f16[128,128]{1,0:T(8,128)(2,1)S(1)}, u32[]{:S(2)}, u32[]{:S(2)}) collective-permute-start(f16[128,128]{1,0:T(8,128)(2,1)S(1)} %get-tuple-element.47), channel_id=1, source_target_pairs={{0,96},{32,64},{64,32},{96,0},{1,97},{33,65},{65,33},{97,1},{2,98}... | collective-permute-start | bytes 98312 | tf_op jit(solution)/shard_map/ppermute | solution.py:189
  83.3 2.3 %collective-permute-start.7 = (f16[128,128]{1,0:T(8,128)(2,1)S(1)}, f16[128,128]{1,0:T(8,128)(2,1)S(1)}, u32[]{:S(2)}, u32[]{:S(2)}) collective-permute-start(f16[128,128]{1,0:T(8,128)(2,1)S(1)} %get-tuple-element.48), channel_id=1, source_target_pairs={{0,64},{32,96},{64,0},{96,32},{1,65},{33,97},{65,1},{97,33},{2,66}... | collective-permute-start | bytes 98312 | tf_op jit(solution)/shard_map/ppermute | solution.py:189
  85.6 8.2 %collective-permute-start.9 = (f32[128,256]{1,0:T(8,128)S(1)}, f32[128,256]{1,0:T(8,128)S(1)}, u32[]{:S(2)}, u32[]{:S(2)}) collective-permute-start(f32[128,256]{1,0:T(8,128)S(1)} %add.44), channel_id=1, source_target_pairs={{0,512},{128,640},{256,768},{384,896},{512,0},{640,128},{768,256},... | collective-permute-start | bytes 393224 | tf_op jit(solution)/shard_map/ppermute | solution.py:193
  93.8 0.0 collective-permute-done.6
  93.8 0.0 collective-permute-done.8
  93.8 0.0 collective-permute-done.7
  93.9 0.6 fusion.6.bottom
  94.5 0.0 all-to-all-done.1
  94.5 0.7 convert_reduce_fusion.top
  95.2 1.7 %turn_and_square.1 = (f32[128,256]{1,0:T(8,128)}, f32[128,1,128]{2,1,0:T(1,128)}) custom-call(f32[128,128]{1,0:T(8,128)} %convert_reduce_fusion.top, f32[128,128]{1,0:T(8,128)} %fusion.6.bottom), custom_call_target="tpu_custom_call" | custom-call | flops 131072 | bytes 262144 | tf_op jit(solution)/shard_map/turn_and_square/pallas_call | solution.py:142
  96.9 16.0 %all-to-all-start.2 = ((f32[128,1,128]{2,1,0:T(1,128)}), f32[128,1,128]{2,1,0:T(1,128)S(1)}, u32[]{:S(2)}, u32[]{:S(2)}) async-start(f32[128,1,128]{2,1,0:T(1,128)} %get-tuple-element.35), calls=%async_computation.2 | async-start | bytes 131072 | tf_op jit(solution)/shard_map/all_to_all | solution.py:239
  112.9 0.0 collective-permute-done.9
  113.0 1.7 %bitcast_subtract_fusion = (f32[128,256]{1,0:T(8,128)}, f32[128,256]{1,0:T(8,128)}) fusion(f32[8,128,256]{2,1,0:T(8,128)} %param.17, s32[]{:T(128)S(6)} %select_n.6, f32[128,256]{1,0:T(8,128)S(1)} %add.44, f32[128,256]{1,0:T(8,128)S(1)} %collective-permute-done.9, f32[8,128,256]{2,1,0:T(8,128)} %param.18), kind=kLoop, calls=%fused_computation.11 | loop fusion | flops 294912 | bytes 786436 | tf_op jit(solution)/shard_map/sub | solution.py:36
  114.7 9.6 %all-to-all-done.2.rows = f32[128,1,128]{2,1,0:T(1,128)S(1)} async-done(((f32[128,1,128]{2,1,0:T(1,128)}), f32[128,1,128]{2,1,0:T(1,128)S(1)}, u32[]{:S(2)}, u32[]{:S(2)}) %all-to-all-start.2) | async-done | bytes 65568 | tf_op jit(solution)/shard_map/all_to_all | solution.py:239
  124.3 0.6 copy-done.5
  124.9 2.2 %inner_update.1 = (f32[1,128,256]{2,1,0:T(8,128)}, f32[1,128,256]{2,1,0:T(8,128)}, f32[1,128,256]{2,1,0:T(8,128)}) custom-call(f32[128,1,128]{2,1,0:T(1,128)} %copy-done.5, f32[128,256]{1,0:T(8,128)} %get-tuple-element.36.gradient, f32[1,128,256]{2,1,0:T(8,128)} %params.1, f32[1,128,256]{2,1,0:T(8,128)} %first.1, f32[1,128,256]{2,1,0:T(8,128)} %second.1), custom_call_target="tpu_custom_call" | custom-call | flops 524288 | bytes 1048576 | tf_op jit(solution)/shard_map/inner_update/pallas_call | solution.py:176
  (8 shorter events, 0.1 us)
Async XLA Ops:
  0.7 1.6 %copy-start = (bf16[128,8192]{1,0:T(8,128)(2,1)S(1)}, bf16[128,8192]{1,0:T(8,128)(2,1)}, u32[]{:S(2)}) copy-start(bf16[128,8192]{1,0:T(8,128)(2,1)} %hidden.1) | copy-start | bytes 6291460
  2.3 0.8 copy-start.2
  3.1 0.7 copy-start.4
  3.9 28.9 %copy-start.3 = (bf16[128,256]{1,0:T(8,128)(2,1)S(1)}, bf16[128,256]{1,0:T(8,128)(2,1)}, u32[]{:S(2)}) copy-start(bf16[128,256]{1,0:T(8,128)(2,1)} %cot.3) | copy-start | bytes 196612
  7.1 25.6 %collective-permute-start = (bf16[128,4352]{1,0:T(8,128)(2,1)}, bf16[128,4352]{1,0:T(8,128)(2,1)S(1)}, u32[]{:S(2)}, u32[]{:S(2)}) collective-permute-start(bf16[128,4352]{1,0:T(8,128)(2,1)} %get-tuple-element.24), channel_id=1, source_target_pairs={{0,2},{2,0},{1,3},{3,1},{4,6},{6,4},{5,7},{7,5},{8,10},{10,8},{9,1... | collective-permute-start | bytes 3342344 | tf_op jit(solution)/shard_map/ppermute | solution.py:200
  24.8 7.0 %collective-permute-start.1 = (f32[128,256]{1,0:T(8,128)S(1)}, f32[128,256]{1,0:T(8,128)S(1)}, u32[]{:S(2)}, u32[]{:S(2)}) collective-permute-start(f32[128,256]{1,0:T(8,128)S(1)} %dynamic-slice_bitcast_fusion), channel_id=1, source_target_pairs={{0,128},{128,0},{256,384},{384,256},{512,640},{640,512},{768,896},... | collective-permute-start | bytes 393224 | tf_op jit(solution)/shard_map/ppermute | solution.py:193
  32.7 1.2 copy-start.1
  38.0 32.7 %all-to-all-start = ((f16[8,4,128,128]{3,2,1,0:T(8,128)(2,1)}), f16[8,4,128,128]{3,2,1,0:T(8,128)(2,1)S(1)}, u32[]{:S(2)}, u32[]{:S(2)}) async-start(f16[8,4,128,128]{3,2,1,0:T(8,128)(2,1)} %convert_element_type.61), calls=%async_computation | async-start | bytes 2097152 | tf_op jit(solution)/shard_map/all_to_all | solution.py:204
  42.0 19.8 %collective-permute-start.2 = (f16[8,128,128]{2,1,0:T(8,128)(2,1)S(1)}, f16[8,128,128]{2,1,0:T(8,128)(2,1)S(1)}, u32[]{:S(2)}, u32[]{:S(2)}) collective-permute-start(f16[8,128,128]{2,1,0:T(8,128)(2,1)S(1)} %get-tuple-element.28), channel_id=1, source_target_pairs={{0,32},{32,0},{64,96},{96,64},{1,33},{33,1},{65,97},{97,65},{2,34}... | collective-permute-start | bytes 786440 | tf_op jit(solution)/shard_map/ppermute | solution.py:189
  43.9 21.2 %collective-permute-start.3 = (f16[8,128,128]{2,1,0:T(8,128)(2,1)S(1)}, f16[8,128,128]{2,1,0:T(8,128)(2,1)S(1)}, u32[]{:S(2)}, u32[]{:S(2)}) collective-permute-start(f16[8,128,128]{2,1,0:T(8,128)(2,1)S(1)} %get-tuple-element.29), channel_id=1, source_target_pairs={{0,64},{32,96},{64,0},{96,32},{1,65},{33,97},{65,1},{97,33},{2,66}... | collective-permute-start | bytes 786440 | tf_op jit(solution)/shard_map/ppermute | solution.py:189
  45.9 19.3 %collective-permute-start.4 = (f16[8,128,128]{2,1,0:T(8,128)(2,1)S(1)}, f16[8,128,128]{2,1,0:T(8,128)(2,1)S(1)}, u32[]{:S(2)}, u32[]{:S(2)}) collective-permute-start(f16[8,128,128]{2,1,0:T(8,128)(2,1)S(1)} %get-tuple-element.30), channel_id=1, source_target_pairs={{0,96},{32,64},{64,32},{96,0},{1,97},{33,65},{65,33},{97,1},{2,98}... | collective-permute-start | bytes 786440 | tf_op jit(solution)/shard_map/ppermute | solution.py:189
  51.3 10.5 %collective-permute-start.5 = (f32[128,256]{1,0:T(8,128)S(1)}, f32[128,256]{1,0:T(8,128)S(1)}, u32[]{:S(2)}, u32[]{:S(2)}) collective-permute-start(f32[128,256]{1,0:T(8,128)S(1)} %fusion.7), channel_id=1, source_target_pairs={{0,256},{128,384},{256,0},{384,128},{512,768},{640,896},{768,512},... | collective-permute-start | bytes 393224 | tf_op jit(solution)/shard_map/ppermute | solution.py:193
  70.7 23.8 %all-to-all-start.1 = ((f16[8,128,128]{2,1,0:T(8,128)(2,1)}), f16[8,128,128]{2,1,0:T(8,128)(2,1)S(1)}, u32[]{:S(2)}, u32[]{:S(2)}) async-start(f16[8,128,128]{2,1,0:T(8,128)(2,1)} %fusion.3), calls=%async_computation.1 | async-start | bytes 524288 | tf_op jit(solution)/shard_map/all_to_all | solution.py:215
  74.5 19.4 %collective-permute-start.6 = (f16[128,128]{1,0:T(8,128)(2,1)S(1)}, f16[128,128]{1,0:T(8,128)(2,1)S(1)}, u32[]{:S(2)}, u32[]{:S(2)}) collective-permute-start(f16[128,128]{1,0:T(8,128)(2,1)S(1)} %get-tuple-element.46), channel_id=1, source_target_pairs={{0,32},{32,0},{64,96},{96,64},{1,33},{33,1},{65,97},{97,65},{2,34}... | collective-permute-start | bytes 98312 | tf_op jit(solution)/shard_map/ppermute | solution.py:189
  80.6 13.2 %collective-permute-start.8 = (f16[128,128]{1,0:T(8,128)(2,1)S(1)}, f16[128,128]{1,0:T(8,128)(2,1)S(1)}, u32[]{:S(2)}, u32[]{:S(2)}) collective-permute-start(f16[128,128]{1,0:T(8,128)(2,1)S(1)} %get-tuple-element.47), channel_id=1, source_target_pairs={{0,96},{32,64},{64,32},{96,0},{1,97},{33,65},{65,33},{97,1},{2,98}... | collective-permute-start | bytes 98312 | tf_op jit(solution)/shard_map/ppermute | solution.py:189
  83.3 10.5 %collective-permute-start.7 = (f16[128,128]{1,0:T(8,128)(2,1)S(1)}, f16[128,128]{1,0:T(8,128)(2,1)S(1)}, u32[]{:S(2)}, u32[]{:S(2)}) collective-permute-start(f16[128,128]{1,0:T(8,128)(2,1)S(1)} %get-tuple-element.48), channel_id=1, source_target_pairs={{0,64},{32,96},{64,0},{96,32},{1,65},{33,97},{65,1},{97,33},{2,66}... | collective-permute-start | bytes 98312 | tf_op jit(solution)/shard_map/ppermute | solution.py:189
  85.6 27.3 %collective-permute-start.9 = (f32[128,256]{1,0:T(8,128)S(1)}, f32[128,256]{1,0:T(8,128)S(1)}, u32[]{:S(2)}, u32[]{:S(2)}) collective-permute-start(f32[128,256]{1,0:T(8,128)S(1)} %add.44), channel_id=1, source_target_pairs={{0,512},{128,640},{256,768},{384,896},{512,0},{640,128},{768,256},... | collective-permute-start | bytes 393224 | tf_op jit(solution)/shard_map/ppermute | solution.py:193
  96.9 27.4 %all-to-all-start.2 = ((f32[128,1,128]{2,1,0:T(1,128)}), f32[128,1,128]{2,1,0:T(1,128)S(1)}, u32[]{:S(2)}, u32[]{:S(2)}) async-start(f32[128,1,128]{2,1,0:T(1,128)} %get-tuple-element.35), calls=%async_computation.2 | async-start | bytes 131072 | tf_op jit(solution)/shard_map/all_to_all | solution.py:239
  124.3 0.6 copy-start.5

commit v3 on v2

--- a/solution.py
+++ b/solution.py
@@ -1,3 +1,5 @@
+import functools
+
 import jax
 import jax.numpy as jnp
 from jax import lax
@@ -195,19 +197,23 @@
 
 def worker_gradient(hidden_in, norm_gain, key_cotangent, local_layer):
     place = jnp.stack([lax.axis_index("xl"), lax.axis_index("c")]).astype(jnp.int32)
-    local_layer = add_replica(local_layer, 1)
+    in_hbm = functools.partial(pltpu.with_memory_space_constraint, memory_space=pltpu.HBM)
+    hidden_in, norm_gain, key_cotangent = map(in_hbm, (hidden_in, norm_gain, key_cotangent))
+    far_layer = lax.ppermute(local_layer, "z", [(i, i ^ 4) for i in range(8)])
     keep, send = split_norm(place, hidden_in, norm_gain, key_cotangent)
     recv = lax.ppermute(send, "c", [(0, 1), (1, 0)])
-    recv, local_layer = lax.optimization_barrier((recv, local_layer))
-    x_wide, y_wide = chip_partial(place, keep, recv, key_cotangent)
-
-    y_parts = lax.all_to_all(y_wide.astype(jnp.float16), "y", 0, 0, tiled=True)
-    x_parts = [x_wide[k].astype(jnp.float16) for k in range(1, XL)]
-    x_parts, local_layer = lax.optimization_barrier((x_parts, local_layer))
-    x_sum = x_wide[0]
-    for k in range(1, XL):
-        x_sum = x_sum + swap_x(x_parts[k - 1], k).astype(jnp.float32)
-    summed = add_replica(local_layer, 2)
+    x_wide, y_wide = chip_partial(place, in_hbm(keep), recv, key_cotangent)
+
+    y_half = y_wide.astype(jnp.float16)
+    y_half, far_layer = lax.optimization_barrier((y_half, far_layer))
+    y_parts = lax.all_to_all(y_half, "y", 0, 0, tiled=True)
+    x_near = swap_x(x_wide[1].astype(jnp.float16), 1)
+    local_layer = local_layer + far_layer
+    x_near, local_layer = lax.optimization_barrier((x_near, local_layer))
+    x_sum = x_wide[0] + x_near.astype(jnp.float32)
+    for k in range(2, XL):
+        x_sum = x_sum + swap_x(x_wide[k].astype(jnp.float16), k).astype(jnp.float32)
+    summed = add_replica(add_replica(local_layer, 1), 2)
     x_sum = (x_sum * (X_SCALE / CHIP_SCALE)).astype(jnp.float16)
     x_sum, y_parts, summed = lax.optimization_barrier((x_sum, y_parts, summed))
     y_sum = jnp.sum(y_parts.astype(jnp.float32) * (Y_SCALE / CHIP_SCALE), axis=0)
@@ -217,7 +223,7 @@
     for k in range(1, XL):
         bottom = bottom + swap_x(y_sum[k].astype(jnp.float16), k).astype(jnp.float32)
     top = jnp.sum(top.astype(jnp.float32), axis=0)
-    return top, bottom, add_replica(summed, 4)
+    return top, bottom, summed
 
 
 def on_device(

time: 128 us -> 121 us (0.945)
  local copies, waits for them, and re-layouts: 6.14 us -> 1.78 us
  Pallas kernels: 10 us -> 13 us
  waiting for transfers between devices: 31.3 us -> 28.4 us
  starting transfers between devices: 71.5 us -> 68.9 us
    ppermute x3 -> x2, waiting for transfers between devices: 13.6 us -> 5.53 us  [add_replica(): return value + lax.ppermute(value, 'z', [(i, i ^ step) for i in range(8)])]
    ppermute x0 -> x1, waiting for transfers between devices: none -> 6.45 us  [worker_gradient(): far_layer = lax.ppermute(local_layer, 'z', [(i, i ^ 4) for i in range(8)])]
    unnamed x12 -> x2, local copies, waits for them, and re-layouts: 4.99 us -> 0.63 us
    ppermute x3 -> x2, starting transfers between devices: 12 us -> 7.7 us  [add_replica(): return value + lax.ppermute(value, 'z', [(i, i ^ step) for i in range(8)])]
    all_to_all x1, waiting for transfers between devices: 4.76 us -> 2.78 us  [worker_gradient(): y_parts = lax.all_to_all(y_half, 'y', 0, 0, tiled=True)]
    ppermute x0 -> x1, starting transfers between devices: none -> 1.92 us  [worker_gradient(): far_layer = lax.ppermute(local_layer, 'z', [(i, i ^ 4) for i in range(8)])]
    pallas_call x1, Pallas kernels: 3.28 us -> 5.02 us  [split_norm(): pl.pallas_call(norm_kernel, grid_spec=pltpu.PrefetchScalarGridSpec(num_sc...]
  transfers between devices with their start and end apart: 13 -> 13, of which waited for: 5 -> 9; matrix products, arithmetic and copies ran while one was open for 5% -> 6% of each run, Pallas kernels for 1% -> 3%
where the time goes in v3:
time: 121 us; the launch traced here: 120 us
  starting transfers between devices  68.9 us (57%)
  waiting for transfers between devices  28.4 us (23%)
  Pallas kernels  13 us (11%)
  other arithmetic  6.59 us (5%)
  local copies, waits for them, and re-layouts  1.78 us (1%)
  between operations  1.47 us (1%)
    ppermute x6, starting transfers between devices, swap_x(): return lax.ppermute(block, 'xl', [(i, i ^ k) for i in range(XL)])  21.2 us
    ppermute x1, starting transfers between devices, worker_gradient(): recv = lax.ppermute(send, 'c', [(0, 1), (1, 0)])  16.1 us
    all_to_all x1, starting transfers between devices, on_device(): rows = lax.all_to_all(rows, ('xl', 'y', 'c', 'xh'), 0, 0, tiled=True)  15 us
    all_to_all x1, waiting for transfers between devices, on_device(): rows = lax.all_to_all(rows, ('xl', 'y', 'c', 'xh'), 0, 0, tiled=True)  9.64 us
    ppermute x2, starting transfers between devices, add_replica(): return value + lax.ppermute(value, 'z', [(i, i ^ step) for i in range(8)])  7.7 us
    ppermute x1, waiting for transfers between devices, worker_gradient(): far_layer = lax.ppermute(local_layer, 'z', [(i, i ^ 4) for i in range(8)])  6.45 us
    ppermute x2, waiting for transfers between devices, add_replica(): return value + lax.ppermute(value, 'z', [(i, i ^ step) for i in range(8)])  5.53 us
    pallas_call x1, Pallas kernels, split_norm(): pl.pallas_call(norm_kernel, grid_spec=pltpu.PrefetchScalarGridSpec(num_sc...  5.02 us
  transfers between devices with their start and end apart: 13, of which 9 were waited for; matrix products, arithmetic and copies ran while one was open for 6% of the time, Pallas kernels for 3%

profile of v3, /device:TPU:1, one launch (start us, length us, event | category | flops | bytes accessed | tf_op | source)
XLA Modules:
  0.0 120.1 jit_solution(8586791561310320059)
XLA Ops:
  0.6 0.1 pad_add_fusion.place
  0.7 5.0 %split_norm.1 = (bf16[128,4096]{1,0:T(8,128)(2,1)}, bf16[128,4352]{1,0:T(8,128)(2,1)}) custom-call(s32[2]{0:T(128)S(1)} %pad_add_fusion.place, bf16[128,8192]{1,0:T(8,128)(2,1)} %hidden.1, bf16[8192]{0:T(1024)(128)(2,1)} %gain.1, bf16[128,256]{1,0:T(8,128)(2,1)} %cot.3), custom_call_target="tpu_custom_call" | custom-call | flops 8388608 | bytes 4194304 | tf_op jit(solution)/shard_map/split_norm/pallas_call | solution.py:64
  5.7 16.1 %collective-permute-start = (bf16[128,4352]{1,0:T(8,128)(2,1)}, bf16[128,4352]{1,0:T(8,128)(2,1)S(1)}, u32[]{:S(2)}, u32[]{:S(2)}) collective-permute-start(bf16[128,4352]{1,0:T(8,128)(2,1)} %get-tuple-element.22), channel_id=1, source_target_pairs={{0,2},{2,0},{1,3},{3,1},{4,6},{6,4},{5,7},{7,5},{8,10},{10,8},{9,1... | collective-permute-start | bytes 3342344 | tf_op jit(solution)/shard_map/ppermute | solution.py:204
  22.4 0.9 dynamic-slice_bitcast_fusion
  23.4 1.9 %collective-permute-start.2 = (f32[128,256]{1,0:T(8,128)S(1)}, f32[128,256]{1,0:T(8,128)S(1)}, u32[]{:S(2)}, u32[]{:S(2)}) collective-permute-start(f32[128,256]{1,0:T(8,128)S(1)} %dynamic-slice_bitcast_fusion), channel_id=1, source_target_pairs={{0,512},{128,640},{256,768},{384,896},{512,0},{640,128},{768,256},... | collective-permute-start | bytes 393224 | tf_op jit(solution)/shard_map/ppermute | solution.py:202
  25.3 0.0 collective-permute-done.recv.other_cot
  25.3 4.1 %chip_partial.1 = (f32[4,8,128,128]{3,2,1,0:T(8,128)S(1)}, f32[8,4,128,128]{3,2,1,0:T(8,128)S(1)}) custom-call(s32[2]{0:T(128)S(1)} %pad_add_fusion.place, bf16[128,4096]{1,0:T(8,128)(2,1)} %get-tuple-element.21.keep, bf16[128,4352]{1,0:T(8,128)(2,1)S(1)} %collective-permute-done.recv.other_cot, bf16[128,256]{1,0:T(8,128)(2,1)} %cot.3, ...), custom_call_target="tpu_custom_call" | custom-call | flops 536870912 | bytes 6291456 | tf_op jit(solution)/shard_map/chip_partial/pallas_call | solution.py:111
  29.4 1.2 convert_element_type.55
  30.6 6.5 %collective-permute-done.2 = f32[128,256]{1,0:T(8,128)S(1)} collective-permute-done((f32[128,256]{1,0:T(8,128)S(1)}, f32[128,256]{1,0:T(8,128)S(1)}, u32[]{:S(2)}, u32[]{:S(2)}) %collective-permute-start.2) | collective-permute-done | bytes 131104 | tf_op jit(solution)/shard_map/ppermute | solution.py:202
  37.0 3.6 %all-to-all-start = ((f16[8,4,128,128]{3,2,1,0:T(8,128)(2,1)}), f16[8,4,128,128]{3,2,1,0:T(8,128)(2,1)S(1)}, u32[]{:S(2)}, u32[]{:S(2)}) async-start(f16[8,4,128,128]{3,2,1,0:T(8,128)(2,1)} %convert_element_type.55), calls=%async_computation | async-start | bytes 2097152 | tf_op jit(solution)/shard_map/all_to_all | solution.py:209
  40.6 0.2 convert.10
  40.8 0.2 slice_bitcast_fusion.2
  41.0 1.9 %collective-permute-start.1 = (f16[8,128,128]{2,1,0:T(8,128)(2,1)S(1)}, f16[8,128,128]{2,1,0:T(8,128)(2,1)S(1)}, u32[]{:S(2)}, u32[]{:S(2)}) collective-permute-start(f16[8,128,128]{2,1,0:T(8,128)(2,1)S(1)} %get-tuple-element.39), channel_id=1, source_target_pairs={{0,32},{32,0},{64,96},{96,64},{1,33},{33,1},{65,97},{97,65},{2,34}... | collective-permute-start | bytes 786440 | tf_op jit(solution)/shard_map/ppermute | solution.py:191
  42.9 2.2 %collective-permute-start.3 = (f16[8,128,128]{2,1,0:T(8,128)(2,1)S(1)}, f16[8,128,128]{2,1,0:T(8,128)(2,1)S(1)}, u32[]{:S(2)}, u32[]{:S(2)}) collective-permute-start(f16[8,128,128]{2,1,0:T(8,128)(2,1)S(1)} %get-tuple-element.41), channel_id=1, source_target_pairs={{0,64},{32,96},{64,0},{96,32},{1,65},{33,97},{65,1},{97,33},{2,66}... | collective-permute-start | bytes 786440 | tf_op jit(solution)/shard_map/ppermute | solution.py:191
  45.2 5.1 %collective-permute-start.4 = (f16[8,128,128]{2,1,0:T(8,128)(2,1)S(1)}, f16[8,128,128]{2,1,0:T(8,128)(2,1)S(1)}, u32[]{:S(2)}, u32[]{:S(2)}) collective-permute-start(f16[8,128,128]{2,1,0:T(8,128)(2,1)S(1)} %get-tuple-element.40), channel_id=1, source_target_pairs={{0,96},{32,64},{64,32},{96,0},{1,97},{33,65},{65,33},{97,1},{2,98}... | collective-permute-start | bytes 786440 | tf_op jit(solution)/shard_map/ppermute | solution.py:191
  50.3 0.9 fusion.7
  51.2 0.4 collective-permute-done.1
  51.6 2.4 %collective-permute-start.5 = (f32[128,256]{1,0:T(8,128)S(1)}, f32[128,256]{1,0:T(8,128)S(1)}, u32[]{:S(2)}, u32[]{:S(2)}) collective-permute-start(f32[128,256]{1,0:T(8,128)S(1)} %fusion.7), channel_id=1, source_target_pairs={{0,128},{128,0},{256,384},{384,256},{512,640},{640,512},{768,896},... | collective-permute-start | bytes 393224 | tf_op jit(solution)/shard_map/ppermute | solution.py:195
  54.0 3.6 %collective-permute-done.5 = f32[128,256]{1,0:T(8,128)S(1)} collective-permute-done((f32[128,256]{1,0:T(8,128)S(1)}, f32[128,256]{1,0:T(8,128)S(1)}, u32[]{:S(2)}, u32[]{:S(2)}) %collective-permute-start.5) | collective-permute-done | bytes 131104 | tf_op jit(solution)/shard_map/ppermute | solution.py:195
  57.6 5.3 %collective-permute-start.6 = (f32[128,256]{1,0:T(8,128)S(1)}, f32[128,256]{1,0:T(8,128)S(1)}, u32[]{:S(2)}, u32[]{:S(2)}) collective-permute-start(f32[128,256]{1,0:T(8,128)S(1)} %add.44), channel_id=1, source_target_pairs={{0,256},{128,384},{256,0},{384,128},{512,768},{640,896},{768,512},... | collective-permute-start | bytes 393224 | tf_op jit(solution)/shard_map/ppermute | solution.py:195
  62.9 1.2 %collective-permute-done.3 = f16[8,128,128]{2,1,0:T(8,128)(2,1)S(1)} collective-permute-done((f16[8,128,128]{2,1,0:T(8,128)(2,1)S(1)}, f16[8,128,128]{2,1,0:T(8,128)(2,1)S(1)}, u32[]{:S(2)}, u32[]{:S(2)}) %collective-permute-start.3) | collective-permute-done | bytes 262176 | tf_op jit(solution)/shard_map/ppermute | solution.py:191
  64.1 0.0 collective-permute-done.4
  64.1 0.9 fusion.3
  65.0 2.0 %collective-permute-done.6 = f32[128,256]{1,0:T(8,128)S(1)} collective-permute-done((f32[128,256]{1,0:T(8,128)S(1)}, f32[128,256]{1,0:T(8,128)S(1)}, u32[]{:S(2)}, u32[]{:S(2)}) %collective-permute-start.6) | collective-permute-done | bytes 131104 | tf_op jit(solution)/shard_map/ppermute | solution.py:195
  67.0 2.8 %all-to-all-done = f16[8,4,128,128]{3,2,1,0:T(8,128)(2,1)S(1)} async-done(((f16[8,4,128,128]{3,2,1,0:T(8,128)(2,1)}), f16[8,4,128,128]{3,2,1,0:T(8,128)(2,1)S(1)}, u32[]{:S(2)}, u32[]{:S(2)}) %all-to-all-start) | async-done | bytes 1048608 | tf_op jit(solution)/shard_map/all_to_all | solution.py:209
  69.7 0.2 multiply_reduce_fusion
  70.0 3.4 %all-to-all-start.1 = ((f16[8,128,128]{2,1,0:T(8,128)(2,1)}), f16[8,128,128]{2,1,0:T(8,128)(2,1)S(1)}, u32[]{:S(2)}, u32[]{:S(2)}) async-start(f16[8,128,128]{2,1,0:T(8,128)(2,1)} %fusion.3), calls=%async_computation.1 | async-start | bytes 524288 | tf_op jit(solution)/shard_map/all_to_all | solution.py:221
  73.5 6.0 %collective-permute-start.7 = (f16[128,128]{1,0:T(8,128)(2,1)S(1)}, f16[128,128]{1,0:T(8,128)(2,1)S(1)}, u32[]{:S(2)}, u32[]{:S(2)}) collective-permute-start(f16[128,128]{1,0:T(8,128)(2,1)S(1)} %get-tuple-element.42), channel_id=1, source_target_pairs={{0,32},{32,0},{64,96},{96,64},{1,33},{33,1},{65,97},{97,65},{2,34}... | collective-permute-start | bytes 98312 | tf_op jit(solution)/shard_map/ppermute | solution.py:191
  79.5 1.9 %collective-permute-start.8 = (f16[128,128]{1,0:T(8,128)(2,1)S(1)}, f16[128,128]{1,0:T(8,128)(2,1)S(1)}, u32[]{:S(2)}, u32[]{:S(2)}) collective-permute-start(f16[128,128]{1,0:T(8,128)(2,1)S(1)} %get-tuple-element.44), channel_id=1, source_target_pairs={{0,64},{32,96},{64,0},{96,32},{1,65},{33,97},{65,1},{97,33},{2,66}... | collective-permute-start | bytes 98312 | tf_op jit(solution)/shard_map/ppermute | solution.py:191
  81.4 4.0 %collective-permute-start.9 = (f16[128,128]{1,0:T(8,128)(2,1)S(1)}, f16[128,128]{1,0:T(8,128)(2,1)S(1)}, u32[]{:S(2)}, u32[]{:S(2)}) collective-permute-start(f16[128,128]{1,0:T(8,128)(2,1)S(1)} %get-tuple-element.43), channel_id=1, source_target_pairs={{0,96},{32,64},{64,32},{96,0},{1,97},{33,65},{65,33},{97,1},{2,98}... | collective-permute-start | bytes 98312 | tf_op jit(solution)/shard_map/ppermute | solution.py:191
  85.4 0.0 collective-permute-done.7
  85.5 0.1 collective-permute-done.8
  85.5 2.4 %collective-permute-done.9 = f16[128,128]{1,0:T(8,128)(2,1)S(1)} collective-permute-done((f16[128,128]{1,0:T(8,128)(2,1)S(1)}, f16[128,128]{1,0:T(8,128)(2,1)S(1)}, u32[]{:S(2)}, u32[]{:S(2)}) %collective-permute-start.9) | collective-permute-done | bytes 32800 | tf_op jit(solution)/shard_map/ppermute | solution.py:191
  87.9 0.6 fusion.6.bottom
  88.5 0.0 all-to-all-done.1
  88.5 0.7 convert_reduce_fusion.top
  89.2 1.7 %turn_and_square.1 = (f32[128,256]{1,0:T(8,128)}, f32[128,1,128]{2,1,0:T(1,128)}) custom-call(f32[128,128]{1,0:T(8,128)} %convert_reduce_fusion.top, f32[128,128]{1,0:T(8,128)} %fusion.6.bottom), custom_call_target="tpu_custom_call" | custom-call | flops 131072 | bytes 262144 | tf_op jit(solution)/shard_map/turn_and_square/pallas_call | solution.py:144
  91.0 15.0 %all-to-all-start.2 = ((f32[128,1,128]{2,1,0:T(1,128)}), f32[128,1,128]{2,1,0:T(1,128)S(1)}, u32[]{:S(2)}, u32[]{:S(2)}) async-start(f32[128,1,128]{2,1,0:T(1,128)} %get-tuple-element.31), calls=%async_computation.2 | async-start | bytes 131072 | tf_op jit(solution)/shard_map/all_to_all | solution.py:245
  106.0 1.7 %bitcast_subtract_fusion = (f32[128,256]{1,0:T(8,128)}, f32[128,256]{1,0:T(8,128)}) fusion(f32[8,128,256]{2,1,0:T(8,128)} %param.17, s32[]{:T(128)S(6)} %select_n.6, f32[128,256]{1,0:T(8,128)S(1)} %add.45, f32[8,128,256]{2,1,0:T(8,128)} %param.18), kind=kLoop, calls=%fused_computation.11 | loop fusion | flops 262144 | bytes 655364 | tf_op jit(solution)/shard_map/sub | solution.py:38
  107.7 9.6 %all-to-all-done.2.rows = f32[128,1,128]{2,1,0:T(1,128)S(1)} async-done(((f32[128,1,128]{2,1,0:T(1,128)}), f32[128,1,128]{2,1,0:T(1,128)S(1)}, u32[]{:S(2)}, u32[]{:S(2)}) %all-to-all-start.2) | async-done | bytes 65568 | tf_op jit(solution)/shard_map/all_to_all | solution.py:245
  117.3 0.0 copy-start
  117.3 0.6 copy-done
  117.9 2.2 %inner_update.1 = (f32[1,128,256]{2,1,0:T(8,128)}, f32[1,128,256]{2,1,0:T(8,128)}, f32[1,128,256]{2,1,0:T(8,128)}) custom-call(f32[128,1,128]{2,1,0:T(1,128)} %copy-done, f32[128,256]{1,0:T(8,128)} %get-tuple-element.32.gradient, f32[1,128,256]{2,1,0:T(8,128)} %params.1, f32[1,128,256]{2,1,0:T(8,128)} %first.1, f32[1,128,256]{2,1,0:T(8,128)} %second.1), custom_call_target="tpu_custom_call" | custom-call | flops 524288 | bytes 1048576 | tf_op jit(solution)/shard_map/inner_update/pallas_call | solution.py:178
  (4 shorter events, 0.1 us)
Async XLA Ops:
  5.7 19.6 %collective-permute-start = (bf16[128,4352]{1,0:T(8,128)(2,1)}, bf16[128,4352]{1,0:T(8,128)(2,1)S(1)}, u32[]{:S(2)}, u32[]{:S(2)}) collective-permute-start(bf16[128,4352]{1,0:T(8,128)(2,1)} %get-tuple-element.22), channel_id=1, source_target_pairs={{0,2},{2,0},{1,3},{3,1},{4,6},{6,4},{5,7},{7,5},{8,10},{10,8},{9,1... | collective-permute-start | bytes 3342344 | tf_op jit(solution)/shard_map/ppermute | solution.py:204
  23.4 13.7 %collective-permute-start.2 = (f32[128,256]{1,0:T(8,128)S(1)}, f32[128,256]{1,0:T(8,128)S(1)}, u32[]{:S(2)}, u32[]{:S(2)}) collective-permute-start(f32[128,256]{1,0:T(8,128)S(1)} %dynamic-slice_bitcast_fusion), channel_id=1, source_target_pairs={{0,512},{128,640},{256,768},{384,896},{512,0},{640,128},{768,256},... | collective-permute-start | bytes 393224 | tf_op jit(solution)/shard_map/ppermute | solution.py:202
  37.0 32.7 %all-to-all-start = ((f16[8,4,128,128]{3,2,1,0:T(8,128)(2,1)}), f16[8,4,128,128]{3,2,1,0:T(8,128)(2,1)S(1)}, u32[]{:S(2)}, u32[]{:S(2)}) async-start(f16[8,4,128,128]{3,2,1,0:T(8,128)(2,1)} %convert_element_type.55), calls=%async_computation | async-start | bytes 2097152 | tf_op jit(solution)/shard_map/all_to_all | solution.py:209
  41.0 10.6 %collective-permute-start.1 = (f16[8,128,128]{2,1,0:T(8,128)(2,1)S(1)}, f16[8,128,128]{2,1,0:T(8,128)(2,1)S(1)}, u32[]{:S(2)}, u32[]{:S(2)}) collective-permute-start(f16[8,128,128]{2,1,0:T(8,128)(2,1)S(1)} %get-tuple-element.39), channel_id=1, source_target_pairs={{0,32},{32,0},{64,96},{96,64},{1,33},{33,1},{65,97},{97,65},{2,34}... | collective-permute-start | bytes 786440 | tf_op jit(solution)/shard_map/ppermute | solution.py:191
  42.9 21.2 %collective-permute-start.3 = (f16[8,128,128]{2,1,0:T(8,128)(2,1)S(1)}, f16[8,128,128]{2,1,0:T(8,128)(2,1)S(1)}, u32[]{:S(2)}, u32[]{:S(2)}) collective-permute-start(f16[8,128,128]{2,1,0:T(8,128)(2,1)S(1)} %get-tuple-element.41), channel_id=1, source_target_pairs={{0,64},{32,96},{64,0},{96,32},{1,65},{33,97},{65,1},{97,33},{2,66}... | collective-permute-start | bytes 786440 | tf_op jit(solution)/shard_map/ppermute | solution.py:191
  45.2 18.9 %collective-permute-start.4 = (f16[8,128,128]{2,1,0:T(8,128)(2,1)S(1)}, f16[8,128,128]{2,1,0:T(8,128)(2,1)S(1)}, u32[]{:S(2)}, u32[]{:S(2)}) collective-permute-start(f16[8,128,128]{2,1,0:T(8,128)(2,1)S(1)} %get-tuple-element.40), channel_id=1, source_target_pairs={{0,96},{32,64},{64,32},{96,0},{1,97},{33,65},{65,33},{97,1},{2,98}... | collective-permute-start | bytes 786440 | tf_op jit(solution)/shard_map/ppermute | solution.py:191
  51.6 6.0 %collective-permute-start.5 = (f32[128,256]{1,0:T(8,128)S(1)}, f32[128,256]{1,0:T(8,128)S(1)}, u32[]{:S(2)}, u32[]{:S(2)}) collective-permute-start(f32[128,256]{1,0:T(8,128)S(1)} %fusion.7), channel_id=1, source_target_pairs={{0,128},{128,0},{256,384},{384,256},{512,640},{640,512},{768,896},... | collective-permute-start | bytes 393224 | tf_op jit(solution)/shard_map/ppermute | solution.py:195
  57.6 9.3 %collective-permute-start.6 = (f32[128,256]{1,0:T(8,128)S(1)}, f32[128,256]{1,0:T(8,128)S(1)}, u32[]{:S(2)}, u32[]{:S(2)}) collective-permute-start(f32[128,256]{1,0:T(8,128)S(1)} %add.44), channel_id=1, source_target_pairs={{0,256},{128,384},{256,0},{384,128},{512,768},{640,896},{768,512},... | collective-permute-start | bytes 393224 | tf_op jit(solution)/shard_map/ppermute | solution.py:195
  70.0 18.6 %all-to-all-start.1 = ((f16[8,128,128]{2,1,0:T(8,128)(2,1)}), f16[8,128,128]{2,1,0:T(8,128)(2,1)S(1)}, u32[]{:S(2)}, u32[]{:S(2)}) async-start(f16[8,128,128]{2,1,0:T(8,128)(2,1)} %fusion.3), calls=%async_computation.1 | async-start | bytes 524288 | tf_op jit(solution)/shard_map/all_to_all | solution.py:221
  73.5 12.0 %collective-permute-start.7 = (f16[128,128]{1,0:T(8,128)(2,1)S(1)}, f16[128,128]{1,0:T(8,128)(2,1)S(1)}, u32[]{:S(2)}, u32[]{:S(2)}) collective-permute-start(f16[128,128]{1,0:T(8,128)(2,1)S(1)} %get-tuple-element.42), channel_id=1, source_target_pairs={{0,32},{32,0},{64,96},{96,64},{1,33},{33,1},{65,97},{97,65},{2,34}... | collective-permute-start | bytes 98312 | tf_op jit(solution)/shard_map/ppermute | solution.py:191
  79.5 6.0 %collective-permute-start.8 = (f16[128,128]{1,0:T(8,128)(2,1)S(1)}, f16[128,128]{1,0:T(8,128)(2,1)S(1)}, u32[]{:S(2)}, u32[]{:S(2)}) collective-permute-start(f16[128,128]{1,0:T(8,128)(2,1)S(1)} %get-tuple-element.44), channel_id=1, source_target_pairs={{0,64},{32,96},{64,0},{96,32},{1,65},{33,97},{65,1},{97,33},{2,66}... | collective-permute-start | bytes 98312 | tf_op jit(solution)/shard_map/ppermute | solution.py:191
  81.4 6.5 %collective-permute-start.9 = (f16[128,128]{1,0:T(8,128)(2,1)S(1)}, f16[128,128]{1,0:T(8,128)(2,1)S(1)}, u32[]{:S(2)}, u32[]{:S(2)}) collective-permute-start(f16[128,128]{1,0:T(8,128)(2,1)S(1)} %get-tuple-element.43), channel_id=1, source_target_pairs={{0,96},{32,64},{64,32},{96,0},{1,97},{33,65},{65,33},{97,1},{2,98}... | collective-permute-start | bytes 98312 | tf_op jit(solution)/shard_map/ppermute | solution.py:191
  91.0 26.4 %all-to-all-start.2 = ((f32[128,1,128]{2,1,0:T(1,128)}), f32[128,1,128]{2,1,0:T(1,128)S(1)}, u32[]{:S(2)}, u32[]{:S(2)}) async-start(f32[128,1,128]{2,1,0:T(1,128)} %get-tuple-element.31), calls=%async_computation.2 | async-start | bytes 131072 | tf_op jit(solution)/shard_map/all_to_all | solution.py:245
  117.3 0.6 copy-start

commit v4 on v3

--- a/solution.py
+++ b/solution.py
@@ -25,10 +25,11 @@
 HALF = XL * YN * FEAT
 WIDE = HALF * CORES
 HC = COLS // 2
-NORM_ROWS = 32
+NORM_ROWS = 16
+STEP_ROWS = 4
 CHIP_SCALE = 2.0**-8
 X_SCALE = 2.0**-10
-Y_SCALE = 2.0**-11
+Y_SCALE = 2.0**-12
 VMEM_BYTES = 24 * 2**20
 
 
@@ -86,7 +87,7 @@
 
 
 def partial_kernel(place, keep, recv, cot, other_cot, x_out, y_out, turned):
-    @pl.when(pl.program_id(0) == 0)
+    @pl.when((pl.program_id(0) == 0) & (pl.program_id(1) == 0))
     def _():
         turned[:, :TOK] = cot[...].T
         turned[:, TOK:] = other_cot[...].T
@@ -98,31 +99,37 @@
         turned[:, TOK:], recv[...], contract, preferred_element_type=jnp.float32
     )
     product = product * CHIP_SCALE
-    for row in range(YN):
+    for row in range(STEP_ROWS):
         block = product[:, row * FEAT : (row + 1) * FEAT]
         x_out[0, row] = block[:HC]
-        y_out[row, 0] = block[HC:]
+        y_out[0, row, 0] = block[HC:]
 
 
 def chip_partial(place, keep, recv, cot):
-    chunk = pl.BlockSpec((TOK, YN * FEAT), lambda k, place: (0, place[0] ^ k))
-    mine = pl.BlockSpec((TOK, COLS), lambda k, place: (0, 0))
-    other = pl.BlockSpec((TOK, COLS), lambda k, place: (0, HALF // COLS))
+    steps = YN // STEP_ROWS
+    chunk = pl.BlockSpec(
+        (TOK, STEP_ROWS * FEAT), lambda k, h, place: (0, (place[0] ^ k) * steps + h)
+    )
+    mine = pl.BlockSpec((TOK, COLS), lambda k, h, place: (0, 0))
+    other = pl.BlockSpec((TOK, COLS), lambda k, h, place: (0, HALF // COLS))
     return pl.pallas_call(
         partial_kernel,
         grid_spec=pltpu.PrefetchScalarGridSpec(
             num_scalar_prefetch=1,
-            grid=(XL,),
+            grid=(XL, steps),
             in_specs=[chunk, chunk, mine, other],
             out_specs=[
-                pl.BlockSpec((1, YN, HC, FEAT), lambda k, place: (k, 0, 0, 0)),
-                pl.BlockSpec((YN, 1, HC, FEAT), lambda k, place: (0, k, 0, 0)),
+                pl.BlockSpec((1, STEP_ROWS, HC, FEAT), lambda k, h, place: (k, h, 0, 0)),
+                pl.BlockSpec(
+                    (1, STEP_ROWS, 1, HC, FEAT),
+                    lambda k, h, place: ((place[0] ^ k) & 1, h, k // 2, 0, 0),
+                ),
             ],
             scratch_shapes=[pltpu.VMEM((COLS, CORES * TOK), jnp.bfloat16)],
         ),
         out_shape=[
             jax.ShapeDtypeStruct((XL, YN, HC, FEAT), jnp.float32),
-            jax.ShapeDtypeStruct((YN, XL, HC, FEAT), jnp.float32),
+            jax.ShapeDtypeStruct((XL // 2, YN, 2, HC, FEAT), jnp.float32),
         ],
         cost_estimate=pl.CostEstimate(
             flops=4 * TOK * HALF * COLS, bytes_accessed=6 * 2**20, transcendentals=0
@@ -188,7 +195,7 @@
 
 
 def swap_x(block, k):
-    return lax.ppermute(block, "xl", [(i, i ^ k) for i in range(XL)])
+    return lax.ppermute(block, ("xp", "xb"), [(i, i ^ k) for i in range(XL)])
 
 
 def add_replica(value, step):
@@ -196,7 +203,7 @@
 
 
 def worker_gradient(hidden_in, norm_gain, key_cotangent, local_layer):
-    place = jnp.stack([lax.axis_index("xl"), lax.axis_index("c")]).astype(jnp.int32)
+    place = jnp.stack([lax.axis_index(("xp", "xb")), lax.axis_index("c")]).astype(jnp.int32)
     in_hbm = functools.partial(pltpu.with_memory_space_constraint, memory_space=pltpu.HBM)
     hidden_in, norm_gain, key_cotangent = map(in_hbm, (hidden_in, norm_gain, key_cotangent))
     far_layer = lax.ppermute(local_layer, "z", [(i, i ^ 4) for i in range(8)])
@@ -204,9 +211,9 @@
     recv = lax.ppermute(send, "c", [(0, 1), (1, 0)])
     x_wide, y_wide = chip_partial(place, in_hbm(keep), recv, key_cotangent)
 
-    y_half = y_wide.astype(jnp.float16)
+    y_half = y_wide.astype(jnp.float16).reshape(YN * XL // 2, 2, HC, FEAT)
     y_half, far_layer = lax.optimization_barrier((y_half, far_layer))
-    y_parts = lax.all_to_all(y_half, "y", 0, 0, tiled=True)
+    y_parts = lax.all_to_all(y_half, ("xb", "y"), 0, 0, tiled=True)
     x_near = swap_x(x_wide[1].astype(jnp.float16), 1)
     local_layer = local_layer + far_layer
     x_near, local_layer = lax.optimization_barrier((x_near, local_layer))
@@ -219,9 +226,7 @@
     y_sum = jnp.sum(y_parts.astype(jnp.float32) * (Y_SCALE / CHIP_SCALE), axis=0)
 
     top = lax.all_to_all(x_sum, "y", 0, 0, tiled=True)
-    bottom = y_sum[0]
-    for k in range(1, XL):
-        bottom = bottom + swap_x(y_sum[k].astype(jnp.float16), k).astype(jnp.float32)
+    bottom = y_sum[0] + swap_x(y_sum[1].astype(jnp.float16), 2).astype(jnp.float32)
     top = jnp.sum(top.astype(jnp.float32), axis=0)
     return top, bottom, summed
 
@@ -242,7 +247,7 @@
     local_layer = lax.dynamic_index_in_dim(frag_local[0], layer_index, 0, keepdims=False)
     top, bottom, summed = worker_gradient(hidden_in, norm_gain, key_cotangent, local_layer)
     gradient, rows = turn_and_square(top, bottom)
-    rows = lax.all_to_all(rows, ("xl", "y", "c", "xh"), 0, 0, tiled=True)
+    rows = lax.all_to_all(rows, ("xp", "xb", "y", "c", "xh"), 0, 0, tiled=True)
     new_params, new_first, new_second = inner_update(
         rows, gradient, inner_params, inner_first, inner_second
     )
@@ -256,9 +261,9 @@
 
 def solution(mesh):
     workers = mesh.shape["replica"]
-    devices = mesh.devices.reshape(workers, XL, YN, CORES, XH)
-    split = Mesh(devices, ("z", "xl", "y", "c", "xh"))
-    fsdp = ("xl", "y", "c")
+    devices = mesh.devices.reshape(workers, XL // 2, 2, YN, CORES, XH)
+    split = Mesh(devices, ("z", "xp", "xb", "y", "c", "xh"))
+    fsdp = ("xp", "xb", "y", "c")
     return jax.shard_map(
         on_device,
         mesh=split,

time: 121 us -> 131 us (1.083)
  waiting for transfers between devices: 28.4 us -> 40.6 us
  starting transfers between devices: 68.9 us -> 62.7 us
  Pallas kernels: 13 us -> 17.1 us
    ppermute x6 -> x4, waiting for transfers between devices: 4.01 us -> 17.5 us  [swap_x(): return lax.ppermute(block, ('xp', 'xb'), [(i, i ^ k) for i in range(XL)])]
    ppermute x6 -> x4, starting transfers between devices: 21.2 us -> 11.7 us  [swap_x(): return lax.ppermute(block, ('xp', 'xb'), [(i, i ^ k) for i in range(XL)])]
    all_to_all x1, waiting for transfers between devices: 0.01 us -> 3.23 us  [worker_gradient(): top = lax.all_to_all(x_sum, 'y', 0, 0, tiled=True)]
    all_to_all x2, waiting for transfers between devices: 12.4 us -> 9.64 us  [the longest x1 9.64 us: on_device(): rows = lax.all_to_all(rows, ('xp', 'xb', 'y', 'c', 'xh'), 0, 0, tiled=True)]
    ppermute x2, starting transfers between devices: 7.7 us -> 9.95 us  [add_replica(): return value + lax.ppermute(value, 'z', [(i, i ^ step) for i in range(8)])]
    pallas_call x1, Pallas kernels: 4.06 us -> 6.17 us  [chip_partial(): pl.pallas_call(partial_kernel, grid_spec=pltpu.PrefetchScalarGridSpec(num...]
    ppermute x1, waiting for transfers between devices: 6.45 us -> 4.35 us  [worker_gradient(): far_layer = lax.ppermute(local_layer, 'z', [(i, i ^ 4) for i in range(8)])]
    all_to_all x1, starting transfers between devices: 3.42 us -> 5.52 us  [worker_gradient(): top = lax.all_to_all(x_sum, 'y', 0, 0, tiled=True)]
  transfers between devices with their start and end apart: 13 -> 11, of which waited for: 9 -> 7; matrix products, arithmetic and copies ran while one was open for 6% -> 5% of each run, Pallas kernels for 3% -> 5%
where the time goes in v4:
time: 131 us; the launch traced here: 130 us
  starting transfers between devices  62.7 us (48%)
  waiting for transfers between devices  40.6 us (31%)
  Pallas kernels  17.1 us (13%)
  other arithmetic  6.56 us (5%)
  local copies, waits for them, and re-layouts  1.74 us (1%)
  between operations  1.45 us (1%)
    ppermute x4, waiting for transfers between devices, swap_x(): return lax.ppermute(block, ('xp', 'xb'), [(i, i ^ k) for i in range(XL)])  17.5 us
    ppermute x1, starting transfers between devices, worker_gradient(): recv = lax.ppermute(send, 'c', [(0, 1), (1, 0)])  16.1 us
    all_to_all x1, starting transfers between devices, on_device(): rows = lax.all_to_all(rows, ('xp', 'xb', 'y', 'c', 'xh'), 0, 0, tiled=True)  13.9 us
    ppermute x4, starting transfers between devices, swap_x(): return lax.ppermute(block, ('xp', 'xb'), [(i, i ^ k) for i in range(XL)])  11.7 us
    ppermute x2, starting transfers between devices, add_replica(): return value + lax.ppermute(value, 'z', [(i, i ^ step) for i in range(8)])  9.95 us
    all_to_all x1, waiting for transfers between devices, on_device(): rows = lax.all_to_all(rows, ('xp', 'xb', 'y', 'c', 'xh'), 0, 0, tiled=True)  9.64 us
    pallas_call x1, Pallas kernels, split_norm(): pl.pallas_call(norm_kernel, grid_spec=pltpu.PrefetchScalarGridSpec(num_sc...  7.01 us
    pallas_call x1, Pallas kernels, chip_partial(): pl.pallas_call(partial_kernel, grid_spec=pltpu.PrefetchScalarGridSpec(num...  6.17 us
  transfers between devices with their start and end apart: 11, of which 7 were waited for; matrix products, arithmetic and copies ran while one was open for 5% of the time, Pallas kernels for 5%

profile of v4, /device:TPU:1, one launch (start us, length us, event | category | flops | bytes accessed | tf_op | source)
XLA Modules:
  0.0 130.1 jit_solution(8619057836996126958)
XLA Ops:
  0.6 0.1 pad_add_fusion.place
  0.7 7.0 %split_norm.1 = (bf16[128,4096]{1,0:T(8,128)(2,1)}, bf16[128,4352]{1,0:T(8,128)(2,1)}) custom-call(s32[2]{0:T(128)S(1)} %pad_add_fusion.place, bf16[128,8192]{1,0:T(8,128)(2,1)} %hidden.1, bf16[8192]{0:T(1024)(128)(2,1)} %gain.1, bf16[128,256]{1,0:T(8,128)(2,1)} %cot.3), custom_call_target="tpu_custom_call" | custom-call | flops 8388608 | bytes 4194304 | tf_op jit(solution)/shard_map/split_norm/pallas_call | solution.py:65
  7.7 16.1 %collective-permute-start = (bf16[128,4352]{1,0:T(8,128)(2,1)}, bf16[128,4352]{1,0:T(8,128)(2,1)S(1)}, u32[]{:S(2)}, u32[]{:S(2)}) collective-permute-start(bf16[128,4352]{1,0:T(8,128)(2,1)} %get-tuple-element.22), channel_id=1, source_target_pairs={{0,2},{2,0},{1,3},{3,1},{4,6},{6,4},{5,7},{7,5},{8,10},{10,8},{9,1... | collective-permute-start | bytes 3342344 | tf_op jit(solution)/shard_map/ppermute | solution.py:211
  24.4 0.9 dynamic-slice_bitcast_fusion
  25.4 1.9 %collective-permute-start.2 = (f32[128,256]{1,0:T(8,128)S(1)}, f32[128,256]{1,0:T(8,128)S(1)}, u32[]{:S(2)}, u32[]{:S(2)}) collective-permute-start(f32[128,256]{1,0:T(8,128)S(1)} %dynamic-slice_bitcast_fusion), channel_id=1, source_target_pairs={{0,512},{128,640},{256,768},{384,896},{512,0},{640,128},{768,256},... | collective-permute-start | bytes 393224 | tf_op jit(solution)/shard_map/ppermute | solution.py:209
  27.3 0.0 collective-permute-done.recv.other_cot
  27.3 6.2 %chip_partial.1 = (f32[4,8,128,128]{3,2,1,0:T(8,128)S(1)}, f32[2,8,2,128,128]{4,3,2,1,0:T(8,128)S(1)}) custom-call(s32[2]{0:T(128)S(1)} %pad_add_fusion.place, bf16[128,4096]{1,0:T(8,128)(2,1)} %get-tuple-element.21.keep, bf16[128,4352]{1,0:T(8,128)(2,1)S(1)} %collective-permute-done.recv.other_cot, bf16[128,256]{1,0:T(8,128)(2,1)} %cot.3, ...), custom_call_target="tpu_custom_call" | custom-call | flops 536870912 | bytes 6291456 | tf_op jit(solution)/shard_map/chip_partial/pallas_call | solution.py:115
  33.5 1.2 convert_element_type.41
  34.7 4.3 %collective-permute-done.2 = f32[128,256]{1,0:T(8,128)S(1)} collective-permute-done((f32[128,256]{1,0:T(8,128)S(1)}, f32[128,256]{1,0:T(8,128)S(1)}, u32[]{:S(2)}, u32[]{:S(2)}) %collective-permute-start.2) | collective-permute-done | bytes 131104 | tf_op jit(solution)/shard_map/ppermute | solution.py:209
  39.0 3.7 %all-to-all-start = ((f16[16,2,128,128]{3,2,1,0:T(8,128)(2,1)}), f16[16,2,128,128]{3,2,1,0:T(8,128)(2,1)S(1)}, u32[]{:S(2)}, u32[]{:S(2)}) async-start(f16[16,2,128,128]{3,2,1,0:T(8,128)(2,1)} %bitcast.6), calls=%async_computation | async-start | bytes 2097152 | tf_op jit(solution)/shard_map/all_to_all | solution.py:216
  42.7 0.2 convert.8
  42.9 0.2 slice_bitcast_fusion.2
  43.1 3.3 %collective-permute-start.1 = (f16[8,128,128]{2,1,0:T(8,128)(2,1)S(1)}, f16[8,128,128]{2,1,0:T(8,128)(2,1)S(1)}, u32[]{:S(2)}, u32[]{:S(2)}) collective-permute-start(f16[8,128,128]{2,1,0:T(8,128)(2,1)S(1)} %get-tuple-element.39), channel_id=1, source_target_pairs={{0,32},{32,0},{64,96},{96,64},{1,33},{33,1},{65,97},{97,65},{2,34}... | collective-permute-start | bytes 786440 | tf_op jit(solution)/shard_map/ppermute | solution.py:198
  46.4 4.0 %collective-permute-start.3 = (f16[8,128,128]{2,1,0:T(8,128)(2,1)S(1)}, f16[8,128,128]{2,1,0:T(8,128)(2,1)S(1)}, u32[]{:S(2)}, u32[]{:S(2)}) collective-permute-start(f16[8,128,128]{2,1,0:T(8,128)(2,1)S(1)} %get-tuple-element.41), channel_id=1, source_target_pairs={{0,64},{32,96},{64,0},{96,32},{1,65},{33,97},{65,1},{97,33},{2,66}... | collective-permute-start | bytes 786440 | tf_op jit(solution)/shard_map/ppermute | solution.py:198
  50.5 2.0 %collective-permute-start.4 = (f16[8,128,128]{2,1,0:T(8,128)(2,1)S(1)}, f16[8,128,128]{2,1,0:T(8,128)(2,1)S(1)}, u32[]{:S(2)}, u32[]{:S(2)}) collective-permute-start(f16[8,128,128]{2,1,0:T(8,128)(2,1)S(1)} %get-tuple-element.40), channel_id=1, source_target_pairs={{0,96},{32,64},{64,32},{96,0},{1,97},{33,65},{65,33},{97,1},{2,98}... | collective-permute-start | bytes 786440 | tf_op jit(solution)/shard_map/ppermute | solution.py:198
  52.4 0.9 fusion.6
  53.3 14.4 %collective-permute-done.1 = f16[8,128,128]{2,1,0:T(8,128)(2,1)S(1)} collective-permute-done((f16[8,128,128]{2,1,0:T(8,128)(2,1)S(1)}, f16[8,128,128]{2,1,0:T(8,128)(2,1)S(1)}, u32[]{:S(2)}, u32[]{:S(2)}) %collective-permute-start.1) | collective-permute-done | bytes 262176 | tf_op jit(solution)/shard_map/ppermute | solution.py:198
  67.7 4.1 %collective-permute-start.5 = (f32[128,256]{1,0:T(8,128)S(1)}, f32[128,256]{1,0:T(8,128)S(1)}, u32[]{:S(2)}, u32[]{:S(2)}) collective-permute-start(f32[128,256]{1,0:T(8,128)S(1)} %fusion.6), channel_id=1, source_target_pairs={{0,128},{128,0},{256,384},{384,256},{512,640},{640,512},{768,896},... | collective-permute-start | bytes 393224 | tf_op jit(solution)/shard_map/ppermute | solution.py:202
  71.8 2.6 %collective-permute-done.5 = f32[128,256]{1,0:T(8,128)S(1)} collective-permute-done((f32[128,256]{1,0:T(8,128)S(1)}, f32[128,256]{1,0:T(8,128)S(1)}, u32[]{:S(2)}, u32[]{:S(2)}) %collective-permute-start.5) | collective-permute-done | bytes 131104 | tf_op jit(solution)/shard_map/ppermute | solution.py:202
  74.5 5.8 %collective-permute-start.6 = (f32[128,256]{1,0:T(8,128)S(1)}, f32[128,256]{1,0:T(8,128)S(1)}, u32[]{:S(2)}, u32[]{:S(2)}) collective-permute-start(f32[128,256]{1,0:T(8,128)S(1)} %add.42), channel_id=1, source_target_pairs={{0,256},{128,384},{256,0},{384,128},{512,768},{640,896},{768,512},... | collective-permute-start | bytes 393224 | tf_op jit(solution)/shard_map/ppermute | solution.py:202
  80.3 0.0 collective-permute-done.3
  80.3 0.0 collective-permute-done.4
  80.4 0.9 fusion.3
  81.2 3.2 %collective-permute-done.6 = f32[128,256]{1,0:T(8,128)S(1)} collective-permute-done((f32[128,256]{1,0:T(8,128)S(1)}, f32[128,256]{1,0:T(8,128)S(1)}, u32[]{:S(2)}, u32[]{:S(2)}) %collective-permute-start.6) | collective-permute-done | bytes 131104 | tf_op jit(solution)/shard_map/ppermute | solution.py:202
  84.5 0.0 all-to-all-done
  84.5 0.2 multiply_reduce_fusion
  84.7 5.5 %all-to-all-start.1 = ((f16[8,128,128]{2,1,0:T(8,128)(2,1)}), f16[8,128,128]{2,1,0:T(8,128)(2,1)S(1)}, u32[]{:S(2)}, u32[]{:S(2)}) async-start(f16[8,128,128]{2,1,0:T(8,128)(2,1)} %fusion.3), calls=%async_computation.1 | async-start | bytes 524288 | tf_op jit(solution)/shard_map/all_to_all | solution.py:228
  90.2 2.4 %collective-permute-start.7 = (f16[128,128]{1,0:T(8,128)(2,1)S(1)}, f16[128,128]{1,0:T(8,128)(2,1)S(1)}, u32[]{:S(2)}, u32[]{:S(2)}) collective-permute-start(f16[128,128]{1,0:T(8,128)(2,1)S(1)} %fusion.5), channel_id=1, source_target_pairs={{0,64},{32,96},{64,0},{96,32},{1,65},{33,97},{65,1},{97,33},{2,66}... | collective-permute-start | bytes 98312 | tf_op jit(solution)/shard_map/ppermute | solution.py:198
  92.6 3.1 %collective-permute-done.7 = f16[128,128]{1,0:T(8,128)(2,1)S(1)} collective-permute-done((f16[128,128]{1,0:T(8,128)(2,1)S(1)}, f16[128,128]{1,0:T(8,128)(2,1)S(1)}, u32[]{:S(2)}, u32[]{:S(2)}) %collective-permute-start.7) | collective-permute-done | bytes 32800 | tf_op jit(solution)/shard_map/ppermute | solution.py:198
  95.8 0.6 fusion.4.bottom
  96.4 3.2 %all-to-all-done.1 = f16[8,128,128]{2,1,0:T(8,128)(2,1)S(1)} async-done(((f16[8,128,128]{2,1,0:T(8,128)(2,1)}), f16[8,128,128]{2,1,0:T(8,128)(2,1)S(1)}, u32[]{:S(2)}, u32[]{:S(2)}) %all-to-all-start.1) | async-done | bytes 262176 | tf_op jit(solution)/shard_map/all_to_all | solution.py:228
  99.6 0.7 convert_reduce_fusion.top
  100.3 1.7 %turn_and_square.1 = (f32[128,256]{1,0:T(8,128)}, f32[128,1,128]{2,1,0:T(1,128)}) custom-call(f32[128,128]{1,0:T(8,128)} %convert_reduce_fusion.top, f32[128,128]{1,0:T(8,128)} %fusion.4.bottom), custom_call_target="tpu_custom_call" | custom-call | flops 131072 | bytes 262144 | tf_op jit(solution)/shard_map/turn_and_square/pallas_call | solution.py:151
  102.0 13.9 %all-to-all-start.2 = ((f32[128,1,128]{2,1,0:T(1,128)}), f32[128,1,128]{2,1,0:T(1,128)S(1)}, u32[]{:S(2)}, u32[]{:S(2)}) async-start(f32[128,1,128]{2,1,0:T(1,128)} %get-tuple-element.31), calls=%async_computation.2 | async-start | bytes 131072 | tf_op jit(solution)/shard_map/all_to_all | solution.py:250
  115.9 1.7 %bitcast_subtract_fusion = (f32[128,256]{1,0:T(8,128)}, f32[128,256]{1,0:T(8,128)}) fusion(f32[8,128,256]{2,1,0:T(8,128)} %param.17, s32[]{:T(128)S(6)} %select_n.6, f32[128,256]{1,0:T(8,128)S(1)} %add.43, f32[8,128,256]{2,1,0:T(8,128)} %param.18), kind=kLoop, calls=%fused_computation.11 | loop fusion | flops 262144 | bytes 655364 | tf_op jit(solution)/shard_map/sub | solution.py:39
  117.6 9.6 %all-to-all-done.2.rows = f32[128,1,128]{2,1,0:T(1,128)S(1)} async-done(((f32[128,1,128]{2,1,0:T(1,128)}), f32[128,1,128]{2,1,0:T(1,128)S(1)}, u32[]{:S(2)}, u32[]{:S(2)}) %all-to-all-start.2) | async-done | bytes 65568 | tf_op jit(solution)/shard_map/all_to_all | solution.py:250
  127.3 0.0 copy-start
  127.3 0.6 copy-done
  127.9 2.2 %inner_update.1 = (f32[1,128,256]{2,1,0:T(8,128)}, f32[1,128,256]{2,1,0:T(8,128)}, f32[1,128,256]{2,1,0:T(8,128)}) custom-call(f32[128,1,128]{2,1,0:T(1,128)} %copy-done, f32[128,256]{1,0:T(8,128)} %get-tuple-element.32.gradient, f32[1,128,256]{2,1,0:T(8,128)} %params.1, f32[1,128,256]{2,1,0:T(8,128)} %first.1, f32[1,128,256]{2,1,0:T(8,128)} %second.1), custom_call_target="tpu_custom_call" | custom-call | flops 524288 | bytes 1048576 | tf_op jit(solution)/shard_map/inner_update/pallas_call | solution.py:185
  (3 shorter events, 0.0 us)
Async XLA Ops:
  7.7 19.6 %collective-permute-start = (bf16[128,4352]{1,0:T(8,128)(2,1)}, bf16[128,4352]{1,0:T(8,128)(2,1)S(1)}, u32[]{:S(2)}, u32[]{:S(2)}) collective-permute-start(bf16[128,4352]{1,0:T(8,128)(2,1)} %get-tuple-element.22), channel_id=1, source_target_pairs={{0,2},{2,0},{1,3},{3,1},{4,6},{6,4},{5,7},{7,5},{8,10},{10,8},{9,1... | collective-permute-start | bytes 3342344 | tf_op jit(solution)/shard_map/ppermute | solution.py:211
  25.4 13.7 %collective-permute-start.2 = (f32[128,256]{1,0:T(8,128)S(1)}, f32[128,256]{1,0:T(8,128)S(1)}, u32[]{:S(2)}, u32[]{:S(2)}) collective-permute-start(f32[128,256]{1,0:T(8,128)S(1)} %dynamic-slice_bitcast_fusion), channel_id=1, source_target_pairs={{0,512},{128,640},{256,768},{384,896},{512,0},{640,128},{768,256},... | collective-permute-start | bytes 393224 | tf_op jit(solution)/shard_map/ppermute | solution.py:209
  39.0 45.4 %all-to-all-start = ((f16[16,2,128,128]{3,2,1,0:T(8,128)(2,1)}), f16[16,2,128,128]{3,2,1,0:T(8,128)(2,1)S(1)}, u32[]{:S(2)}, u32[]{:S(2)}) async-start(f16[16,2,128,128]{3,2,1,0:T(8,128)(2,1)} %bitcast.6), calls=%async_computation | async-start | bytes 2097152 | tf_op jit(solution)/shard_map/all_to_all | solution.py:216
  43.1 24.6 %collective-permute-start.1 = (f16[8,128,128]{2,1,0:T(8,128)(2,1)S(1)}, f16[8,128,128]{2,1,0:T(8,128)(2,1)S(1)}, u32[]{:S(2)}, u32[]{:S(2)}) collective-permute-start(f16[8,128,128]{2,1,0:T(8,128)(2,1)S(1)} %get-tuple-element.39), channel_id=1, source_target_pairs={{0,32},{32,0},{64,96},{96,64},{1,33},{33,1},{65,97},{97,65},{2,34}... | collective-permute-start | bytes 786440 | tf_op jit(solution)/shard_map/ppermute | solution.py:198
  46.4 33.9 %collective-permute-start.3 = (f16[8,128,128]{2,1,0:T(8,128)(2,1)S(1)}, f16[8,128,128]{2,1,0:T(8,128)(2,1)S(1)}, u32[]{:S(2)}, u32[]{:S(2)}) collective-permute-start(f16[8,128,128]{2,1,0:T(8,128)(2,1)S(1)} %get-tuple-element.41), channel_id=1, source_target_pairs={{0,64},{32,96},{64,0},{96,32},{1,65},{33,97},{65,1},{97,33},{2,66}... | collective-permute-start | bytes 786440 | tf_op jit(solution)/shard_map/ppermute | solution.py:198
  50.5 29.9 %collective-permute-start.4 = (f16[8,128,128]{2,1,0:T(8,128)(2,1)S(1)}, f16[8,128,128]{2,1,0:T(8,128)(2,1)S(1)}, u32[]{:S(2)}, u32[]{:S(2)}) collective-permute-start(f16[8,128,128]{2,1,0:T(8,128)(2,1)S(1)} %get-tuple-element.40), channel_id=1, source_target_pairs={{0,96},{32,64},{64,32},{96,0},{1,97},{33,65},{65,33},{97,1},{2,98}... | collective-permute-start | bytes 786440 | tf_op jit(solution)/shard_map/ppermute | solution.py:198
  67.7 6.8 %collective-permute-start.5 = (f32[128,256]{1,0:T(8,128)S(1)}, f32[128,256]{1,0:T(8,128)S(1)}, u32[]{:S(2)}, u32[]{:S(2)}) collective-permute-start(f32[128,256]{1,0:T(8,128)S(1)} %fusion.6), channel_id=1, source_target_pairs={{0,128},{128,0},{256,384},{384,256},{512,640},{640,512},{768,896},... | collective-permute-start | bytes 393224 | tf_op jit(solution)/shard_map/ppermute | solution.py:202
  74.5 10.0 %collective-permute-start.6 = (f32[128,256]{1,0:T(8,128)S(1)}, f32[128,256]{1,0:T(8,128)S(1)}, u32[]{:S(2)}, u32[]{:S(2)}) collective-permute-start(f32[128,256]{1,0:T(8,128)S(1)} %add.42), channel_id=1, source_target_pairs={{0,256},{128,384},{256,0},{384,128},{512,768},{640,896},{768,512},... | collective-permute-start | bytes 393224 | tf_op jit(solution)/shard_map/ppermute | solution.py:202
  84.7 15.0 %all-to-all-start.1 = ((f16[8,128,128]{2,1,0:T(8,128)(2,1)}), f16[8,128,128]{2,1,0:T(8,128)(2,1)S(1)}, u32[]{:S(2)}, u32[]{:S(2)}) async-start(f16[8,128,128]{2,1,0:T(8,128)(2,1)} %fusion.3), calls=%async_computation.1 | async-start | bytes 524288 | tf_op jit(solution)/shard_map/all_to_all | solution.py:228
  90.2 5.6 %collective-permute-start.7 = (f16[128,128]{1,0:T(8,128)(2,1)S(1)}, f16[128,128]{1,0:T(8,128)(2,1)S(1)}, u32[]{:S(2)}, u32[]{:S(2)}) collective-permute-start(f16[128,128]{1,0:T(8,128)(2,1)S(1)} %fusion.5), channel_id=1, source_target_pairs={{0,64},{32,96},{64,0},{96,32},{1,65},{33,97},{65,1},{97,33},{2,66}... | collective-permute-start | bytes 98312 | tf_op jit(solution)/shard_map/ppermute | solution.py:198
  102.0 25.3 %all-to-all-start.2 = ((f32[128,1,128]{2,1,0:T(1,128)}), f32[128,1,128]{2,1,0:T(1,128)S(1)}, u32[]{:S(2)}, u32[]{:S(2)}) async-start(f32[128,1,128]{2,1,0:T(1,128)} %get-tuple-element.31), calls=%async_computation.2 | async-start | bytes 131072 | tf_op jit(solution)/shard_map/all_to_all | solution.py:250
  127.3 0.6 copy-start

commit v5 on v4

--- a/solution.py
+++ b/solution.py
@@ -25,8 +25,7 @@
 HALF = XL * YN * FEAT
 WIDE = HALF * CORES
 HC = COLS // 2
-NORM_ROWS = 16
-STEP_ROWS = 4
+NORM_ROWS = 64
 CHIP_SCALE = 2.0**-8
 X_SCALE = 2.0**-10
 Y_SCALE = 2.0**-12
@@ -87,43 +86,41 @@
 
 
 def partial_kernel(place, keep, recv, cot, other_cot, x_out, y_out, turned):
-    @pl.when((pl.program_id(0) == 0) & (pl.program_id(1) == 0))
+    @pl.when(pl.program_id(0) == 0)
     def _():
         turned[:, :TOK] = cot[...].T
         turned[:, TOK:] = other_cot[...].T
 
     contract = (((1,), (0,)), ((), ()))
-    product = lax.dot_general(
-        turned[:, :TOK], keep[...], contract, preferred_element_type=jnp.float32
-    ) + lax.dot_general(
-        turned[:, TOK:], recv[...], contract, preferred_element_type=jnp.float32
-    )
-    product = product * CHIP_SCALE
-    for row in range(STEP_ROWS):
-        block = product[:, row * FEAT : (row + 1) * FEAT]
-        x_out[0, row] = block[:HC]
-        y_out[0, row, 0] = block[HC:]
+    width = YN * FEAT
+    for near in range(2):
+        dest = (place[0] ^ near) & 1
+        chunk = pl.ds(pl.multiple_of(dest * width, width), width)
+        product = lax.dot_general(
+            turned[:, :TOK], keep[:, chunk], contract, preferred_element_type=jnp.float32
+        ) + lax.dot_general(
+            turned[:, TOK:], recv[:, chunk], contract, preferred_element_type=jnp.float32
+        )
+        product = product * CHIP_SCALE
+        for row in range(YN):
+            block = product[:, row * FEAT : (row + 1) * FEAT]
+            x_out[near, row] = block[:HC]
+            y_out[dest, row, 0] = block[HC:]
 
 
 def chip_partial(place, keep, recv, cot):
-    steps = YN // STEP_ROWS
-    chunk = pl.BlockSpec(
-        (TOK, STEP_ROWS * FEAT), lambda k, h, place: (0, (place[0] ^ k) * steps + h)
-    )
-    mine = pl.BlockSpec((TOK, COLS), lambda k, h, place: (0, 0))
-    other = pl.BlockSpec((TOK, COLS), lambda k, h, place: (0, HALF // COLS))
+    chunk = pl.BlockSpec((TOK, 2 * YN * FEAT), lambda far, place: (0, (place[0] // 2) ^ far))
+    mine = pl.BlockSpec((TOK, COLS), lambda far, place: (0, 0))
+    other = pl.BlockSpec((TOK, COLS), lambda far, place: (0, HALF // COLS))
     return pl.pallas_call(
         partial_kernel,
         grid_spec=pltpu.PrefetchScalarGridSpec(
             num_scalar_prefetch=1,
-            grid=(XL, steps),
+            grid=(XL // 2,),
             in_specs=[chunk, chunk, mine, other],
             out_specs=[
-                pl.BlockSpec((1, STEP_ROWS, HC, FEAT), lambda k, h, place: (k, h, 0, 0)),
-                pl.BlockSpec(
-                    (1, STEP_ROWS, 1, HC, FEAT),
-                    lambda k, h, place: ((place[0] ^ k) & 1, h, k // 2, 0, 0),
-                ),
+                pl.BlockSpec((2, YN, HC, FEAT), lambda far, place: (far, 0, 0, 0)),
+                pl.BlockSpec((2, YN, 1, HC, FEAT), lambda far, place: (0, 0, far, 0, 0)),
             ],
             scratch_shapes=[pltpu.VMEM((COLS, CORES * TOK), jnp.bfloat16)],
         ),
@@ -214,13 +211,11 @@
     y_half = y_wide.astype(jnp.float16).reshape(YN * XL // 2, 2, HC, FEAT)
     y_half, far_layer = lax.optimization_barrier((y_half, far_layer))
     y_parts = lax.all_to_all(y_half, ("xb", "y"), 0, 0, tiled=True)
-    x_near = swap_x(x_wide[1].astype(jnp.float16), 1)
     local_layer = local_layer + far_layer
-    x_near, local_layer = lax.optimization_barrier((x_near, local_layer))
-    x_sum = x_wide[0] + x_near.astype(jnp.float32)
-    for k in range(2, XL):
+    x_sum = x_wide[0]
+    for k in range(1, XL):
         x_sum = x_sum + swap_x(x_wide[k].astype(jnp.float16), k).astype(jnp.float32)
-    summed = add_replica(add_replica(local_layer, 1), 2)
+    summed = add_replica(local_layer, 1)
     x_sum = (x_sum * (X_SCALE / CHIP_SCALE)).astype(jnp.float16)
     x_sum, y_parts, summed = lax.optimization_barrier((x_sum, y_parts, summed))
     y_sum = jnp.sum(y_parts.astype(jnp.float32) * (Y_SCALE / CHIP_SCALE), axis=0)
@@ -228,7 +223,7 @@
     top = lax.all_to_all(x_sum, "y", 0, 0, tiled=True)
     bottom = y_sum[0] + swap_x(y_sum[1].astype(jnp.float16), 2).astype(jnp.float32)
     top = jnp.sum(top.astype(jnp.float32), axis=0)
-    return top, bottom, summed
+    return top, bottom, add_replica(summed, 2)
 
 
 def on_device(

time: 131 us -> 117 us (0.89)
  Pallas kernels: 17.1 us -> 11.3 us
  waiting for transfers between devices: 40.6 us -> 36.2 us
  starting transfers between devices: 62.7 us -> 59.3 us
    ppermute x4, waiting for transfers between devices: 17.5 us -> 13.7 us  [swap_x(): return lax.ppermute(block, ('xp', 'xb'), [(i, i ^ k) for i in range(XL)])]
    pallas_call x1, Pallas kernels: 7.01 us -> 4.07 us  [split_norm(): pl.pallas_call(norm_kernel, grid_spec=pltpu.PrefetchScalarGridSpec(num_sc...]
    pallas_call x1, Pallas kernels: 6.17 us -> 3.31 us  [chip_partial(): pl.pallas_call(partial_kernel, grid_spec=pltpu.PrefetchScalarGridSpec(num...]
    ppermute x1, waiting for transfers between devices: 4.35 us -> 7.2 us  [worker_gradient(): far_layer = lax.ppermute(local_layer, 'z', [(i, i ^ 4) for i in range(8)])]
    ppermute x2, starting transfers between devices: 9.95 us -> 7.26 us  [add_replica(): return value + lax.ppermute(value, 'z', [(i, i ^ step) for i in range(8)])]
    ppermute x2, waiting for transfers between devices: 5.84 us -> 4.08 us  [add_replica(): return value + lax.ppermute(value, 'z', [(i, i ^ step) for i in range(8)])]
    all_to_all x1, waiting for transfers between devices: 3.23 us -> 1.61 us  [worker_gradient(): top = lax.all_to_all(x_sum, 'y', 0, 0, tiled=True)]
  transfers between devices with their start and end apart: 11 -> 11, of which waited for: 7 -> 6; matrix products, arithmetic and copies ran while one was open for 5% -> 6% of each run, Pallas kernels for 5% -> 4%
where the time goes in v5:
time: 117 us
  starting transfers between devices  59.3 us (51%)
  waiting for transfers between devices  36.2 us (31%)
  Pallas kernels  11.3 us (10%)
  other arithmetic  6.55 us (6%)
  local copies, waits for them, and re-layouts  1.74 us (1%)
  between operations  1.44 us (1%)
    ppermute x1, starting transfers between devices, worker_gradient(): recv = lax.ppermute(send, 'c', [(0, 1), (1, 0)])  16.1 us
    ppermute x4, waiting for transfers between devices, swap_x(): return lax.ppermute(block, ('xp', 'xb'), [(i, i ^ k) for i in range(XL)])  13.7 us
    all_to_all x1, starting transfers between devices, on_device(): rows = lax.all_to_all(rows, ('xp', 'xb', 'y', 'c', 'xh'), 0, 0, tiled=True)  12.9 us
    ppermute x4, starting transfers between devices, swap_x(): return lax.ppermute(block, ('xp', 'xb'), [(i, i ^ k) for i in range(XL)])  11.2 us
    all_to_all x1, waiting for transfers between devices, on_device(): rows = lax.all_to_all(rows, ('xp', 'xb', 'y', 'c', 'xh'), 0, 0, tiled=True)  9.62 us
    ppermute x2, starting transfers between devices, add_replica(): return value + lax.ppermute(value, 'z', [(i, i ^ step) for i in range(8)])  7.26 us
    ppermute x1, waiting for transfers between devices, worker_gradient(): far_layer = lax.ppermute(local_layer, 'z', [(i, i ^ 4) for i in range(8)])  7.2 us
    all_to_all x1, starting transfers between devices, worker_gradient(): top = lax.all_to_all(x_sum, 'y', 0, 0, tiled=True)  6.31 us
  transfers between devices with their start and end apart: 11, of which 6 were waited for; matrix products, arithmetic and copies ran while one was open for 6% of the time, Pallas kernels for 4%

profile of v5, /device:TPU:1, one launch (start us, length us, event | category | flops | bytes accessed | tf_op | source)
XLA Modules:
  0.0 116.5 jit_solution(13331474288857857697)
XLA Ops:
  0.6 0.1 pad_add_fusion.place
  0.7 4.1 %split_norm.1 = (bf16[128,4096]{1,0:T(8,128)(2,1)}, bf16[128,4352]{1,0:T(8,128)(2,1)}) custom-call(s32[2]{0:T(128)S(1)} %pad_add_fusion.place, bf16[128,8192]{1,0:T(8,128)(2,1)} %hidden.1, bf16[8192]{0:T(1024)(128)(2,1)} %gain.1, bf16[128,256]{1,0:T(8,128)(2,1)} %cot.3), custom_call_target="tpu_custom_call" | custom-call | flops 8388608 | bytes 4194304 | tf_op jit(solution)/shard_map/split_norm/pallas_call | solution.py:64
  4.8 16.1 %collective-permute-start = (bf16[128,4352]{1,0:T(8,128)(2,1)}, bf16[128,4352]{1,0:T(8,128)(2,1)S(1)}, u32[]{:S(2)}, u32[]{:S(2)}) collective-permute-start(bf16[128,4352]{1,0:T(8,128)(2,1)} %get-tuple-element.20), channel_id=1, source_target_pairs={{0,2},{2,0},{1,3},{3,1},{4,6},{6,4},{5,7},{7,5},{8,10},{10,8},{9,1... | collective-permute-start | bytes 3342344 | tf_op jit(solution)/shard_map/ppermute | solution.py:208
  21.5 0.9 dynamic-slice_bitcast_fusion
  22.4 1.9 %collective-permute-start.4 = (f32[128,256]{1,0:T(8,128)S(1)}, f32[128,256]{1,0:T(8,128)S(1)}, u32[]{:S(2)}, u32[]{:S(2)}) collective-permute-start(f32[128,256]{1,0:T(8,128)S(1)} %dynamic-slice_bitcast_fusion), channel_id=1, source_target_pairs={{0,512},{128,640},{256,768},{384,896},{512,0},{640,128},{768,256},... | collective-permute-start | bytes 393224 | tf_op jit(solution)/shard_map/ppermute | solution.py:206
  24.3 0.0 collective-permute-done.recv.other_cot
  24.4 3.3 %chip_partial.1 = (f32[4,8,128,128]{3,2,1,0:T(8,128)S(1)}, f32[2,8,2,128,128]{4,3,2,1,0:T(8,128)S(1)}) custom-call(s32[2]{0:T(128)S(1)} %pad_add_fusion.place, bf16[128,4096]{1,0:T(8,128)(2,1)} %get-tuple-element.19.keep, bf16[128,4352]{1,0:T(8,128)(2,1)S(1)} %collective-permute-done.recv.other_cot, bf16[128,256]{1,0:T(8,128)(2,1)} %cot.3, ...), custom_call_target="tpu_custom_call" | custom-call | flops 536870912 | bytes 6291456 | tf_op jit(solution)/shard_map/chip_partial/pallas_call | solution.py:115
  27.7 1.2 %convert_element_type.47 = f16[2,8,2,128,128]{4,3,2,1,0:T(8,128)(2,1)} convert(f32[2,8,2,128,128]{4,3,2,1,0:T(8,128)S(1)} %get-tuple-element.22) | non-fusion elementwise | flops 524288 | bytes 3145728 | tf_op jit(solution)/shard_map/convert_element_type | solution.py:211
  28.9 7.2 %collective-permute-done.4 = f32[128,256]{1,0:T(8,128)S(1)} collective-permute-done((f32[128,256]{1,0:T(8,128)S(1)}, f32[128,256]{1,0:T(8,128)S(1)}, u32[]{:S(2)}, u32[]{:S(2)}) %collective-permute-start.4) | collective-permute-done | bytes 131104 | tf_op jit(solution)/shard_map/ppermute | solution.py:206
  36.1 3.7 %all-to-all-start = ((f16[16,2,128,128]{3,2,1,0:T(8,128)(2,1)}), f16[16,2,128,128]{3,2,1,0:T(8,128)(2,1)S(1)}, u32[]{:S(2)}, u32[]{:S(2)}) async-start(f16[16,2,128,128]{3,2,1,0:T(8,128)(2,1)} %bitcast.6), calls=%async_computation | async-start | bytes 2097152 | tf_op jit(solution)/shard_map/all_to_all | solution.py:213
  39.7 0.2 convert.8
  39.9 0.2 slice_bitcast_fusion.2
  40.2 3.2 %collective-permute-start.1 = (f16[8,128,128]{2,1,0:T(8,128)(2,1)S(1)}, f16[8,128,128]{2,1,0:T(8,128)(2,1)S(1)}, u32[]{:S(2)}, u32[]{:S(2)}) collective-permute-start(f16[8,128,128]{2,1,0:T(8,128)(2,1)S(1)} %get-tuple-element.35), channel_id=1, source_target_pairs={{0,32},{32,0},{64,96},{96,64},{1,33},{33,1},{65,97},{97,65},{2,34}... | collective-permute-start | bytes 786440 | tf_op jit(solution)/shard_map/ppermute | solution.py:195
  43.4 1.9 %collective-permute-start.2 = (f16[8,128,128]{2,1,0:T(8,128)(2,1)S(1)}, f16[8,128,128]{2,1,0:T(8,128)(2,1)S(1)}, u32[]{:S(2)}, u32[]{:S(2)}) collective-permute-start(f16[8,128,128]{2,1,0:T(8,128)(2,1)S(1)} %get-tuple-element.37), channel_id=1, source_target_pairs={{0,64},{32,96},{64,0},{96,32},{1,65},{33,97},{65,1},{97,33},{2,66}... | collective-permute-start | bytes 786440 | tf_op jit(solution)/shard_map/ppermute | solution.py:195
  45.3 4.2 %collective-permute-start.3 = (f16[8,128,128]{2,1,0:T(8,128)(2,1)S(1)}, f16[8,128,128]{2,1,0:T(8,128)(2,1)S(1)}, u32[]{:S(2)}, u32[]{:S(2)}) collective-permute-start(f16[8,128,128]{2,1,0:T(8,128)(2,1)S(1)} %get-tuple-element.36), channel_id=1, source_target_pairs={{0,96},{32,64},{64,32},{96,0},{1,97},{33,65},{65,33},{97,1},{2,98}... | collective-permute-start | bytes 786440 | tf_op jit(solution)/shard_map/ppermute | solution.py:195
  49.5 0.9 fusion.6
  50.4 1.9 %collective-permute-start.5 = (f32[128,256]{1,0:T(8,128)S(1)}, f32[128,256]{1,0:T(8,128)S(1)}, u32[]{:S(2)}, u32[]{:S(2)}) collective-permute-start(f32[128,256]{1,0:T(8,128)S(1)} %fusion.6), channel_id=1, source_target_pairs={{0,128},{128,0},{256,384},{384,256},{512,640},{640,512},{768,896},... | collective-permute-start | bytes 393224 | tf_op jit(solution)/shard_map/ppermute | solution.py:199
  52.3 4.1 %collective-permute-done.5 = f32[128,256]{1,0:T(8,128)S(1)} collective-permute-done((f32[128,256]{1,0:T(8,128)S(1)}, f32[128,256]{1,0:T(8,128)S(1)}, u32[]{:S(2)}, u32[]{:S(2)}) %collective-permute-start.5) | collective-permute-done | bytes 131104 | tf_op jit(solution)/shard_map/ppermute | solution.py:199
  56.4 8.1 %collective-permute-done.1 = f16[8,128,128]{2,1,0:T(8,128)(2,1)S(1)} collective-permute-done((f16[8,128,128]{2,1,0:T(8,128)(2,1)S(1)}, f16[8,128,128]{2,1,0:T(8,128)(2,1)S(1)}, u32[]{:S(2)}, u32[]{:S(2)}) %collective-permute-start.1) | collective-permute-done | bytes 262176 | tf_op jit(solution)/shard_map/ppermute | solution.py:195
  64.5 0.0 collective-permute-done.2
  64.5 5.6 %collective-permute-done.3 = f16[8,128,128]{2,1,0:T(8,128)(2,1)S(1)} collective-permute-done((f16[8,128,128]{2,1,0:T(8,128)(2,1)S(1)}, f16[8,128,128]{2,1,0:T(8,128)(2,1)S(1)}, u32[]{:S(2)}, u32[]{:S(2)}) %collective-permute-start.3) | collective-permute-done | bytes 262176 | tf_op jit(solution)/shard_map/ppermute | solution.py:195
  70.1 0.9 fusion.3
  71.0 0.0 all-to-all-done
  71.0 0.2 multiply_reduce_fusion
  71.2 6.3 %all-to-all-start.1 = ((f16[8,128,128]{2,1,0:T(8,128)(2,1)}), f16[8,128,128]{2,1,0:T(8,128)(2,1)S(1)}, u32[]{:S(2)}, u32[]{:S(2)}) async-start(f16[8,128,128]{2,1,0:T(8,128)(2,1)} %fusion.3), calls=%async_computation.1 | async-start | bytes 524288 | tf_op jit(solution)/shard_map/all_to_all | solution.py:223
  77.6 1.9 %collective-permute-start.6 = (f16[128,128]{1,0:T(8,128)(2,1)S(1)}, f16[128,128]{1,0:T(8,128)(2,1)S(1)}, u32[]{:S(2)}, u32[]{:S(2)}) collective-permute-start(f16[128,128]{1,0:T(8,128)(2,1)S(1)} %fusion.5), channel_id=1, source_target_pairs={{0,64},{32,96},{64,0},{96,32},{1,65},{33,97},{65,1},{97,33},{2,66}... | collective-permute-start | bytes 98312 | tf_op jit(solution)/shard_map/ppermute | solution.py:195
  79.5 5.3 %collective-permute-start.7 = (f32[128,256]{1,0:T(8,128)S(1)}, f32[128,256]{1,0:T(8,128)S(1)}, u32[]{:S(2)}, u32[]{:S(2)}) collective-permute-start(f32[128,256]{1,0:T(8,128)S(1)} %add.42), channel_id=1, source_target_pairs={{0,256},{128,384},{256,0},{384,128},{512,768},{640,896},{768,512},... | collective-permute-start | bytes 393224 | tf_op jit(solution)/shard_map/ppermute | solution.py:199
  84.8 0.0 collective-permute-done.6
  84.9 0.6 fusion.4.bottom
  85.5 1.6 %all-to-all-done.1 = f16[8,128,128]{2,1,0:T(8,128)(2,1)S(1)} async-done(((f16[8,128,128]{2,1,0:T(8,128)(2,1)}), f16[8,128,128]{2,1,0:T(8,128)(2,1)S(1)}, u32[]{:S(2)}, u32[]{:S(2)}) %all-to-all-start.1) | async-done | bytes 262176 | tf_op jit(solution)/shard_map/all_to_all | solution.py:223
  87.1 0.7 convert_reduce_fusion.top
  87.8 1.7 %turn_and_square.1 = (f32[128,256]{1,0:T(8,128)}, f32[128,1,128]{2,1,0:T(1,128)}) custom-call(f32[128,128]{1,0:T(8,128)} %convert_reduce_fusion.top, f32[128,128]{1,0:T(8,128)} %fusion.4.bottom), custom_call_target="tpu_custom_call" | custom-call | flops 131072 | bytes 262144 | tf_op jit(solution)/shard_map/turn_and_square/pallas_call | solution.py:148
  89.5 12.9 %all-to-all-start.2 = ((f32[128,1,128]{2,1,0:T(1,128)}), f32[128,1,128]{2,1,0:T(1,128)S(1)}, u32[]{:S(2)}, u32[]{:S(2)}) async-start(f32[128,1,128]{2,1,0:T(1,128)} %get-tuple-element.27), calls=%async_computation.2 | async-start | bytes 131072 | tf_op jit(solution)/shard_map/all_to_all | solution.py:245
  102.4 0.0 collective-permute-done.7
  102.4 1.7 %bitcast_subtract_fusion = (f32[128,256]{1,0:T(8,128)}, f32[128,256]{1,0:T(8,128)}) fusion(f32[8,128,256]{2,1,0:T(8,128)} %param.17, s32[]{:T(128)S(6)} %select_n.6, f32[128,256]{1,0:T(8,128)S(1)} %add.42, f32[128,256]{1,0:T(8,128)S(1)} %collective-permute-done.7, f32[8,128,256]{2,1,0:T(8,128)} %param.18), kind=kLoop, calls=%fused_computation.11 | loop fusion | flops 294912 | bytes 786436 | tf_op jit(solution)/shard_map/sub | solution.py:38
  104.1 9.6 %all-to-all-done.2.rows = f32[128,1,128]{2,1,0:T(1,128)S(1)} async-done(((f32[128,1,128]{2,1,0:T(1,128)}), f32[128,1,128]{2,1,0:T(1,128)S(1)}, u32[]{:S(2)}, u32[]{:S(2)}) %all-to-all-start.2) | async-done | bytes 65568 | tf_op jit(solution)/shard_map/all_to_all | solution.py:245
  113.7 0.0 copy-start
  113.7 0.6 copy-done
  114.4 2.2 %inner_update.1 = (f32[1,128,256]{2,1,0:T(8,128)}, f32[1,128,256]{2,1,0:T(8,128)}, f32[1,128,256]{2,1,0:T(8,128)}) custom-call(f32[128,1,128]{2,1,0:T(1,128)} %copy-done, f32[128,256]{1,0:T(8,128)} %get-tuple-element.28.gradient, f32[1,128,256]{2,1,0:T(8,128)} %params.1, f32[1,128,256]{2,1,0:T(8,128)} %first.1, f32[1,128,256]{2,1,0:T(8,128)} %second.1), custom_call_target="tpu_custom_call" | custom-call | flops 524288 | bytes 1048576 | tf_op jit(solution)/shard_map/inner_update/pallas_call | solution.py:182
  (2 shorter events, 0.0 us)
Async XLA Ops:
  4.8 19.6 %collective-permute-start = (bf16[128,4352]{1,0:T(8,128)(2,1)}, bf16[128,4352]{1,0:T(8,128)(2,1)S(1)}, u32[]{:S(2)}, u32[]{:S(2)}) collective-permute-start(bf16[128,4352]{1,0:T(8,128)(2,1)} %get-tuple-element.20), channel_id=1, source_target_pairs={{0,2},{2,0},{1,3},{3,1},{4,6},{6,4},{5,7},{7,5},{8,10},{10,8},{9,1... | collective-permute-start | bytes 3342344 | tf_op jit(solution)/shard_map/ppermute | solution.py:208
  22.4 13.7 %collective-permute-start.4 = (f32[128,256]{1,0:T(8,128)S(1)}, f32[128,256]{1,0:T(8,128)S(1)}, u32[]{:S(2)}, u32[]{:S(2)}) collective-permute-start(f32[128,256]{1,0:T(8,128)S(1)} %dynamic-slice_bitcast_fusion), channel_id=1, source_target_pairs={{0,512},{128,640},{256,768},{384,896},{512,0},{640,128},{768,256},... | collective-permute-start | bytes 393224 | tf_op jit(solution)/shard_map/ppermute | solution.py:206
  36.1 35.0 %all-to-all-start = ((f16[16,2,128,128]{3,2,1,0:T(8,128)(2,1)}), f16[16,2,128,128]{3,2,1,0:T(8,128)(2,1)S(1)}, u32[]{:S(2)}, u32[]{:S(2)}) async-start(f16[16,2,128,128]{3,2,1,0:T(8,128)(2,1)} %bitcast.6), calls=%async_computation | async-start | bytes 2097152 | tf_op jit(solution)/shard_map/all_to_all | solution.py:213
  40.2 24.4 %collective-permute-start.1 = (f16[8,128,128]{2,1,0:T(8,128)(2,1)S(1)}, f16[8,128,128]{2,1,0:T(8,128)(2,1)S(1)}, u32[]{:S(2)}, u32[]{:S(2)}) collective-permute-start(f16[8,128,128]{2,1,0:T(8,128)(2,1)S(1)} %get-tuple-element.35), channel_id=1, source_target_pairs={{0,32},{32,0},{64,96},{96,64},{1,33},{33,1},{65,97},{97,65},{2,34}... | collective-permute-start | bytes 786440 | tf_op jit(solution)/shard_map/ppermute | solution.py:195
  43.4 21.1 %collective-permute-start.2 = (f16[8,128,128]{2,1,0:T(8,128)(2,1)S(1)}, f16[8,128,128]{2,1,0:T(8,128)(2,1)S(1)}, u32[]{:S(2)}, u32[]{:S(2)}) collective-permute-start(f16[8,128,128]{2,1,0:T(8,128)(2,1)S(1)} %get-tuple-element.37), channel_id=1, source_target_pairs={{0,64},{32,96},{64,0},{96,32},{1,65},{33,97},{65,1},{97,33},{2,66}... | collective-permute-start | bytes 786440 | tf_op jit(solution)/shard_map/ppermute | solution.py:195
  45.3 24.9 %collective-permute-start.3 = (f16[8,128,128]{2,1,0:T(8,128)(2,1)S(1)}, f16[8,128,128]{2,1,0:T(8,128)(2,1)S(1)}, u32[]{:S(2)}, u32[]{:S(2)}) collective-permute-start(f16[8,128,128]{2,1,0:T(8,128)(2,1)S(1)} %get-tuple-element.36), channel_id=1, source_target_pairs={{0,96},{32,64},{64,32},{96,0},{1,97},{33,65},{65,33},{97,1},{2,98}... | collective-permute-start | bytes 786440 | tf_op jit(solution)/shard_map/ppermute | solution.py:195
  50.4 6.0 %collective-permute-start.5 = (f32[128,256]{1,0:T(8,128)S(1)}, f32[128,256]{1,0:T(8,128)S(1)}, u32[]{:S(2)}, u32[]{:S(2)}) collective-permute-start(f32[128,256]{1,0:T(8,128)S(1)} %fusion.6), channel_id=1, source_target_pairs={{0,128},{128,0},{256,384},{384,256},{512,640},{640,512},{768,896},... | collective-permute-start | bytes 393224 | tf_op jit(solution)/shard_map/ppermute | solution.py:199
  71.2 15.9 %all-to-all-start.1 = ((f16[8,128,128]{2,1,0:T(8,128)(2,1)}), f16[8,128,128]{2,1,0:T(8,128)(2,1)S(1)}, u32[]{:S(2)}, u32[]{:S(2)}) async-start(f16[8,128,128]{2,1,0:T(8,128)(2,1)} %fusion.3), calls=%async_computation.1 | async-start | bytes 524288 | tf_op jit(solution)/shard_map/all_to_all | solution.py:223
  77.6 7.3 %collective-permute-start.6 = (f16[128,128]{1,0:T(8,128)(2,1)S(1)}, f16[128,128]{1,0:T(8,128)(2,1)S(1)}, u32[]{:S(2)}, u32[]{:S(2)}) collective-permute-start(f16[128,128]{1,0:T(8,128)(2,1)S(1)} %fusion.5), channel_id=1, source_target_pairs={{0,64},{32,96},{64,0},{96,32},{1,65},{33,97},{65,1},{97,33},{2,66}... | collective-permute-start | bytes 98312 | tf_op jit(solution)/shard_map/ppermute | solution.py:195
  79.5 22.9 %collective-permute-start.7 = (f32[128,256]{1,0:T(8,128)S(1)}, f32[128,256]{1,0:T(8,128)S(1)}, u32[]{:S(2)}, u32[]{:S(2)}) collective-permute-start(f32[128,256]{1,0:T(8,128)S(1)} %add.42), channel_id=1, source_target_pairs={{0,256},{128,384},{256,0},{384,128},{512,768},{640,896},{768,512},... | collective-permute-start | bytes 393224 | tf_op jit(solution)/shard_map/ppermute | solution.py:199
  89.5 24.2 %all-to-all-start.2 = ((f32[128,1,128]{2,1,0:T(1,128)}), f32[128,1,128]{2,1,0:T(1,128)S(1)}, u32[]{:S(2)}, u32[]{:S(2)}) async-start(f32[128,1,128]{2,1,0:T(1,128)} %get-tuple-element.27), calls=%async_computation.2 | async-start | bytes 131072 | tf_op jit(solution)/shard_map/all_to_all | solution.py:245
  113.7 0.6 copy-start

commit v6 on v5

--- a/solution.py
+++ b/solution.py
@@ -203,19 +203,19 @@
     place = jnp.stack([lax.axis_index(("xp", "xb")), lax.axis_index("c")]).astype(jnp.int32)
     in_hbm = functools.partial(pltpu.with_memory_space_constraint, memory_space=pltpu.HBM)
     hidden_in, norm_gain, key_cotangent = map(in_hbm, (hidden_in, norm_gain, key_cotangent))
-    far_layer = lax.ppermute(local_layer, "z", [(i, i ^ 4) for i in range(8)])
+    other_layer = lax.ppermute(local_layer, "z", [(i, i ^ 2) for i in range(8)])
     keep, send = split_norm(place, hidden_in, norm_gain, key_cotangent)
     recv = lax.ppermute(send, "c", [(0, 1), (1, 0)])
     x_wide, y_wide = chip_partial(place, in_hbm(keep), recv, key_cotangent)
 
     y_half = y_wide.astype(jnp.float16).reshape(YN * XL // 2, 2, HC, FEAT)
-    y_half, far_layer = lax.optimization_barrier((y_half, far_layer))
+    y_half, other_layer = lax.optimization_barrier((y_half, other_layer))
     y_parts = lax.all_to_all(y_half, ("xb", "y"), 0, 0, tiled=True)
-    local_layer = local_layer + far_layer
+    local_layer = local_layer + other_layer
     x_sum = x_wide[0]
     for k in range(1, XL):
         x_sum = x_sum + swap_x(x_wide[k].astype(jnp.float16), k).astype(jnp.float32)
-    summed = add_replica(local_layer, 1)
+    summed = add_replica(local_layer, 4)
     x_sum = (x_sum * (X_SCALE / CHIP_SCALE)).astype(jnp.float16)
     x_sum, y_parts, summed = lax.optimization_barrier((x_sum, y_parts, summed))
     y_sum = jnp.sum(y_parts.astype(jnp.float32) * (Y_SCALE / CHIP_SCALE), axis=0)
@@ -223,7 +223,7 @@
     top = lax.all_to_all(x_sum, "y", 0, 0, tiled=True)
     bottom = y_sum[0] + swap_x(y_sum[1].astype(jnp.float16), 2).astype(jnp.float32)
     top = jnp.sum(top.astype(jnp.float32), axis=0)
-    return top, bottom, add_replica(summed, 2)
+    return top, bottom, add_replica(summed, 1)
 
 
 def on_device(

time: 117 us -> 110 us (0.940)
  waiting for transfers between devices: 36.2 us -> 20.9 us
  starting transfers between devices: 59.3 us -> 67.1 us
    ppermute x2, starting transfers between devices: 7.26 us -> 15.7 us  [add_replica(): return value + lax.ppermute(value, 'z', [(i, i ^ step) for i in range(8)])]
    ppermute x4, waiting for transfers between devices: 13.7 us -> 5.57 us  [swap_x(): return lax.ppermute(block, ('xp', 'xb'), [(i, i ^ k) for i in range(XL)])]
    ppermute x1, waiting for transfers between devices: 7.2 us -> 1.45 us  [worker_gradient(): other_layer = lax.ppermute(local_layer, 'z', [(i, i ^ 2) for i in range(8)])]
    ppermute x2, waiting for transfers between devices: 4.08 us -> 2.45 us  [add_replica(): return value + lax.ppermute(value, 'z', [(i, i ^ step) for i in range(8)])]
  transfers between devices with their start and end apart: 11 -> 11, of which waited for: 6 -> 6; matrix products, arithmetic and copies ran while one was open for 6% -> 7% of each run, Pallas kernels for 4% -> 5%
where the time goes in v6:
time: 110 us; the launch traced here: 109 us
  starting transfers between devices  67.1 us (61%)
  waiting for transfers between devices  20.9 us (19%)
  Pallas kernels  11.3 us (10%)
  other arithmetic  6.55 us (6%)
  local copies, waits for them, and re-layouts  1.74 us (2%)
  between operations  1.44 us (1%)
    ppermute x1, starting transfers between devices, worker_gradient(): recv = lax.ppermute(send, 'c', [(0, 1), (1, 0)])  16.1 us
    ppermute x2, starting transfers between devices, add_replica(): return value + lax.ppermute(value, 'z', [(i, i ^ step) for i in range(8)])  15.7 us
    all_to_all x1, starting transfers between devices, on_device(): rows = lax.all_to_all(rows, ('xp', 'xb', 'y', 'c', 'xh'), 0, 0, tiled=True)  12.2 us
    ppermute x4, starting transfers between devices, swap_x(): return lax.ppermute(block, ('xp', 'xb'), [(i, i ^ k) for i in range(XL)])  11.2 us
    all_to_all x1, waiting for transfers between devices, on_device(): rows = lax.all_to_all(rows, ('xp', 'xb', 'y', 'c', 'xh'), 0, 0, tiled=True)  9.62 us
    all_to_all x1, starting transfers between devices, worker_gradient(): top = lax.all_to_all(x_sum, 'y', 0, 0, tiled=True)  6.33 us
    ppermute x4, waiting for transfers between devices, swap_x(): return lax.ppermute(block, ('xp', 'xb'), [(i, i ^ k) for i in range(XL)])  5.57 us
    pallas_call x1, Pallas kernels, split_norm(): pl.pallas_call(norm_kernel, grid_spec=pltpu.PrefetchScalarGridSpec(num_sc...  4.07 us
  transfers between devices with their start and end apart: 11, of which 6 were waited for; matrix products, arithmetic and copies ran while one was open for 7% of the time, Pallas kernels for 5%

profile of v6, /device:TPU:1, one launch (start us, length us, event | category | flops | bytes accessed | tf_op | source)
XLA Modules:
  0.0 108.9 jit_solution(10790407157551666144)
XLA Ops:
  0.6 0.1 pad_add_fusion.place
  0.7 4.1 %split_norm.1 = (bf16[128,4096]{1,0:T(8,128)(2,1)}, bf16[128,4352]{1,0:T(8,128)(2,1)}) custom-call(s32[2]{0:T(128)S(1)} %pad_add_fusion.place, bf16[128,8192]{1,0:T(8,128)(2,1)} %hidden.1, bf16[8192]{0:T(1024)(128)(2,1)} %gain.1, bf16[128,256]{1,0:T(8,128)(2,1)} %cot.3), custom_call_target="tpu_custom_call" | custom-call | flops 8388608 | bytes 4194304 | tf_op jit(solution)/shard_map/split_norm/pallas_call | solution.py:64
  4.8 16.1 %collective-permute-start = (bf16[128,4352]{1,0:T(8,128)(2,1)}, bf16[128,4352]{1,0:T(8,128)(2,1)S(1)}, u32[]{:S(2)}, u32[]{:S(2)}) collective-permute-start(bf16[128,4352]{1,0:T(8,128)(2,1)} %get-tuple-element.20), channel_id=1, source_target_pairs={{0,2},{2,0},{1,3},{3,1},{4,6},{6,4},{5,7},{7,5},{8,10},{10,8},{9,1... | collective-permute-start | bytes 3342344 | tf_op jit(solution)/shard_map/ppermute | solution.py:208
  21.5 0.9 dynamic-slice_bitcast_fusion
  22.4 1.9 %collective-permute-start.4 = (f32[128,256]{1,0:T(8,128)S(1)}, f32[128,256]{1,0:T(8,128)S(1)}, u32[]{:S(2)}, u32[]{:S(2)}) collective-permute-start(f32[128,256]{1,0:T(8,128)S(1)} %dynamic-slice_bitcast_fusion), channel_id=1, source_target_pairs={{0,256},{128,384},{256,0},{384,128},{512,768},{640,896},{768,512},... | collective-permute-start | bytes 393224 | tf_op jit(solution)/shard_map/ppermute | solution.py:206
  24.3 0.0 collective-permute-done.recv.other_cot
  24.4 3.3 %chip_partial.1 = (f32[4,8,128,128]{3,2,1,0:T(8,128)S(1)}, f32[2,8,2,128,128]{4,3,2,1,0:T(8,128)S(1)}) custom-call(s32[2]{0:T(128)S(1)} %pad_add_fusion.place, bf16[128,4096]{1,0:T(8,128)(2,1)} %get-tuple-element.19.keep, bf16[128,4352]{1,0:T(8,128)(2,1)S(1)} %collective-permute-done.recv.other_cot, bf16[128,256]{1,0:T(8,128)(2,1)} %cot.3, ...), custom_call_target="tpu_custom_call" | custom-call | flops 536870912 | bytes 6291456 | tf_op jit(solution)/shard_map/chip_partial/pallas_call | solution.py:115
  27.7 1.2 %convert_element_type.47 = f16[2,8,2,128,128]{4,3,2,1,0:T(8,128)(2,1)} convert(f32[2,8,2,128,128]{4,3,2,1,0:T(8,128)S(1)} %get-tuple-element.22) | non-fusion elementwise | flops 524288 | bytes 3145728 | tf_op jit(solution)/shard_map/convert_element_type | solution.py:211
  28.9 1.5 %collective-permute-done.4 = f32[128,256]{1,0:T(8,128)S(1)} collective-permute-done((f32[128,256]{1,0:T(8,128)S(1)}, f32[128,256]{1,0:T(8,128)S(1)}, u32[]{:S(2)}, u32[]{:S(2)}) %collective-permute-start.4) | collective-permute-done | bytes 131104 | tf_op jit(solution)/shard_map/ppermute | solution.py:206
  30.3 3.7 %all-to-all-start = ((f16[16,2,128,128]{3,2,1,0:T(8,128)(2,1)}), f16[16,2,128,128]{3,2,1,0:T(8,128)(2,1)S(1)}, u32[]{:S(2)}, u32[]{:S(2)}) async-start(f16[16,2,128,128]{3,2,1,0:T(8,128)(2,1)} %bitcast.6), calls=%async_computation | async-start | bytes 2097152 | tf_op jit(solution)/shard_map/all_to_all | solution.py:213
  34.0 0.2 convert.8
  34.2 0.2 slice_bitcast_fusion.2
  34.4 3.2 %collective-permute-start.1 = (f16[8,128,128]{2,1,0:T(8,128)(2,1)S(1)}, f16[8,128,128]{2,1,0:T(8,128)(2,1)S(1)}, u32[]{:S(2)}, u32[]{:S(2)}) collective-permute-start(f16[8,128,128]{2,1,0:T(8,128)(2,1)S(1)} %get-tuple-element.35), channel_id=1, source_target_pairs={{0,32},{32,0},{64,96},{96,64},{1,33},{33,1},{65,97},{97,65},{2,34}... | collective-permute-start | bytes 786440 | tf_op jit(solution)/shard_map/ppermute | solution.py:195
  37.6 1.9 %collective-permute-start.2 = (f16[8,128,128]{2,1,0:T(8,128)(2,1)S(1)}, f16[8,128,128]{2,1,0:T(8,128)(2,1)S(1)}, u32[]{:S(2)}, u32[]{:S(2)}) collective-permute-start(f16[8,128,128]{2,1,0:T(8,128)(2,1)S(1)} %get-tuple-element.37), channel_id=1, source_target_pairs={{0,64},{32,96},{64,0},{96,32},{1,65},{33,97},{65,1},{97,33},{2,66}... | collective-permute-start | bytes 786440 | tf_op jit(solution)/shard_map/ppermute | solution.py:195
  39.5 4.2 %collective-permute-start.3 = (f16[8,128,128]{2,1,0:T(8,128)(2,1)S(1)}, f16[8,128,128]{2,1,0:T(8,128)(2,1)S(1)}, u32[]{:S(2)}, u32[]{:S(2)}) collective-permute-start(f16[8,128,128]{2,1,0:T(8,128)(2,1)S(1)} %get-tuple-element.36), channel_id=1, source_target_pairs={{0,96},{32,64},{64,32},{96,0},{1,97},{33,65},{65,33},{97,1},{2,98}... | collective-permute-start | bytes 786440 | tf_op jit(solution)/shard_map/ppermute | solution.py:195
  43.7 0.9 fusion.6
  44.6 10.9 %collective-permute-start.5 = (f32[128,256]{1,0:T(8,128)S(1)}, f32[128,256]{1,0:T(8,128)S(1)}, u32[]{:S(2)}, u32[]{:S(2)}) collective-permute-start(f32[128,256]{1,0:T(8,128)S(1)} %fusion.6), channel_id=1, source_target_pairs={{0,512},{128,640},{256,768},{384,896},{512,0},{640,128},{768,256},... | collective-permute-start | bytes 393224 | tf_op jit(solution)/shard_map/ppermute | solution.py:199
  55.5 2.4 %collective-permute-done.5 = f32[128,256]{1,0:T(8,128)S(1)} collective-permute-done((f32[128,256]{1,0:T(8,128)S(1)}, f32[128,256]{1,0:T(8,128)S(1)}, u32[]{:S(2)}, u32[]{:S(2)}) %collective-permute-start.5) | collective-permute-done | bytes 131104 | tf_op jit(solution)/shard_map/ppermute | solution.py:199
  58.0 1.7 %collective-permute-done.1 = f16[8,128,128]{2,1,0:T(8,128)(2,1)S(1)} collective-permute-done((f16[8,128,128]{2,1,0:T(8,128)(2,1)S(1)}, f16[8,128,128]{2,1,0:T(8,128)(2,1)S(1)}, u32[]{:S(2)}, u32[]{:S(2)}) %collective-permute-start.1) | collective-permute-done | bytes 262176 | tf_op jit(solution)/shard_map/ppermute | solution.py:195
  59.6 0.0 collective-permute-done.2
  59.6 3.9 %collective-permute-done.3 = f16[8,128,128]{2,1,0:T(8,128)(2,1)S(1)} collective-permute-done((f16[8,128,128]{2,1,0:T(8,128)(2,1)S(1)}, f16[8,128,128]{2,1,0:T(8,128)(2,1)S(1)}, u32[]{:S(2)}, u32[]{:S(2)}) %collective-permute-start.3) | collective-permute-done | bytes 262176 | tf_op jit(solution)/shard_map/ppermute | solution.py:195
  63.5 0.9 fusion.3
  64.4 0.0 all-to-all-done
  64.4 0.2 multiply_reduce_fusion
  64.6 6.3 %all-to-all-start.1 = ((f16[8,128,128]{2,1,0:T(8,128)(2,1)}), f16[8,128,128]{2,1,0:T(8,128)(2,1)S(1)}, u32[]{:S(2)}, u32[]{:S(2)}) async-start(f16[8,128,128]{2,1,0:T(8,128)(2,1)} %fusion.3), calls=%async_computation.1 | async-start | bytes 524288 | tf_op jit(solution)/shard_map/all_to_all | solution.py:223
  71.0 1.9 %collective-permute-start.6 = (f16[128,128]{1,0:T(8,128)(2,1)S(1)}, f16[128,128]{1,0:T(8,128)(2,1)S(1)}, u32[]{:S(2)}, u32[]{:S(2)}) collective-permute-start(f16[128,128]{1,0:T(8,128)(2,1)S(1)} %fusion.5), channel_id=1, source_target_pairs={{0,64},{32,96},{64,0},{96,32},{1,65},{33,97},{65,1},{97,33},{2,66}... | collective-permute-start | bytes 98312 | tf_op jit(solution)/shard_map/ppermute | solution.py:195
  72.9 4.8 %collective-permute-start.7 = (f32[128,256]{1,0:T(8,128)S(1)}, f32[128,256]{1,0:T(8,128)S(1)}, u32[]{:S(2)}, u32[]{:S(2)}) collective-permute-start(f32[128,256]{1,0:T(8,128)S(1)} %add.42), channel_id=1, source_target_pairs={{0,128},{128,0},{256,384},{384,256},{512,640},{640,512},{768,896},... | collective-permute-start | bytes 393224 | tf_op jit(solution)/shard_map/ppermute | solution.py:199
  77.7 0.0 collective-permute-done.6
  77.7 0.6 fusion.4.bottom
  78.4 1.8 %all-to-all-done.1 = f16[8,128,128]{2,1,0:T(8,128)(2,1)S(1)} async-done(((f16[8,128,128]{2,1,0:T(8,128)(2,1)}), f16[8,128,128]{2,1,0:T(8,128)(2,1)S(1)}, u32[]{:S(2)}, u32[]{:S(2)}) %all-to-all-start.1) | async-done | bytes 262176 | tf_op jit(solution)/shard_map/all_to_all | solution.py:223
  80.2 0.7 convert_reduce_fusion.top
  80.8 1.7 %turn_and_square.1 = (f32[128,256]{1,0:T(8,128)}, f32[128,1,128]{2,1,0:T(1,128)}) custom-call(f32[128,128]{1,0:T(8,128)} %convert_reduce_fusion.top, f32[128,128]{1,0:T(8,128)} %fusion.4.bottom), custom_call_target="tpu_custom_call" | custom-call | flops 131072 | bytes 262144 | tf_op jit(solution)/shard_map/turn_and_square/pallas_call | solution.py:148
  82.6 12.2 %all-to-all-start.2 = ((f32[128,1,128]{2,1,0:T(1,128)}), f32[128,1,128]{2,1,0:T(1,128)S(1)}, u32[]{:S(2)}, u32[]{:S(2)}) async-start(f32[128,1,128]{2,1,0:T(1,128)} %get-tuple-element.27), calls=%async_computation.2 | async-start | bytes 131072 | tf_op jit(solution)/shard_map/all_to_all | solution.py:245
  94.8 0.0 collective-permute-done.7
  94.8 1.7 %bitcast_subtract_fusion = (f32[128,256]{1,0:T(8,128)}, f32[128,256]{1,0:T(8,128)}) fusion(f32[8,128,256]{2,1,0:T(8,128)} %param.17, s32[]{:T(128)S(6)} %select_n.6, f32[128,256]{1,0:T(8,128)S(1)} %add.42, f32[128,256]{1,0:T(8,128)S(1)} %collective-permute-done.7, f32[8,128,256]{2,1,0:T(8,128)} %param.18), kind=kLoop, calls=%fused_computation.11 | loop fusion | flops 294912 | bytes 786436 | tf_op jit(solution)/shard_map/sub | solution.py:38
  96.5 9.6 %all-to-all-done.2.rows = f32[128,1,128]{2,1,0:T(1,128)S(1)} async-done(((f32[128,1,128]{2,1,0:T(1,128)}), f32[128,1,128]{2,1,0:T(1,128)S(1)}, u32[]{:S(2)}, u32[]{:S(2)}) %all-to-all-start.2) | async-done | bytes 65568 | tf_op jit(solution)/shard_map/all_to_all | solution.py:245
  106.2 0.0 copy-start
  106.2 0.6 copy-done
  106.8 2.2 %inner_update.1 = (f32[1,128,256]{2,1,0:T(8,128)}, f32[1,128,256]{2,1,0:T(8,128)}, f32[1,128,256]{2,1,0:T(8,128)}) custom-call(f32[128,1,128]{2,1,0:T(1,128)} %copy-done, f32[128,256]{1,0:T(8,128)} %get-tuple-element.28.gradient, f32[1,128,256]{2,1,0:T(8,128)} %params.1, f32[1,128,256]{2,1,0:T(8,128)} %first.1, f32[1,128,256]{2,1,0:T(8,128)} %second.1), custom_call_target="tpu_custom_call" | custom-call | flops 524288 | bytes 1048576 | tf_op jit(solution)/shard_map/inner_update/pallas_call | solution.py:182
  (2 shorter events, 0.0 us)
Async XLA Ops:
  4.8 19.6 %collective-permute-start = (bf16[128,4352]{1,0:T(8,128)(2,1)}, bf16[128,4352]{1,0:T(8,128)(2,1)S(1)}, u32[]{:S(2)}, u32[]{:S(2)}) collective-permute-start(bf16[128,4352]{1,0:T(8,128)(2,1)} %get-tuple-element.20), channel_id=1, source_target_pairs={{0,2},{2,0},{1,3},{3,1},{4,6},{6,4},{5,7},{7,5},{8,10},{10,8},{9,1... | collective-permute-start | bytes 3342344 | tf_op jit(solution)/shard_map/ppermute | solution.py:208
  22.4 7.9 %collective-permute-start.4 = (f32[128,256]{1,0:T(8,128)S(1)}, f32[128,256]{1,0:T(8,128)S(1)}, u32[]{:S(2)}, u32[]{:S(2)}) collective-permute-start(f32[128,256]{1,0:T(8,128)S(1)} %dynamic-slice_bitcast_fusion), channel_id=1, source_target_pairs={{0,256},{128,384},{256,0},{384,128},{512,768},{640,896},{768,512},... | collective-permute-start | bytes 393224 | tf_op jit(solution)/shard_map/ppermute | solution.py:206
  30.3 34.1 %all-to-all-start = ((f16[16,2,128,128]{3,2,1,0:T(8,128)(2,1)}), f16[16,2,128,128]{3,2,1,0:T(8,128)(2,1)S(1)}, u32[]{:S(2)}, u32[]{:S(2)}) async-start(f16[16,2,128,128]{3,2,1,0:T(8,128)(2,1)} %bitcast.6), calls=%async_computation | async-start | bytes 2097152 | tf_op jit(solution)/shard_map/all_to_all | solution.py:213
  34.4 25.2 %collective-permute-start.1 = (f16[8,128,128]{2,1,0:T(8,128)(2,1)S(1)}, f16[8,128,128]{2,1,0:T(8,128)(2,1)S(1)}, u32[]{:S(2)}, u32[]{:S(2)}) collective-permute-start(f16[8,128,128]{2,1,0:T(8,128)(2,1)S(1)} %get-tuple-element.35), channel_id=1, source_target_pairs={{0,32},{32,0},{64,96},{96,64},{1,33},{33,1},{65,97},{97,65},{2,34}... | collective-permute-start | bytes 786440 | tf_op jit(solution)/shard_map/ppermute | solution.py:195
  37.6 22.0 %collective-permute-start.2 = (f16[8,128,128]{2,1,0:T(8,128)(2,1)S(1)}, f16[8,128,128]{2,1,0:T(8,128)(2,1)S(1)}, u32[]{:S(2)}, u32[]{:S(2)}) collective-permute-start(f16[8,128,128]{2,1,0:T(8,128)(2,1)S(1)} %get-tuple-element.37), channel_id=1, source_target_pairs={{0,64},{32,96},{64,0},{96,32},{1,65},{33,97},{65,1},{97,33},{2,66}... | collective-permute-start | bytes 786440 | tf_op jit(solution)/shard_map/ppermute | solution.py:195
  39.5 24.0 %collective-permute-start.3 = (f16[8,128,128]{2,1,0:T(8,128)(2,1)S(1)}, f16[8,128,128]{2,1,0:T(8,128)(2,1)S(1)}, u32[]{:S(2)}, u32[]{:S(2)}) collective-permute-start(f16[8,128,128]{2,1,0:T(8,128)(2,1)S(1)} %get-tuple-element.36), channel_id=1, source_target_pairs={{0,96},{32,64},{64,32},{96,0},{1,97},{33,65},{65,33},{97,1},{2,98}... | collective-permute-start | bytes 786440 | tf_op jit(solution)/shard_map/ppermute | solution.py:195
  44.6 13.3 %collective-permute-start.5 = (f32[128,256]{1,0:T(8,128)S(1)}, f32[128,256]{1,0:T(8,128)S(1)}, u32[]{:S(2)}, u32[]{:S(2)}) collective-permute-start(f32[128,256]{1,0:T(8,128)S(1)} %fusion.6), channel_id=1, source_target_pairs={{0,512},{128,640},{256,768},{384,896},{512,0},{640,128},{768,256},... | collective-permute-start | bytes 393224 | tf_op jit(solution)/shard_map/ppermute | solution.py:199
  64.6 15.5 %all-to-all-start.1 = ((f16[8,128,128]{2,1,0:T(8,128)(2,1)}), f16[8,128,128]{2,1,0:T(8,128)(2,1)S(1)}, u32[]{:S(2)}, u32[]{:S(2)}) async-start(f16[8,128,128]{2,1,0:T(8,128)(2,1)} %fusion.3), calls=%async_computation.1 | async-start | bytes 524288 | tf_op jit(solution)/shard_map/all_to_all | solution.py:223
  71.0 6.7 %collective-permute-start.6 = (f16[128,128]{1,0:T(8,128)(2,1)S(1)}, f16[128,128]{1,0:T(8,128)(2,1)S(1)}, u32[]{:S(2)}, u32[]{:S(2)}) collective-permute-start(f16[128,128]{1,0:T(8,128)(2,1)S(1)} %fusion.5), channel_id=1, source_target_pairs={{0,64},{32,96},{64,0},{96,32},{1,65},{33,97},{65,1},{97,33},{2,66}... | collective-permute-start | bytes 98312 | tf_op jit(solution)/shard_map/ppermute | solution.py:195
  72.9 21.9 %collective-permute-start.7 = (f32[128,256]{1,0:T(8,128)S(1)}, f32[128,256]{1,0:T(8,128)S(1)}, u32[]{:S(2)}, u32[]{:S(2)}) collective-permute-start(f32[128,256]{1,0:T(8,128)S(1)} %add.42), channel_id=1, source_target_pairs={{0,128},{128,0},{256,384},{384,256},{512,640},{640,512},{768,896},... | collective-permute-start | bytes 393224 | tf_op jit(solution)/shard_map/ppermute | solution.py:199
  82.6 23.6 %all-to-all-start.2 = ((f32[128,1,128]{2,1,0:T(1,128)}), f32[128,1,128]{2,1,0:T(1,128)S(1)}, u32[]{:S(2)}, u32[]{:S(2)}) async-start(f32[128,1,128]{2,1,0:T(1,128)} %get-tuple-element.27), calls=%async_computation.2 | async-start | bytes 131072 | tf_op jit(solution)/shard_map/all_to_all | solution.py:245
  106.2 0.6 copy-start

commit v7 on v6

--- a/solution.py
+++ b/solution.py
@@ -203,7 +203,7 @@
     place = jnp.stack([lax.axis_index(("xp", "xb")), lax.axis_index("c")]).astype(jnp.int32)
     in_hbm = functools.partial(pltpu.with_memory_space_constraint, memory_space=pltpu.HBM)
     hidden_in, norm_gain, key_cotangent = map(in_hbm, (hidden_in, norm_gain, key_cotangent))
-    other_layer = lax.ppermute(local_layer, "z", [(i, i ^ 2) for i in range(8)])
+    other_layer = lax.ppermute(local_layer, "z", [(i, i ^ 1) for i in range(8)])
     keep, send = split_norm(place, hidden_in, norm_gain, key_cotangent)
     recv = lax.ppermute(send, "c", [(0, 1), (1, 0)])
     x_wide, y_wide = chip_partial(place, in_hbm(keep), recv, key_cotangent)
@@ -213,7 +213,7 @@
     y_parts = lax.all_to_all(y_half, ("xb", "y"), 0, 0, tiled=True)
     local_layer = local_layer + other_layer
     x_sum = x_wide[0]
-    for k in range(1, XL):
+    for k in reversed(range(1, XL)):
         x_sum = x_sum + swap_x(x_wide[k].astype(jnp.float16), k).astype(jnp.float32)
     summed = add_replica(local_layer, 4)
     x_sum = (x_sum * (X_SCALE / CHIP_SCALE)).astype(jnp.float16)
@@ -223,7 +223,7 @@
     top = lax.all_to_all(x_sum, "y", 0, 0, tiled=True)
     bottom = y_sum[0] + swap_x(y_sum[1].astype(jnp.float16), 2).astype(jnp.float32)
     top = jnp.sum(top.astype(jnp.float32), axis=0)
-    return top, bottom, add_replica(summed, 1)
+    return top, bottom, add_replica(summed, 2)
 
 
 def on_device(

time: 110 us -> 109 us (level)
  starting transfers between devices: 67.1 us -> 64.3 us
  waiting for transfers between devices: 20.9 us -> 23 us
    ppermute x4, waiting for transfers between devices: 5.57 us -> 9.31 us  [swap_x(): return lax.ppermute(block, ('xp', 'xb'), [(i, i ^ k) for i in range(XL)])]
    ppermute x2, starting transfers between devices: 15.7 us -> 13.6 us  [add_replica(): return value + lax.ppermute(value, 'z', [(i, i ^ step) for i in range(8)])]
where the time goes in v7:
time: 109 us; the launch traced here: 108 us
  starting transfers between devices  64.3 us (59%)
  waiting for transfers between devices  23 us (21%)
  Pallas kernels  11.3 us (10%)
  other arithmetic  6.55 us (6%)
  local copies, waits for them, and re-layouts  1.74 us (2%)
  between operations  1.45 us (1%)
    ppermute x1, starting transfers between devices, worker_gradient(): recv = lax.ppermute(send, 'c', [(0, 1), (1, 0)])  16.1 us
    ppermute x2, starting transfers between devices, add_replica(): return value + lax.ppermute(value, 'z', [(i, i ^ step) for i in range(8)])  13.6 us
    all_to_all x1, starting transfers between devices, on_device(): rows = lax.all_to_all(rows, ('xp', 'xb', 'y', 'c', 'xh'), 0, 0, tiled=True)  12.2 us
    ppermute x4, starting transfers between devices, swap_x(): return lax.ppermute(block, ('xp', 'xb'), [(i, i ^ k) for i in range(XL)])  11.2 us
    all_to_all x1, waiting for transfers between devices, on_device(): rows = lax.all_to_all(rows, ('xp', 'xb', 'y', 'c', 'xh'), 0, 0, tiled=True)  9.62 us
    ppermute x4, waiting for transfers between devices, swap_x(): return lax.ppermute(block, ('xp', 'xb'), [(i, i ^ k) for i in range(XL)])  9.31 us
    all_to_all x1, starting transfers between devices, worker_gradient(): top = lax.all_to_all(x_sum, 'y', 0, 0, tiled=True)  5.7 us
    pallas_call x1, Pallas kernels, split_norm(): pl.pallas_call(norm_kernel, grid_spec=pltpu.PrefetchScalarGridSpec(num_sc...  4.07 us
  transfers between devices with their start and end apart: 11, of which 6 were waited for; matrix products, arithmetic and copies ran while one was open for 7% of the time, Pallas kernels for 5%

profile of v7, /device:TPU:1, one launch (start us, length us, event | category | flops | bytes accessed | tf_op | source)
XLA Modules:
  0.0 108.3 jit_solution(15718746653476063024)
XLA Ops:
  0.6 0.1 pad_add_fusion.place
  0.7 4.1 %split_norm.1 = (bf16[128,4096]{1,0:T(8,128)(2,1)}, bf16[128,4352]{1,0:T(8,128)(2,1)}) custom-call(s32[2]{0:T(128)S(1)} %pad_add_fusion.place, bf16[128,8192]{1,0:T(8,128)(2,1)} %hidden.1, bf16[8192]{0:T(1024)(128)(2,1)} %gain.1, bf16[128,256]{1,0:T(8,128)(2,1)} %cot.3), custom_call_target="tpu_custom_call" | custom-call | flops 8388608 | bytes 4194304 | tf_op jit(solution)/shard_map/split_norm/pallas_call | solution.py:64
  4.8 16.1 %collective-permute-start = (bf16[128,4352]{1,0:T(8,128)(2,1)}, bf16[128,4352]{1,0:T(8,128)(2,1)S(1)}, u32[]{:S(2)}, u32[]{:S(2)}) collective-permute-start(bf16[128,4352]{1,0:T(8,128)(2,1)} %get-tuple-element.20), channel_id=1, source_target_pairs={{0,2},{2,0},{1,3},{3,1},{4,6},{6,4},{5,7},{7,5},{8,10},{10,8},{9,1... | collective-permute-start | bytes 3342344 | tf_op jit(solution)/shard_map/ppermute | solution.py:208
  21.5 0.9 dynamic-slice_bitcast_fusion
  22.4 1.9 %collective-permute-start.4 = (f32[128,256]{1,0:T(8,128)S(1)}, f32[128,256]{1,0:T(8,128)S(1)}, u32[]{:S(2)}, u32[]{:S(2)}) collective-permute-start(f32[128,256]{1,0:T(8,128)S(1)} %dynamic-slice_bitcast_fusion), channel_id=1, source_target_pairs={{0,128},{128,0},{256,384},{384,256},{512,640},{640,512},{768,896},... | collective-permute-start | bytes 393224 | tf_op jit(solution)/shard_map/ppermute | solution.py:206
  24.3 0.0 collective-permute-done.recv.other_cot
  24.4 3.3 %chip_partial.1 = (f32[4,8,128,128]{3,2,1,0:T(8,128)S(1)}, f32[2,8,2,128,128]{4,3,2,1,0:T(8,128)S(1)}) custom-call(s32[2]{0:T(128)S(1)} %pad_add_fusion.place, bf16[128,4096]{1,0:T(8,128)(2,1)} %get-tuple-element.19.keep, bf16[128,4352]{1,0:T(8,128)(2,1)S(1)} %collective-permute-done.recv.other_cot, bf16[128,256]{1,0:T(8,128)(2,1)} %cot.3, ...), custom_call_target="tpu_custom_call" | custom-call | flops 536870912 | bytes 6291456 | tf_op jit(solution)/shard_map/chip_partial/pallas_call | solution.py:115
  27.7 1.2 %convert_element_type.47 = f16[2,8,2,128,128]{4,3,2,1,0:T(8,128)(2,1)} convert(f32[2,8,2,128,128]{4,3,2,1,0:T(8,128)S(1)} %get-tuple-element.22) | non-fusion elementwise | flops 524288 | bytes 3145728 | tf_op jit(solution)/shard_map/convert_element_type | solution.py:211
  28.9 0.6 collective-permute-done.4
  29.4 3.7 %all-to-all-start = ((f16[16,2,128,128]{3,2,1,0:T(8,128)(2,1)}), f16[16,2,128,128]{3,2,1,0:T(8,128)(2,1)S(1)}, u32[]{:S(2)}, u32[]{:S(2)}) async-start(f16[16,2,128,128]{3,2,1,0:T(8,128)(2,1)} %bitcast.6), calls=%async_computation | async-start | bytes 2097152 | tf_op jit(solution)/shard_map/all_to_all | solution.py:213
  33.1 0.2 convert.8
  33.3 0.2 slice_bitcast_fusion.2
  33.5 1.9 %collective-permute-start.1 = (f16[8,128,128]{2,1,0:T(8,128)(2,1)S(1)}, f16[8,128,128]{2,1,0:T(8,128)(2,1)S(1)}, u32[]{:S(2)}, u32[]{:S(2)}) collective-permute-start(f16[8,128,128]{2,1,0:T(8,128)(2,1)S(1)} %get-tuple-element.35), channel_id=1, source_target_pairs={{0,96},{32,64},{64,32},{96,0},{1,97},{33,65},{65,33},{97,1},{2,98}... | collective-permute-start | bytes 786440 | tf_op jit(solution)/shard_map/ppermute | solution.py:195
  35.4 4.4 %collective-permute-start.2 = (f16[8,128,128]{2,1,0:T(8,128)(2,1)S(1)}, f16[8,128,128]{2,1,0:T(8,128)(2,1)S(1)}, u32[]{:S(2)}, u32[]{:S(2)}) collective-permute-start(f16[8,128,128]{2,1,0:T(8,128)(2,1)S(1)} %get-tuple-element.37), channel_id=1, source_target_pairs={{0,64},{32,96},{64,0},{96,32},{1,65},{33,97},{65,1},{97,33},{2,66}... | collective-permute-start | bytes 786440 | tf_op jit(solution)/shard_map/ppermute | solution.py:195
  39.8 3.0 %collective-permute-start.3 = (f16[8,128,128]{2,1,0:T(8,128)(2,1)S(1)}, f16[8,128,128]{2,1,0:T(8,128)(2,1)S(1)}, u32[]{:S(2)}, u32[]{:S(2)}) collective-permute-start(f16[8,128,128]{2,1,0:T(8,128)(2,1)S(1)} %get-tuple-element.36), channel_id=1, source_target_pairs={{0,32},{32,0},{64,96},{96,64},{1,33},{33,1},{65,97},{97,65},{2,34}... | collective-permute-start | bytes 786440 | tf_op jit(solution)/shard_map/ppermute | solution.py:195
  42.8 0.9 fusion.6
  43.7 7.8 %collective-permute-start.5 = (f32[128,256]{1,0:T(8,128)S(1)}, f32[128,256]{1,0:T(8,128)S(1)}, u32[]{:S(2)}, u32[]{:S(2)}) collective-permute-start(f32[128,256]{1,0:T(8,128)S(1)} %fusion.6), channel_id=1, source_target_pairs={{0,512},{128,640},{256,768},{384,896},{512,0},{640,128},{768,256},... | collective-permute-start | bytes 393224 | tf_op jit(solution)/shard_map/ppermute | solution.py:199
  51.6 2.6 %collective-permute-done.5 = f32[128,256]{1,0:T(8,128)S(1)} collective-permute-done((f32[128,256]{1,0:T(8,128)S(1)}, f32[128,256]{1,0:T(8,128)S(1)}, u32[]{:S(2)}, u32[]{:S(2)}) %collective-permute-start.5) | collective-permute-done | bytes 131104 | tf_op jit(solution)/shard_map/ppermute | solution.py:199
  54.2 0.0 collective-permute-done.1
  54.2 5.8 %collective-permute-done.2 = f16[8,128,128]{2,1,0:T(8,128)(2,1)S(1)} collective-permute-done((f16[8,128,128]{2,1,0:T(8,128)(2,1)S(1)}, f16[8,128,128]{2,1,0:T(8,128)(2,1)S(1)}, u32[]{:S(2)}, u32[]{:S(2)}) %collective-permute-start.2) | collective-permute-done | bytes 262176 | tf_op jit(solution)/shard_map/ppermute | solution.py:195
  60.0 3.5 %collective-permute-done.3 = f16[8,128,128]{2,1,0:T(8,128)(2,1)S(1)} collective-permute-done((f16[8,128,128]{2,1,0:T(8,128)(2,1)S(1)}, f16[8,128,128]{2,1,0:T(8,128)(2,1)S(1)}, u32[]{:S(2)}, u32[]{:S(2)}) %collective-permute-start.3) | collective-permute-done | bytes 262176 | tf_op jit(solution)/shard_map/ppermute | solution.py:195
  63.5 0.9 fusion.3
  64.4 0.0 all-to-all-done
  64.4 0.2 multiply_reduce_fusion
  64.6 5.7 %all-to-all-start.1 = ((f16[8,128,128]{2,1,0:T(8,128)(2,1)}), f16[8,128,128]{2,1,0:T(8,128)(2,1)S(1)}, u32[]{:S(2)}, u32[]{:S(2)}) async-start(f16[8,128,128]{2,1,0:T(8,128)(2,1)} %fusion.3), calls=%async_computation.1 | async-start | bytes 524288 | tf_op jit(solution)/shard_map/all_to_all | solution.py:223
  70.3 1.9 %collective-permute-start.6 = (f16[128,128]{1,0:T(8,128)(2,1)S(1)}, f16[128,128]{1,0:T(8,128)(2,1)S(1)}, u32[]{:S(2)}, u32[]{:S(2)}) collective-permute-start(f16[128,128]{1,0:T(8,128)(2,1)S(1)} %fusion.5), channel_id=1, source_target_pairs={{0,64},{32,96},{64,0},{96,32},{1,65},{33,97},{65,1},{97,33},{2,66}... | collective-permute-start | bytes 98312 | tf_op jit(solution)/shard_map/ppermute | solution.py:195
  72.3 5.7 %collective-permute-start.7 = (f32[128,256]{1,0:T(8,128)S(1)}, f32[128,256]{1,0:T(8,128)S(1)}, u32[]{:S(2)}, u32[]{:S(2)}) collective-permute-start(f32[128,256]{1,0:T(8,128)S(1)} %add.42), channel_id=1, source_target_pairs={{0,256},{128,384},{256,0},{384,128},{512,768},{640,896},{768,512},... | collective-permute-start | bytes 393224 | tf_op jit(solution)/shard_map/ppermute | solution.py:199
  78.0 0.0 collective-permute-done.6
  78.0 0.6 fusion.4.bottom
  78.7 0.9 all-to-all-done.1
  79.5 0.7 convert_reduce_fusion.top
  80.2 1.7 %turn_and_square.1 = (f32[128,256]{1,0:T(8,128)}, f32[128,1,128]{2,1,0:T(1,128)}) custom-call(f32[128,128]{1,0:T(8,128)} %convert_reduce_fusion.top, f32[128,128]{1,0:T(8,128)} %fusion.4.bottom), custom_call_target="tpu_custom_call" | custom-call | flops 131072 | bytes 262144 | tf_op jit(solution)/shard_map/turn_and_square/pallas_call | solution.py:148
  81.9 12.2 %all-to-all-start.2 = ((f32[128,1,128]{2,1,0:T(1,128)}), f32[128,1,128]{2,1,0:T(1,128)S(1)}, u32[]{:S(2)}, u32[]{:S(2)}) async-start(f32[128,1,128]{2,1,0:T(1,128)} %get-tuple-element.27), calls=%async_computation.2 | async-start | bytes 131072 | tf_op jit(solution)/shard_map/all_to_all | solution.py:245
  94.1 0.0 collective-permute-done.7
  94.2 1.7 %bitcast_subtract_fusion = (f32[128,256]{1,0:T(8,128)}, f32[128,256]{1,0:T(8,128)}) fusion(f32[8,128,256]{2,1,0:T(8,128)} %param.17, s32[]{:T(128)S(6)} %select_n.6, f32[128,256]{1,0:T(8,128)S(1)} %add.42, f32[128,256]{1,0:T(8,128)S(1)} %collective-permute-done.7, f32[8,128,256]{2,1,0:T(8,128)} %param.18), kind=kLoop, calls=%fused_computation.11 | loop fusion | flops 294912 | bytes 786436 | tf_op jit(solution)/shard_map/sub | solution.py:38
  95.9 9.6 %all-to-all-done.2.rows = f32[128,1,128]{2,1,0:T(1,128)S(1)} async-done(((f32[128,1,128]{2,1,0:T(1,128)}), f32[128,1,128]{2,1,0:T(1,128)S(1)}, u32[]{:S(2)}, u32[]{:S(2)}) %all-to-all-start.2) | async-done | bytes 65568 | tf_op jit(solution)/shard_map/all_to_all | solution.py:245
  105.5 0.0 copy-start
  105.5 0.6 copy-done
  106.1 2.2 %inner_update.1 = (f32[1,128,256]{2,1,0:T(8,128)}, f32[1,128,256]{2,1,0:T(8,128)}, f32[1,128,256]{2,1,0:T(8,128)}) custom-call(f32[128,1,128]{2,1,0:T(1,128)} %copy-done, f32[128,256]{1,0:T(8,128)} %get-tuple-element.28.gradient, f32[1,128,256]{2,1,0:T(8,128)} %params.1, f32[1,128,256]{2,1,0:T(8,128)} %first.1, f32[1,128,256]{2,1,0:T(8,128)} %second.1), custom_call_target="tpu_custom_call" | custom-call | flops 524288 | bytes 1048576 | tf_op jit(solution)/shard_map/inner_update/pallas_call | solution.py:182
  (2 shorter events, 0.0 us)
Async XLA Ops:
  4.8 19.6 %collective-permute-start = (bf16[128,4352]{1,0:T(8,128)(2,1)}, bf16[128,4352]{1,0:T(8,128)(2,1)S(1)}, u32[]{:S(2)}, u32[]{:S(2)}) collective-permute-start(bf16[128,4352]{1,0:T(8,128)(2,1)} %get-tuple-element.20), channel_id=1, source_target_pairs={{0,2},{2,0},{1,3},{3,1},{4,6},{6,4},{5,7},{7,5},{8,10},{10,8},{9,1... | collective-permute-start | bytes 3342344 | tf_op jit(solution)/shard_map/ppermute | solution.py:208
  22.4 7.0 %collective-permute-start.4 = (f32[128,256]{1,0:T(8,128)S(1)}, f32[128,256]{1,0:T(8,128)S(1)}, u32[]{:S(2)}, u32[]{:S(2)}) collective-permute-start(f32[128,256]{1,0:T(8,128)S(1)} %dynamic-slice_bitcast_fusion), channel_id=1, source_target_pairs={{0,128},{128,0},{256,384},{384,256},{512,640},{640,512},{768,896},... | collective-permute-start | bytes 393224 | tf_op jit(solution)/shard_map/ppermute | solution.py:206
  29.4 35.0 %all-to-all-start = ((f16[16,2,128,128]{3,2,1,0:T(8,128)(2,1)}), f16[16,2,128,128]{3,2,1,0:T(8,128)(2,1)S(1)}, u32[]{:S(2)}, u32[]{:S(2)}) async-start(f16[16,2,128,128]{3,2,1,0:T(8,128)(2,1)} %bitcast.6), calls=%async_computation | async-start | bytes 2097152 | tf_op jit(solution)/shard_map/all_to_all | solution.py:213
  33.5 20.7 %collective-permute-start.1 = (f16[8,128,128]{2,1,0:T(8,128)(2,1)S(1)}, f16[8,128,128]{2,1,0:T(8,128)(2,1)S(1)}, u32[]{:S(2)}, u32[]{:S(2)}) collective-permute-start(f16[8,128,128]{2,1,0:T(8,128)(2,1)S(1)} %get-tuple-element.35), channel_id=1, source_target_pairs={{0,96},{32,64},{64,32},{96,0},{1,97},{33,65},{65,33},{97,1},{2,98}... | collective-permute-start | bytes 786440 | tf_op jit(solution)/shard_map/ppermute | solution.py:195
  35.4 24.6 %collective-permute-start.2 = (f16[8,128,128]{2,1,0:T(8,128)(2,1)S(1)}, f16[8,128,128]{2,1,0:T(8,128)(2,1)S(1)}, u32[]{:S(2)}, u32[]{:S(2)}) collective-permute-start(f16[8,128,128]{2,1,0:T(8,128)(2,1)S(1)} %get-tuple-element.37), channel_id=1, source_target_pairs={{0,64},{32,96},{64,0},{96,32},{1,65},{33,97},{65,1},{97,33},{2,66}... | collective-permute-start | bytes 786440 | tf_op jit(solution)/shard_map/ppermute | solution.py:195
  39.8 23.7 %collective-permute-start.3 = (f16[8,128,128]{2,1,0:T(8,128)(2,1)S(1)}, f16[8,128,128]{2,1,0:T(8,128)(2,1)S(1)}, u32[]{:S(2)}, u32[]{:S(2)}) collective-permute-start(f16[8,128,128]{2,1,0:T(8,128)(2,1)S(1)} %get-tuple-element.36), channel_id=1, source_target_pairs={{0,32},{32,0},{64,96},{96,64},{1,33},{33,1},{65,97},{97,65},{2,34}... | collective-permute-start | bytes 786440 | tf_op jit(solution)/shard_map/ppermute | solution.py:195
  43.7 10.5 %collective-permute-start.5 = (f32[128,256]{1,0:T(8,128)S(1)}, f32[128,256]{1,0:T(8,128)S(1)}, u32[]{:S(2)}, u32[]{:S(2)}) collective-permute-start(f32[128,256]{1,0:T(8,128)S(1)} %fusion.6), channel_id=1, source_target_pairs={{0,512},{128,640},{256,768},{384,896},{512,0},{640,128},{768,256},... | collective-permute-start | bytes 393224 | tf_op jit(solution)/shard_map/ppermute | solution.py:199
  64.6 14.9 %all-to-all-start.1 = ((f16[8,128,128]{2,1,0:T(8,128)(2,1)}), f16[8,128,128]{2,1,0:T(8,128)(2,1)S(1)}, u32[]{:S(2)}, u32[]{:S(2)}) async-start(f16[8,128,128]{2,1,0:T(8,128)(2,1)} %fusion.3), calls=%async_computation.1 | async-start | bytes 524288 | tf_op jit(solution)/shard_map/all_to_all | solution.py:223
  70.3 7.7 %collective-permute-start.6 = (f16[128,128]{1,0:T(8,128)(2,1)S(1)}, f16[128,128]{1,0:T(8,128)(2,1)S(1)}, u32[]{:S(2)}, u32[]{:S(2)}) collective-permute-start(f16[128,128]{1,0:T(8,128)(2,1)S(1)} %fusion.5), channel_id=1, source_target_pairs={{0,64},{32,96},{64,0},{96,32},{1,65},{33,97},{65,1},{97,33},{2,66}... | collective-permute-start | bytes 98312 | tf_op jit(solution)/shard_map/ppermute | solution.py:195
  72.3 21.9 %collective-permute-start.7 = (f32[128,256]{1,0:T(8,128)S(1)}, f32[128,256]{1,0:T(8,128)S(1)}, u32[]{:S(2)}, u32[]{:S(2)}) collective-permute-start(f32[128,256]{1,0:T(8,128)S(1)} %add.42), channel_id=1, source_target_pairs={{0,256},{128,384},{256,0},{384,128},{512,768},{640,896},{768,512},... | collective-permute-start | bytes 393224 | tf_op jit(solution)/shard_map/ppermute | solution.py:199
  81.9 23.6 %all-to-all-start.2 = ((f32[128,1,128]{2,1,0:T(1,128)}), f32[128,1,128]{2,1,0:T(1,128)S(1)}, u32[]{:S(2)}, u32[]{:S(2)}) async-start(f32[128,1,128]{2,1,0:T(1,128)} %get-tuple-element.27), calls=%async_computation.2 | async-start | bytes 131072 | tf_op jit(solution)/shard_map/all_to_all | solution.py:245
  105.5 0.6 copy-start

commit v8 on v7

--- a/solution.py
+++ b/solution.py
@@ -24,7 +24,7 @@
 TOK, COLS, FEAT = 128, 256, 128
 HALF = XL * YN * FEAT
 WIDE = HALF * CORES
-HC = COLS // 2
+XC, YC = 96, COLS - 96
 NORM_ROWS = 64
 CHIP_SCALE = 2.0**-8
 X_SCALE = 2.0**-10
@@ -104,8 +104,8 @@
         product = product * CHIP_SCALE
         for row in range(YN):
             block = product[:, row * FEAT : (row + 1) * FEAT]
-            x_out[near, row] = block[:HC]
-            y_out[dest, row, 0] = block[HC:]
+            x_out[near, row] = block[:XC]
+            y_out[dest, row, 0] = block[XC:]
 
 
 def chip_partial(place, keep, recv, cot):
@@ -119,14 +119,14 @@
             grid=(XL // 2,),
             in_specs=[chunk, chunk, mine, other],
             out_specs=[
-                pl.BlockSpec((2, YN, HC, FEAT), lambda far, place: (far, 0, 0, 0)),
-                pl.BlockSpec((2, YN, 1, HC, FEAT), lambda far, place: (0, 0, far, 0, 0)),
+                pl.BlockSpec((2, YN, XC, FEAT), lambda far, place: (far, 0, 0, 0)),
+                pl.BlockSpec((2, YN, 1, YC, FEAT), lambda far, place: (0, 0, far, 0, 0)),
             ],
             scratch_shapes=[pltpu.VMEM((COLS, CORES * TOK), jnp.bfloat16)],
         ),
         out_shape=[
-            jax.ShapeDtypeStruct((XL, YN, HC, FEAT), jnp.float32),
-            jax.ShapeDtypeStruct((XL // 2, YN, 2, HC, FEAT), jnp.float32),
+            jax.ShapeDtypeStruct((XL, YN, XC, FEAT), jnp.float32),
+            jax.ShapeDtypeStruct((XL // 2, YN, 2, YC, FEAT), jnp.float32),
         ],
         cost_estimate=pl.CostEstimate(
             flops=4 * TOK * HALF * COLS, bytes_accessed=6 * 2**20, transcendentals=0
@@ -138,9 +138,9 @@
 
 def square_kernel(top, bottom, gradient, rows):
     upper, lower = top[...] * (1.0 / X_SCALE), bottom[...] * (1.0 / Y_SCALE)
-    gradient[:, :HC] = upper.T
-    gradient[:, HC:] = lower.T
-    total = jnp.sum(upper * upper + lower * lower)
+    both = jnp.concatenate([upper, lower], axis=0)
+    gradient[...] = both.T
+    total = jnp.sum(both * both)
     rows[...] = jnp.full(rows.shape, total, jnp.float32)
 
 
@@ -208,7 +208,7 @@
     recv = lax.ppermute(send, "c", [(0, 1), (1, 0)])
     x_wide, y_wide = chip_partial(place, in_hbm(keep), recv, key_cotangent)
 
-    y_half = y_wide.astype(jnp.float16).reshape(YN * XL // 2, 2, HC, FEAT)
+    y_half = y_wide.astype(jnp.float16).reshape(YN * XL // 2, 2, YC, FEAT)
     y_half, other_layer = lax.optimization_barrier((y_half, other_layer))
     y_parts = lax.all_to_all(y_half, ("xb", "y"), 0, 0, tiled=True)
     local_layer = local_layer + other_layer

time: 109 us -> 112 us (1.028)
  other arithmetic: 6.55 us -> 7.85 us
    all_to_all x1, waiting for transfers between devices: 0.01 us -> 1.49 us  [worker_gradient(): y_parts = lax.all_to_all(y_half, ('xb', 'y'), 0, 0, tiled=True)]
    reduce_sum x1, other arithmetic: 0.21 us -> 1.59 us  [worker_gradient(): jnp.sum(y_parts.astype(jnp.float32) * (Y_SCALE / CHIP_SCALE), axis=0)]
    all_to_all x1, starting transfers between devices: 5.7 us -> 7.02 us  [worker_gradient(): top = lax.all_to_all(x_sum, 'y', 0, 0, tiled=True)]
    ppermute x2, starting transfers between devices: 13.6 us -> 12.4 us  [add_replica(): return value + lax.ppermute(value, 'z', [(i, i ^ step) for i in range(8)])]
  transfers between devices with their start and end apart: 11 -> 11, of which waited for: 6 -> 8; matrix products, arithmetic and copies ran while one was open for 7% -> 6% of each run, Pallas kernels for 5% -> 5%
where the time goes in v8:
time: 112 us; the launch traced here: 111 us
  starting transfers between devices  65.2 us (58%)
  waiting for transfers between devices  23.9 us (21%)
  Pallas kernels  11.4 us (10%)
  other arithmetic  7.85 us (7%)
  local copies, waits for them, and re-layouts  1.65 us (1%)
  between operations  1.44 us (1%)
    ppermute x1, starting transfers between devices, worker_gradient(): recv = lax.ppermute(send, 'c', [(0, 1), (1, 0)])  16.1 us
    ppermute x2, starting transfers between devices, add_replica(): return value + lax.ppermute(value, 'z', [(i, i ^ step) for i in range(8)])  12.4 us
    all_to_all x1, starting transfers between devices, on_device(): rows = lax.all_to_all(rows, ('xp', 'xb', 'y', 'c', 'xh'), 0, 0, tiled=True)  12.2 us
    ppermute x4, starting transfers between devices, swap_x(): return lax.ppermute(block, ('xp', 'xb'), [(i, i ^ k) for i in range(XL)])  11.2 us
    all_to_all x1, waiting for transfers between devices, on_device(): rows = lax.all_to_all(rows, ('xp', 'xb', 'y', 'c', 'xh'), 0, 0, tiled=True)  9.62 us
    ppermute x4, waiting for transfers between devices, swap_x(): return lax.ppermute(block, ('xp', 'xb'), [(i, i ^ k) for i in range(XL)])  9.06 us
    all_to_all x1, starting transfers between devices, worker_gradient(): top = lax.all_to_all(x_sum, 'y', 0, 0, tiled=True)  7.02 us
    all_to_all x1, starting transfers between devices, worker_gradient(): y_parts = lax.all_to_all(y_half, ('xb', 'y'), 0, 0, tiled=True)  4.39 us
  transfers between devices with their start and end apart: 11, of which 8 were waited for; matrix products, arithmetic and copies ran while one was open for 6% of the time, Pallas kernels for 5%

profile of v8, /device:TPU:1, one launch (start us, length us, event | category | flops | bytes accessed | tf_op | source)
XLA Modules:
  0.0 111.4 jit_solution(1775802770570213074)
XLA Ops:
  0.6 0.1 pad_add_fusion.place
  0.7 4.1 %split_norm.1 = (bf16[128,4096]{1,0:T(8,128)(2,1)}, bf16[128,4352]{1,0:T(8,128)(2,1)}) custom-call(s32[2]{0:T(128)S(1)} %pad_add_fusion.place, bf16[128,8192]{1,0:T(8,128)(2,1)} %hidden.1, bf16[8192]{0:T(1024)(128)(2,1)} %gain.1, bf16[128,256]{1,0:T(8,128)(2,1)} %cot.3), custom_call_target="tpu_custom_call" | custom-call | flops 8388608 | bytes 4194304 | tf_op jit(solution)/shard_map/split_norm/pallas_call | solution.py:64
  4.8 16.1 %collective-permute-start = (bf16[128,4352]{1,0:T(8,128)(2,1)}, bf16[128,4352]{1,0:T(8,128)(2,1)S(1)}, u32[]{:S(2)}, u32[]{:S(2)}) collective-permute-start(bf16[128,4352]{1,0:T(8,128)(2,1)} %get-tuple-element.20), channel_id=1, source_target_pairs={{0,2},{2,0},{1,3},{3,1},{4,6},{6,4},{5,7},{7,5},{8,10},{10,8},{9,1... | collective-permute-start | bytes 3342344 | tf_op jit(solution)/shard_map/ppermute | solution.py:208
  21.5 0.9 dynamic-slice_bitcast_fusion
  22.4 1.9 %collective-permute-start.4 = (f32[128,256]{1,0:T(8,128)S(1)}, f32[128,256]{1,0:T(8,128)S(1)}, u32[]{:S(2)}, u32[]{:S(2)}) collective-permute-start(f32[128,256]{1,0:T(8,128)S(1)} %dynamic-slice_bitcast_fusion), channel_id=1, source_target_pairs={{0,128},{128,0},{256,384},{384,256},{512,640},{640,512},{768,896},... | collective-permute-start | bytes 393224 | tf_op jit(solution)/shard_map/ppermute | solution.py:206
  24.3 0.0 collective-permute-done.recv.other_cot
  24.4 3.3 %chip_partial.1 = (f32[4,8,96,128]{3,2,1,0:T(8,128)S(1)}, f32[2,8,2,160,128]{4,3,2,1,0:T(8,128)S(1)}) custom-call(s32[2]{0:T(128)S(1)} %pad_add_fusion.place, bf16[128,4096]{1,0:T(8,128)(2,1)} %get-tuple-element.19.keep, bf16[128,4352]{1,0:T(8,128)(2,1)S(1)} %collective-permute-done.recv.other_cot, bf16[128,256]{1,0:T(8,128)(2,1)} %cot.3, ...), custom_call_target="tpu_custom_call" | custom-call | flops 536870912 | bytes 6291456 | tf_op jit(solution)/shard_map/chip_partial/pallas_call | solution.py:115
  27.7 1.3 %convert_element_type.47 = f16[2,8,2,160,128]{4,3,2,1,0:T(8,128)(2,1)} convert(f32[2,8,2,160,128]{4,3,2,1,0:T(8,128)S(1)} %get-tuple-element.22) | non-fusion elementwise | flops 655360 | bytes 3932160 | tf_op jit(solution)/shard_map/convert_element_type | solution.py:211
  29.0 0.4 collective-permute-done.4
  29.4 4.4 %all-to-all-start = ((f16[16,2,160,128]{3,2,1,0:T(8,128)(2,1)}), f16[16,2,160,128]{3,2,1,0:T(8,128)(2,1)}, u32[]{:S(2)}, u32[]{:S(2)}) async-start(f16[16,2,160,128]{3,2,1,0:T(8,128)(2,1)} %bitcast.6), calls=%async_computation | async-start | bytes 2621440 | tf_op jit(solution)/shard_map/all_to_all | solution.py:213
  33.8 0.1 convert.8
  33.9 0.1 slice_bitcast_fusion.2
  34.1 1.9 %collective-permute-start.1 = (f16[8,96,128]{2,1,0:T(8,128)(2,1)S(1)}, f16[8,96,128]{2,1,0:T(8,128)(2,1)S(1)}, u32[]{:S(2)}, u32[]{:S(2)}) collective-permute-start(f16[8,96,128]{2,1,0:T(8,128)(2,1)S(1)} %get-tuple-element.35), channel_id=1, source_target_pairs={{0,96},{32,64},{64,32},{96,0},{1,97},{33,65},{65,33},{97,1},{2,98}... | collective-permute-start | bytes 589832 | tf_op jit(solution)/shard_map/ppermute | solution.py:195
  36.0 4.3 %collective-permute-start.2 = (f16[8,96,128]{2,1,0:T(8,128)(2,1)S(1)}, f16[8,96,128]{2,1,0:T(8,128)(2,1)S(1)}, u32[]{:S(2)}, u32[]{:S(2)}) collective-permute-start(f16[8,96,128]{2,1,0:T(8,128)(2,1)S(1)} %get-tuple-element.37), channel_id=1, source_target_pairs={{0,64},{32,96},{64,0},{96,32},{1,65},{33,97},{65,1},{97,33},{2,66}... | collective-permute-start | bytes 589832 | tf_op jit(solution)/shard_map/ppermute | solution.py:195
  40.3 3.0 %collective-permute-start.3 = (f16[8,96,128]{2,1,0:T(8,128)(2,1)S(1)}, f16[8,96,128]{2,1,0:T(8,128)(2,1)S(1)}, u32[]{:S(2)}, u32[]{:S(2)}) collective-permute-start(f16[8,96,128]{2,1,0:T(8,128)(2,1)S(1)} %get-tuple-element.36), channel_id=1, source_target_pairs={{0,32},{32,0},{64,96},{96,64},{1,33},{33,1},{65,97},{97,65},{2,34}... | collective-permute-start | bytes 589832 | tf_op jit(solution)/shard_map/ppermute | solution.py:195
  43.4 0.9 fusion.6
  44.3 7.3 %collective-permute-start.5 = (f32[128,256]{1,0:T(8,128)S(1)}, f32[128,256]{1,0:T(8,128)S(1)}, u32[]{:S(2)}, u32[]{:S(2)}) collective-permute-start(f32[128,256]{1,0:T(8,128)S(1)} %fusion.6), channel_id=1, source_target_pairs={{0,512},{128,640},{256,768},{384,896},{512,0},{640,128},{768,256},... | collective-permute-start | bytes 393224 | tf_op jit(solution)/shard_map/ppermute | solution.py:199
  51.6 2.4 %collective-permute-done.5 = f32[128,256]{1,0:T(8,128)S(1)} collective-permute-done((f32[128,256]{1,0:T(8,128)S(1)}, f32[128,256]{1,0:T(8,128)S(1)}, u32[]{:S(2)}, u32[]{:S(2)}) %collective-permute-start.5) | collective-permute-done | bytes 131104 | tf_op jit(solution)/shard_map/ppermute | solution.py:199
  53.9 0.6 collective-permute-done.1
  54.6 4.2 %collective-permute-done.2 = f16[8,96,128]{2,1,0:T(8,128)(2,1)S(1)} collective-permute-done((f16[8,96,128]{2,1,0:T(8,128)(2,1)S(1)}, f16[8,96,128]{2,1,0:T(8,128)(2,1)S(1)}, u32[]{:S(2)}, u32[]{:S(2)}) %collective-permute-start.2) | collective-permute-done | bytes 196640 | tf_op jit(solution)/shard_map/ppermute | solution.py:195
  58.8 4.2 %collective-permute-done.3 = f16[8,96,128]{2,1,0:T(8,128)(2,1)S(1)} collective-permute-done((f16[8,96,128]{2,1,0:T(8,128)(2,1)S(1)}, f16[8,96,128]{2,1,0:T(8,128)(2,1)S(1)}, u32[]{:S(2)}, u32[]{:S(2)}) %collective-permute-start.3) | collective-permute-done | bytes 196640 | tf_op jit(solution)/shard_map/ppermute | solution.py:195
  63.0 0.8 fusion.3
  63.8 1.5 %all-to-all-done = f16[16,2,160,128]{3,2,1,0:T(8,128)(2,1)} async-done(((f16[16,2,160,128]{3,2,1,0:T(8,128)(2,1)}), f16[16,2,160,128]{3,2,1,0:T(8,128)(2,1)}, u32[]{:S(2)}, u32[]{:S(2)}) %all-to-all-start) | async-done | bytes 1310752 | tf_op jit(solution)/shard_map/all_to_all | solution.py:213
  65.3 1.6 %multiply_reduce_fusion = f32[2,160,128]{2,1,0:T(8,128)S(1)} fusion(f16[16,2,160,128]{3,2,1,0:T(8,128)(2,1)} %all-to-all-done), kind=kLoop, calls=%fused_computation | loop fusion | flops 1925120 | bytes 1474560 | tf_op jit(solution)/shard_map/reduce_sum | solution.py:221
  66.9 7.0 %all-to-all-start.1 = ((f16[8,96,128]{2,1,0:T(8,128)(2,1)}), f16[8,96,128]{2,1,0:T(8,128)(2,1)S(1)}, u32[]{:S(2)}, u32[]{:S(2)}) async-start(f16[8,96,128]{2,1,0:T(8,128)(2,1)} %fusion.3), calls=%async_computation.1 | async-start | bytes 393216 | tf_op jit(solution)/shard_map/all_to_all | solution.py:223
  73.9 1.9 %collective-permute-start.6 = (f16[160,128]{1,0:T(8,128)(2,1)S(1)}, f16[160,128]{1,0:T(8,128)(2,1)S(1)}, u32[]{:S(2)}, u32[]{:S(2)}) collective-permute-start(f16[160,128]{1,0:T(8,128)(2,1)S(1)} %fusion.5), channel_id=1, source_target_pairs={{0,64},{32,96},{64,0},{96,32},{1,65},{33,97},{65,1},{97,33},{2,66}... | collective-permute-start | bytes 122888 | tf_op jit(solution)/shard_map/ppermute | solution.py:195
  75.9 5.2 %collective-permute-start.7 = (f32[128,256]{1,0:T(8,128)S(1)}, f32[128,256]{1,0:T(8,128)S(1)}, u32[]{:S(2)}, u32[]{:S(2)}) collective-permute-start(f32[128,256]{1,0:T(8,128)S(1)} %add.42), channel_id=1, source_target_pairs={{0,256},{128,384},{256,0},{384,128},{512,768},{640,896},{768,512},... | collective-permute-start | bytes 393224 | tf_op jit(solution)/shard_map/ppermute | solution.py:199
  81.0 0.0 collective-permute-done.6
  81.0 0.6 fusion.4.bottom
  81.7 0.9 all-to-all-done.1
  82.6 0.6 convert_reduce_fusion.top
  83.3 1.8 %turn_and_square.1 = (f32[128,256]{1,0:T(8,128)}, f32[128,1,128]{2,1,0:T(1,128)}) custom-call(f32[96,128]{1,0:T(8,128)} %convert_reduce_fusion.top, f32[160,128]{1,0:T(8,128)} %fusion.4.bottom), custom_call_target="tpu_custom_call" | custom-call | flops 131072 | bytes 262144 | tf_op jit(solution)/shard_map/turn_and_square/pallas_call | solution.py:148
  85.1 12.2 %all-to-all-start.2 = ((f32[128,1,128]{2,1,0:T(1,128)}), f32[128,1,128]{2,1,0:T(1,128)S(1)}, u32[]{:S(2)}, u32[]{:S(2)}) async-start(f32[128,1,128]{2,1,0:T(1,128)} %get-tuple-element.27), calls=%async_computation.2 | async-start | bytes 131072 | tf_op jit(solution)/shard_map/all_to_all | solution.py:245
  97.3 0.0 collective-permute-done.7
  97.3 1.7 %bitcast_subtract_fusion = (f32[128,256]{1,0:T(8,128)}, f32[128,256]{1,0:T(8,128)}) fusion(f32[8,128,256]{2,1,0:T(8,128)} %param.17, s32[]{:T(128)S(6)} %select_n.6, f32[128,256]{1,0:T(8,128)S(1)} %add.42, f32[128,256]{1,0:T(8,128)S(1)} %collective-permute-done.7, f32[8,128,256]{2,1,0:T(8,128)} %param.18), kind=kLoop, calls=%fused_computation.11 | loop fusion | flops 294912 | bytes 786436 | tf_op jit(solution)/shard_map/sub | solution.py:38
  99.0 9.6 %all-to-all-done.2.rows = f32[128,1,128]{2,1,0:T(1,128)S(1)} async-done(((f32[128,1,128]{2,1,0:T(1,128)}), f32[128,1,128]{2,1,0:T(1,128)S(1)}, u32[]{:S(2)}, u32[]{:S(2)}) %all-to-all-start.2) | async-done | bytes 65568 | tf_op jit(solution)/shard_map/all_to_all | solution.py:245
  108.6 0.0 copy-start
  108.6 0.6 copy-done
  109.2 2.2 %inner_update.1 = (f32[1,128,256]{2,1,0:T(8,128)}, f32[1,128,256]{2,1,0:T(8,128)}, f32[1,128,256]{2,1,0:T(8,128)}) custom-call(f32[128,1,128]{2,1,0:T(1,128)} %copy-done, f32[128,256]{1,0:T(8,128)} %get-tuple-element.28.gradient, f32[1,128,256]{2,1,0:T(8,128)} %params.1, f32[1,128,256]{2,1,0:T(8,128)} %first.1, f32[1,128,256]{2,1,0:T(8,128)} %second.1), custom_call_target="tpu_custom_call" | custom-call | flops 524288 | bytes 1048576 | tf_op jit(solution)/shard_map/inner_update/pallas_call | solution.py:182
  (2 shorter events, 0.0 us)
Async XLA Ops:
  4.8 19.6 %collective-permute-start = (bf16[128,4352]{1,0:T(8,128)(2,1)}, bf16[128,4352]{1,0:T(8,128)(2,1)S(1)}, u32[]{:S(2)}, u32[]{:S(2)}) collective-permute-start(bf16[128,4352]{1,0:T(8,128)(2,1)} %get-tuple-element.20), channel_id=1, source_target_pairs={{0,2},{2,0},{1,3},{3,1},{4,6},{6,4},{5,7},{7,5},{8,10},{10,8},{9,1... | collective-permute-start | bytes 3342344 | tf_op jit(solution)/shard_map/ppermute | solution.py:208
  22.4 7.0 %collective-permute-start.4 = (f32[128,256]{1,0:T(8,128)S(1)}, f32[128,256]{1,0:T(8,128)S(1)}, u32[]{:S(2)}, u32[]{:S(2)}) collective-permute-start(f32[128,256]{1,0:T(8,128)S(1)} %dynamic-slice_bitcast_fusion), channel_id=1, source_target_pairs={{0,128},{128,0},{256,384},{384,256},{512,640},{640,512},{768,896},... | collective-permute-start | bytes 393224 | tf_op jit(solution)/shard_map/ppermute | solution.py:206
  29.4 35.9 %all-to-all-start = ((f16[16,2,160,128]{3,2,1,0:T(8,128)(2,1)}), f16[16,2,160,128]{3,2,1,0:T(8,128)(2,1)}, u32[]{:S(2)}, u32[]{:S(2)}) async-start(f16[16,2,160,128]{3,2,1,0:T(8,128)(2,1)} %bitcast.6), calls=%async_computation | async-start | bytes 2621440 | tf_op jit(solution)/shard_map/all_to_all | solution.py:213
  34.1 20.5 %collective-permute-start.1 = (f16[8,96,128]{2,1,0:T(8,128)(2,1)S(1)}, f16[8,96,128]{2,1,0:T(8,128)(2,1)S(1)}, u32[]{:S(2)}, u32[]{:S(2)}) collective-permute-start(f16[8,96,128]{2,1,0:T(8,128)(2,1)S(1)} %get-tuple-element.35), channel_id=1, source_target_pairs={{0,96},{32,64},{64,32},{96,0},{1,97},{33,65},{65,33},{97,1},{2,98}... | collective-permute-start | bytes 589832 | tf_op jit(solution)/shard_map/ppermute | solution.py:195
  36.0 22.8 %collective-permute-start.2 = (f16[8,96,128]{2,1,0:T(8,128)(2,1)S(1)}, f16[8,96,128]{2,1,0:T(8,128)(2,1)S(1)}, u32[]{:S(2)}, u32[]{:S(2)}) collective-permute-start(f16[8,96,128]{2,1,0:T(8,128)(2,1)S(1)} %get-tuple-element.37), channel_id=1, source_target_pairs={{0,64},{32,96},{64,0},{96,32},{1,65},{33,97},{65,1},{97,33},{2,66}... | collective-permute-start | bytes 589832 | tf_op jit(solution)/shard_map/ppermute | solution.py:195
  40.3 22.7 %collective-permute-start.3 = (f16[8,96,128]{2,1,0:T(8,128)(2,1)S(1)}, f16[8,96,128]{2,1,0:T(8,128)(2,1)S(1)}, u32[]{:S(2)}, u32[]{:S(2)}) collective-permute-start(f16[8,96,128]{2,1,0:T(8,128)(2,1)S(1)} %get-tuple-element.36), channel_id=1, source_target_pairs={{0,32},{32,0},{64,96},{96,64},{1,33},{33,1},{65,97},{97,65},{2,34}... | collective-permute-start | bytes 589832 | tf_op jit(solution)/shard_map/ppermute | solution.py:195
  44.3 9.6 %collective-permute-start.5 = (f32[128,256]{1,0:T(8,128)S(1)}, f32[128,256]{1,0:T(8,128)S(1)}, u32[]{:S(2)}, u32[]{:S(2)}) collective-permute-start(f32[128,256]{1,0:T(8,128)S(1)} %fusion.6), channel_id=1, source_target_pairs={{0,512},{128,640},{256,768},{384,896},{512,0},{640,128},{768,256},... | collective-permute-start | bytes 393224 | tf_op jit(solution)/shard_map/ppermute | solution.py:199
  66.9 15.7 %all-to-all-start.1 = ((f16[8,96,128]{2,1,0:T(8,128)(2,1)}), f16[8,96,128]{2,1,0:T(8,128)(2,1)S(1)}, u32[]{:S(2)}, u32[]{:S(2)}) async-start(f16[8,96,128]{2,1,0:T(8,128)(2,1)} %fusion.3), calls=%async_computation.1 | async-start | bytes 393216 | tf_op jit(solution)/shard_map/all_to_all | solution.py:223
  73.9 7.1 %collective-permute-start.6 = (f16[160,128]{1,0:T(8,128)(2,1)S(1)}, f16[160,128]{1,0:T(8,128)(2,1)S(1)}, u32[]{:S(2)}, u32[]{:S(2)}) collective-permute-start(f16[160,128]{1,0:T(8,128)(2,1)S(1)} %fusion.5), channel_id=1, source_target_pairs={{0,64},{32,96},{64,0},{96,32},{1,65},{33,97},{65,1},{97,33},{2,66}... | collective-permute-start | bytes 122888 | tf_op jit(solution)/shard_map/ppermute | solution.py:195
  75.9 21.4 %collective-permute-start.7 = (f32[128,256]{1,0:T(8,128)S(1)}, f32[128,256]{1,0:T(8,128)S(1)}, u32[]{:S(2)}, u32[]{:S(2)}) collective-permute-start(f32[128,256]{1,0:T(8,128)S(1)} %add.42), channel_id=1, source_target_pairs={{0,256},{128,384},{256,0},{384,128},{512,768},{640,896},{768,512},... | collective-permute-start | bytes 393224 | tf_op jit(solution)/shard_map/ppermute | solution.py:199
  85.1 23.5 %all-to-all-start.2 = ((f32[128,1,128]{2,1,0:T(1,128)}), f32[128,1,128]{2,1,0:T(1,128)S(1)}, u32[]{:S(2)}, u32[]{:S(2)}) async-start(f32[128,1,128]{2,1,0:T(1,128)} %get-tuple-element.27), calls=%async_computation.2 | async-start | bytes 131072 | tf_op jit(solution)/shard_map/all_to_all | solution.py:245
  108.6 0.6 copy-start
